TPU v7x, 32 devices: a whole 2x2x4 slice. The times are simulated.
32 devices in a mesh: req: 4 (over z), exp: 8 (over y, x, core).
Axes of the slice: x: 2, y: 2, z: 4, core: 2. Of those that a mesh axis runs over, the one named last changes fastest.
Arguments:
- hidden: bfloat16 [4096, 2048], P(('req', 'exp')), may hold values from -6 to 6
- attn_gain: float32 [2048], replicated, may hold values from 0.5 to 1.5
- w_query: bfloat16 [2048, 1024], P(None, 'exp'), may hold values from -0.125 to 0.125
- w_keyval: bfloat16 [2, 2048, 1024], P(None, None, 'exp'), may hold values from -0.3125 to 0.3125
- k_pool: bfloat16 [640, 128, 1024], P('req', None, 'exp'), may hold values from -86 to 86
- v_pool: bfloat16 [640, 128, 1024], P('req', None, 'exp'), may hold values from -16 to 16
- dec_len: int32 [16], P('req'), may hold values from 1 to 4096, as said below
- dec_pages: int32 [16, 32], P('req'), may hold values from 0 to 159, as said below
- pre_pos: int32 [4], P('req'), may hold values from 0 to 4096, as said below
- pre_pages: int32 [4, 32], P('req'), may hold values from 0 to 159
- w_out: bfloat16 [1024, 2048], P('exp'), may hold values from -0.1875 to 0.1875
- moe_gain: float32 [2048], replicated, may hold values from 0.1 to 1.9
- expert_ids: int32 [4096, 8], P(('req', 'exp')), may hold values from 0 to 15, all different within a row; in each aligned block of 128 rows (0 to 127, 128 to 255, ...) at most 80 rows name the same one
- router_logits: float32 [4096, 8], P(('req', 'exp')), may hold values from -0.4 to 283
- w_in: bfloat16 [32, 2048, 1024], P(('req', 'exp')), may hold values from -0.125 to 0.125
- w_down: bfloat16 [32, 512, 2048], P(('req', 'exp')), may hold values from -0.25 to 0.25
Outputs:
- mixed: bfloat16 [4096, 2048], P(('req', 'exp'))
- new_kv: bfloat16 [2, 4096, 1024], P(None, 'req', 'exp')
Inputs may be any that keep to these rules, and one draw needn't show every extreme that they name: Within each group, the rows of dec_pages of its 4 requests and its row of pre_pages name every one of the group's 160 pages exactly once. `dec_len`: some request has exactly 4096 cached positions. `pre_pos`: some group's prefix has exactly 4096 positions. `expert_ids`: each row names 8 different experts; among the rows of one device no expert is named by more than 80 rows.
All inputs are finite; a program needn't handle non-finite values.
Results may differ from a plain program's by a relative error of at most 0.02.
Values may be sent and summed in bfloat16 or wider, within the bound.
No kernel may reach another device: no remote copies, remote signals or barrier semaphores. Data moves between devices by JAX's collectives and lax.ppermute only.
A program may use at most 128 MiB of HBM per device.

v0:
```python
import functools
import math

import jax
import jax.numpy as jnp
from jax import lax
from jax.experimental import pallas as pl
from jax.experimental.pallas import tpu as pltpu
from jax.sharding import PartitionSpec as P

HD = 128
SPLIT = 2


EPSILON = 1e-05
THETA = 10000.0


WIDE = jnp.float32


def swap(values, bits):
    count = lax.axis_size("exp")
    return lax.ppermute(values, "exp", [(d, d ^ bits) for d in range(count)])


def shift(values, steps):
    count = lax.axis_size("req")
    return lax.ppermute(values, "req", [(d, (d + steps) % count) for d in range(count)])


def after(values, *others):
    return lax.optimization_barrier((values, *others))[0]


def experts_kernel(part, wide, *refs):
    blocks, (own_in, own_down, pair_in, pair_down) = refs[:4], refs[4:8]
    outs = refs[8:12]
    rows_s, in_s, down_s, active_s, made_s, block_sem, in_sem, down_sem, out_sem = refs[12:]
    units, width = own_down.shape
    size = blocks[0].shape[0]
    parts, tiles = units // part, width // wide

    loads = [
        pltpu.make_async_copy(block, rows_s.at[pl.ds(at * size, size)], block_sem.at[at])
        for at, block in enumerate(blocks)
    ]
    arrivals = []
    for piece, weight in enumerate((own_in, pair_in)):
        for at in range(parts):
            number = piece * parts + at
            here = pl.ds(number * 2 * part, part), pl.ds((number * 2 + 1) * part, part)
            arrivals.append(
                [
                    pltpu.make_async_copy(
                        weight.at[:, pl.ds(half * units + at * part, part)],
                        in_s.at[:, here[half]],
                        in_sem.at[2 * number + half],
                    )
                    for half in range(2)
                ]
            )
    downs = [
        pltpu.make_async_copy(weight, down_s.at[pl.ds(piece * units, units)], down_sem.at[piece])
        for piece, weight in enumerate((own_down, pair_down))
    ]
    for copy in loads:
        copy.start()
    for pair in arrivals:
        for copy in pair:
            copy.start()
    for copy in downs:
        copy.start()
    for copy in loads:
        copy.wait()
    rows = rows_s[...]
    for number, pair in enumerate(arrivals):
        for copy in pair:
            copy.wait()
        both = jnp.dot(
            rows,
            in_s[:, 2 * part * number : 2 * part * (number + 1)],
            preferred_element_type=WIDE,
        )
        gate, up = both[:, :part], both[:, part:]
        active = gate / (1.0 + jnp.exp(-gate)) * up
        active_s[:, part * number : part * (number + 1)] = active.astype(jnp.bfloat16)
    for copy in downs:
        copy.wait()
    active = active_s[...]
    stores = []
    for tile in range(tiles):
        here = slice(tile * wide, (tile + 1) * wide)
        made = jnp.dot(active, down_s[:, here], preferred_element_type=WIDE)
        for at, out in enumerate(outs):
            mine = slice(at * size, (at + 1) * size)
            made_s[mine, here] = made[mine].astype(jnp.bfloat16)
            copy = pltpu.make_async_copy(
                made_s.at[pl.ds(at * size, size), pl.ds(tile * wide, wide)],
                out.at[:, pl.ds(tile * wide, wide)],
                out_sem.at[tile * len(outs) + at],
            )
            copy.start()
            stores.append(copy)
    for copy in stores:
        copy.wait()


def expert_rows(blocks, pieces):
    (own_in, own_down), (pair_in, pair_down) = pieces
    units, width = own_down.shape
    size, count = blocks[0].shape[0], len(blocks)
    rows = size * count
    part, wide = math.gcd(units, 256), math.gcd(width, 512)
    apart = pl.BlockSpec(memory_space=pl.ANY)
    return pl.pallas_call(
        functools.partial(experts_kernel, part, wide),
        out_shape=[jax.ShapeDtypeStruct((size, width), jnp.bfloat16)] * count,
        in_specs=[apart] * (count + 4),
        out_specs=[apart] * count,
        scratch_shapes=[
            pltpu.VMEM((rows, width), jnp.bfloat16),
            pltpu.VMEM((width, 4 * units), jnp.bfloat16),
            pltpu.VMEM((2 * units, width), jnp.bfloat16),
            pltpu.VMEM((rows, 2 * units), jnp.bfloat16),
            pltpu.VMEM((rows, width), jnp.bfloat16),
            pltpu.SemaphoreType.DMA((count,)),
            pltpu.SemaphoreType.DMA((4 * (units // part),)),
            pltpu.SemaphoreType.DMA((2,)),
            pltpu.SemaphoreType.DMA((count * (width // wide),)),
        ],
        compiler_params=pltpu.CompilerParams(vmem_limit_bytes=30 * MIB),
        cost_estimate=pl.CostEstimate(
            flops=12 * rows * width * units,
            bytes_accessed=16 * MIB,
            transcendentals=2 * rows * units,
        ),
        name="experts",
    )(*blocks, own_in, own_down, pair_in, pair_down)


def pick_kernel(gate_ref, place_ref, rows_ref, *refs):
    outs, (made_s, sem) = refs[:-2], refs[-2:]
    rows = rows_ref[...]
    capacity = outs[0].shape[0]
    stores = []
    for at, out in enumerate(outs):
        room = lax.broadcasted_iota(jnp.int32, (capacity, rows.shape[0]), 0)
        chosen = jnp.logical_and(gate_ref[at : at + 1, :] > 0, place_ref[at : at + 1, :] == room)
        picked = jnp.where(chosen, 1.0, 0.0).astype(jnp.bfloat16)
        made = jnp.dot(picked, rows, preferred_element_type=WIDE).astype(jnp.bfloat16)
        made_s[at * capacity : (at + 1) * capacity, :] = made
        copy = pltpu.make_async_copy(
            made_s.at[pl.ds(at * capacity, capacity)], out, sem.at[at]
        )
        copy.start()
        stores.append(copy)
    for copy in stores:
        copy.wait()


def pick(rows, gates, places, count, capacity):
    array = pl.BlockSpec(memory_space=pltpu.VMEM)
    width = rows.shape[1]
    return pl.pallas_call(
        pick_kernel,
        out_shape=[jax.ShapeDtypeStruct((capacity, width), jnp.bfloat16)] * count,
        in_specs=[array] * 3,
        out_specs=[pl.BlockSpec(memory_space=pl.ANY)] * count,
        scratch_shapes=[
            pltpu.VMEM((count * capacity, width), jnp.bfloat16),
            pltpu.SemaphoreType.DMA((count,)),
        ],
        compiler_params=pltpu.CompilerParams(vmem_limit_bytes=12 * MIB),
        cost_estimate=pl.CostEstimate(
            flops=2 * count * capacity * rows.size, bytes_accessed=MIB, transcendentals=0
        ),
        name="pick",
    )(gates, places, rows)


def merge_kernel(count, gate_ref, place_ref, *refs):
    parts, terms, (out_ref, parts_s, sem) = refs[:count], refs[count:-3], refs[-3:]
    capacity = parts[0].shape[0]
    loads = []
    for at, part in enumerate(parts):
        here = parts_s.at[pl.ds(at * capacity, capacity)]
        loads.append(pltpu.make_async_copy(part, here, sem.at[at]))
        loads[-1].start()
    gates, places = gate_ref[...].T, place_ref[...].T
    total = 0.0
    for at in range(count):
        gate, place = gates[:, at : at + 1], places[:, at : at + 1]
        room = lax.broadcasted_iota(jnp.int32, (gates.shape[0], capacity), 1)
        chosen = jnp.logical_and(gate > 0, place == room)
        spread = jnp.where(chosen, 1.0, 0.0).astype(jnp.bfloat16)
        loads[at].wait()
        part = parts_s[at * capacity : (at + 1) * capacity, :]
        total = total + gate * jnp.dot(spread, part, preferred_element_type=WIDE)
    for term in terms:
        total = total + term[...].astype(WIDE)
    out_ref[...] = total.astype(jnp.bfloat16)


def merge(parts, gates, places, terms):
    array = pl.BlockSpec(memory_space=pltpu.VMEM)
    count, (capacity, width) = len(parts), parts[0].shape
    rows = gates.shape[1]
    return pl.pallas_call(
        functools.partial(merge_kernel, count),
        out_shape=jax.ShapeDtypeStruct((rows, width), jnp.bfloat16),
        in_specs=[array] * 2
        + [pl.BlockSpec(memory_space=pl.ANY)] * count
        + [array] * len(terms),
        out_specs=array,
        scratch_shapes=[
            pltpu.VMEM((count * capacity, width), jnp.bfloat16),
            pltpu.SemaphoreType.DMA((count,)),
        ],
        compiler_params=pltpu.CompilerParams(vmem_limit_bytes=16 * MIB),
        cost_estimate=pl.CostEstimate(
            flops=2 * rows * width * count * capacity, bytes_accessed=MIB, transcendentals=0
        ),
        name="merge",
    )(gates, places, *parts, *terms)


def plane_experts(normed_moe, residual, gates, places, pieces, capacity):
    steps = lax.axis_size("req")
    count = lax.axis_size("exp") // 2
    rounds = []

    def exchange(parts):
        mine, *others = parts
        others = after(tuple(others), *rounds[-2:-1])
        rounds.append(tuple(swap(part, 2 * at) for at, part in enumerate(others, 1)))
        return [mine, *rounds[-1]]

    moved, came = normed_moe, []
    for step in range(steps):
        following = shift(moved, 1) if step + 1 < steps else None
        came.append(exchange(pick(moved, gates[step], places[step], count, capacity)))
        moved = following if step else after(following, rounds[0])
    made = []
    for step in range(steps):
        made.append(expert_rows(after(came[step], *made[-1:]), pieces))
    sums = []
    for step in range(1, steps):
        sums.append(merge(exchange(made[step]), gates[step], places[step], []))
    terms = [shift(total, -step) for step, total in enumerate(sums, 1)]
    return merge(exchange(made[0]), gates[0], places[0], [*terms, residual])


LOW = -1e30
MIB = 1 << 20


def rope_tables(positions):
    half = HD // 2
    steps = jnp.arange(half, dtype=WIDE)
    frequency = jnp.exp(steps * (-2.0 * math.log(THETA) / HD))
    angles = positions.astype(WIDE)[:, None] * frequency[None, :]
    cosine, sine = jnp.cos(angles), jnp.sin(angles)
    return (
        jnp.concatenate([cosine, cosine], axis=1),
        jnp.concatenate([-sine, sine], axis=1),
    )


def dot_rows(left, right):
    return lax.dot_general(left, right, (((1,), (1,)), ((), ())), preferred_element_type=WIDE)


def attention_kernel(layout, block_rows, tile, *refs):
    ref_count = sum(count for count, _ in layout)
    place_ref, length_ref, limits_ref, dec_pages_ref, pre_pages_ref = refs[:5]
    sources = refs[5 : 5 + ref_count]
    w_query, w_keyval, same_ref, other_ref, k_pool, v_pool, _, out_ref, kv_ref = refs[
        5 + ref_count : 14 + ref_count
    ]
    (rows_s, weight_s, query_s, turned_s, pre_k, pre_v, dec_k, dec_v) = refs[
        14 + ref_count : 22 + ref_count
    ]
    row_sem, weight_sem, pre_sem, dec_sem = refs[22 + ref_count :]
    page_size = k_pool.shape[1]
    dec_count, dec_pages = dec_pages_ref.shape
    pre_pages = pre_pages_ref.shape[1]
    pre_keys = pre_pages * page_size
    rows = query_s.shape[0]
    dec_keys = dec_pages * page_size
    place = place_ref[0]
    length = length_ref[0]
    rate = math.log2(math.e) / math.sqrt(HD)

    weight_copies = [
        pltpu.make_async_copy(part, weight_s.at[:, pl.ds(at * HD, HD)], weight_sem.at[at])
        for at, part in enumerate((w_query, w_keyval.at[0], w_keyval.at[1]))
    ]
    row_copies, start = [], 0
    for at, source in enumerate(sources):
        here = rows_s.at[pl.ds(start, source.shape[0])]
        row_copies.append(pltpu.make_async_copy(source, here, row_sem.at[at]))
        start += source.shape[0]
    for copy in weight_copies + row_copies:
        copy.start()

    def fetch_prefix(at, carry):
        page = pre_pages_ref[0, at]
        here = pl.ds(pl.multiple_of(at * page_size, page_size), page_size)
        pltpu.make_async_copy(k_pool.at[page], pre_k.at[here], pre_sem.at[0]).start()
        pltpu.make_async_copy(v_pool.at[page], pre_v.at[here], pre_sem.at[1]).start()
        return carry

    lax.fori_loop(0, pre_pages, fetch_prefix, 0)
    for request in range(dec_count):

        def fetch_decode(at, carry):
            page = dec_pages_ref[request, at]
            here = pl.ds(pl.multiple_of(at * page_size, page_size), page_size)
            pltpu.make_async_copy(
                k_pool.at[page], dec_k.at[request, here], dec_sem.at[0, request]
            ).start()
            pltpu.make_async_copy(
                v_pool.at[page], dec_v.at[request, here], dec_sem.at[1, request]
            ).start()
            return carry

        lax.fori_loop(0, dec_pages, fetch_decode, 0)

    for copy in weight_copies:
        copy.wait()
    start = 0
    for count, names in layout:
        for _ in range(count):
            row_copies.pop(0).wait()
        size = block_rows * len(names)
        made = jnp.dot(rows_s[start : start + size], weight_s[...], preferred_element_type=WIDE)
        start += size
        for at, name in enumerate(names):
            mine = made[at * block_rows : (at + 1) * block_rows]
            first = pl.multiple_of((place ^ name) * block_rows, block_rows)
            here = pl.ds(first, block_rows)
            same, other = same_ref[here, :], other_ref[here, :]
            query, key = mine[:, :HD], mine[:, HD : 2 * HD]
            query_s[here, :] = (query * same + pltpu.roll(query, HD // 2, 1) * other).astype(
                jnp.bfloat16
            )
            kv_ref[0, here, :] = (key * same + pltpu.roll(key, HD // 2, 1) * other).astype(
                jnp.bfloat16
            )
            kv_ref[1, here, :] = mine[:, 2 * HD :].astype(jnp.bfloat16)

    pltpu.make_async_copy(pre_k, pre_k, pre_sem.at[0]).wait()
    pltpu.make_async_copy(pre_v, pre_v, pre_sem.at[1]).wait()

    turned_s[:HD, :pre_keys] = pre_v[...].T
    turned_s[:HD, pre_keys:] = kv_ref[1].T
    turned_s[HD:, :] = jnp.ones((turned_s.shape[0] - HD, turned_s.shape[1]), jnp.bfloat16)
    slots = lax.broadcasted_iota(jnp.int32, (pre_keys, 1), 0)
    bias = jnp.where(slots < length, 0.0, LOW)
    for at in range(rows // tile):
        start = at * tile
        held = start + tile
        query = query_s[start:held, :]
        scores = dot_rows(pre_k[...], query) * rate + bias
        own = dot_rows(kv_ref[0, :held, :], query) * rate
        seen = lax.broadcasted_iota(jnp.int32, own.shape, 0)
        asked = start + lax.broadcasted_iota(jnp.int32, own.shape, 1)
        own = jnp.where(jnp.logical_and(seen >= dec_count, seen <= asked), own, LOW)
        highest = jnp.maximum(
            jnp.max(scores, axis=0, keepdims=True), jnp.max(own, axis=0, keepdims=True)
        )
        weights = jnp.exp2(scores - highest).astype(jnp.bfloat16)
        own_weights = jnp.exp2(own - highest).astype(jnp.bfloat16)
        total = jnp.dot(
            turned_s[:, :pre_keys], weights, preferred_element_type=WIDE
        ) + jnp.dot(
            turned_s[:, pre_keys : pre_keys + held], own_weights, preferred_element_type=WIDE
        )
        done = (total[:HD] / total[HD : HD + 1]).T.astype(jnp.bfloat16)
        for part in range(tile // block_rows):
            target = (at * (tile // block_rows) + part) ^ place
            target = pl.multiple_of(target * block_rows, block_rows)
            out_ref[pl.ds(target, block_rows), :] = done[
                part * block_rows : (part + 1) * block_rows
            ]

    few = 16
    query = query_s[:few, :]
    row = lax.broadcasted_iota(jnp.int32, (few, HD), 0)
    own_scores = dot_rows(query, kv_ref[0, :few, :]) * rate
    first_rows = pl.ds(pl.multiple_of(place * block_rows, block_rows), few)
    result = out_ref[first_rows, :].astype(WIDE)
    for request in range(dec_count):
        pltpu.make_async_copy(dec_k.at[request], dec_k.at[request], dec_sem.at[0, request]).wait()
        pltpu.make_async_copy(dec_v.at[request], dec_v.at[request], dec_sem.at[1, request]).wait()
        scores = dot_rows(query, dec_k[request]) * rate
        slots = lax.broadcasted_iota(jnp.int32, (few, dec_keys), 1)
        scores = jnp.where(slots < limits_ref[request], scores, LOW)
        itself = lax.broadcasted_iota(jnp.int32, (few, few), 1) == request
        own = jnp.where(itself, own_scores, LOW)
        highest = jnp.maximum(
            jnp.max(scores, axis=1, keepdims=True), jnp.max(own, axis=1, keepdims=True)
        )
        weights = jnp.exp2(scores - highest)
        own_weights = jnp.exp2(own - highest)
        total = jnp.sum(weights, axis=1, keepdims=True) + jnp.sum(
            own_weights, axis=1, keepdims=True
        )
        summed = jnp.dot(
            weights.astype(jnp.bfloat16), dec_v[request], preferred_element_type=WIDE
        ) + jnp.dot(
            own_weights.astype(jnp.bfloat16), kv_ref[1, :few, :], preferred_element_type=WIDE
        )
        result = jnp.where(row == request, summed / total, result)
    out_ref[first_rows, :] = result.astype(jnp.bfloat16)


def attention(place, groups, names, weights, positions, pools, tables, earlier):
    pre_pos, dec_len, dec_pages, pre_pages = tables
    k_pool, v_pool = pools
    w_query, w_keyval = weights
    blocks = [block for group in groups for block in group]
    rows = sum(block.shape[0] for block in blocks)
    block_rows = rows // sum(len(group) for group in names)
    layout = [(len(group), name) for group, name in zip(groups, names, strict=True)]
    page_size = k_pool.shape[1]
    pre_keys = pre_pages.shape[1] * page_size
    dec_keys = dec_pages.shape[1] * page_size
    dec_count = dec_pages.shape[0]
    tile = 4 * block_rows
    width = w_query.shape[0]
    same, other = rope_tables(positions)
    number = pl.BlockSpec(memory_space=pltpu.SMEM)
    array = pl.BlockSpec(memory_space=pltpu.VMEM)
    apart = pl.BlockSpec(memory_space=pl.ANY)
    flops = 2 * rows * (3 * HD * width + 2 * HD * (pre_keys + rows))
    return pl.pallas_call(
        functools.partial(attention_kernel, layout, block_rows, tile),
        out_shape=(
            jax.ShapeDtypeStruct((rows, HD), jnp.bfloat16),
            jax.ShapeDtypeStruct((2, rows, HD), jnp.bfloat16),
        ),
        in_specs=[number] * 5 + [apart] * (len(blocks) + 2) + [array] * 2 + [apart] * 3,
        out_specs=(array, array),
        scratch_shapes=[
            pltpu.VMEM((rows, width), jnp.bfloat16),
            pltpu.VMEM((width, 3 * HD), jnp.bfloat16),
            pltpu.VMEM((rows, HD), jnp.bfloat16),
            pltpu.VMEM((HD + 16, pre_keys + rows), jnp.bfloat16),
            pltpu.VMEM((pre_keys, HD), jnp.bfloat16),
            pltpu.VMEM((pre_keys, HD), jnp.bfloat16),
            pltpu.VMEM((dec_count, dec_keys, HD), jnp.bfloat16),
            pltpu.VMEM((dec_count, dec_keys, HD), jnp.bfloat16),
            pltpu.SemaphoreType.DMA((len(blocks),)),
            pltpu.SemaphoreType.DMA((3,)),
            pltpu.SemaphoreType.DMA((2,)),
            pltpu.SemaphoreType.DMA((2, dec_count)),
        ],
        compiler_params=pltpu.CompilerParams(vmem_limit_bytes=48 * MIB),
        cost_estimate=pl.CostEstimate(
            flops=flops, bytes_accessed=20 * MIB, transcendentals=rows * (pre_keys + rows)
        ),
        name="attention",
    )(
        place,
        pre_pos,
        dec_len,
        dec_pages,
        pre_pages,
        *blocks,
        w_query,
        w_keyval,
        same,
        other,
        k_pool,
        v_pool,
        earlier,
    )


def project_kernel(count, *refs):
    heads, weights = refs[:count], refs[count : 2 * count]
    own_ref, other_ref = refs[2 * count :]
    width = weights[0].shape[1]
    rows = own_ref.shape[0]
    step = math.gcd(width, 512)
    for start in range(0, width, step):
        here = slice(start, start + step)
        total = 0.0
        for first in range(0, count, 2):
            left = jnp.concatenate([heads[first][...], heads[first + 1][...]], axis=1)
            right = jnp.concatenate(
                [weights[first][:, here], weights[first + 1][:, here]], axis=0
            )
            total = total + jnp.dot(left, right, preferred_element_type=WIDE)
        own_ref[:, here] = total[:rows]
        other_ref[:, here] = total[rows:].astype(jnp.bfloat16)


def project(heads, weights, rows):
    array = pl.BlockSpec(memory_space=pltpu.VMEM)
    count, all_rows, width = len(heads), heads[0].shape[0], weights[0].shape[1]
    return pl.pallas_call(
        functools.partial(project_kernel, count),
        out_shape=(
            jax.ShapeDtypeStruct((rows, width), WIDE),
            jax.ShapeDtypeStruct((all_rows - rows, width), jnp.bfloat16),
        ),
        in_specs=[array] * (2 * count),
        out_specs=(array, array),
        compiler_params=pltpu.CompilerParams(vmem_limit_bytes=32 * MIB),
        cost_estimate=pl.CostEstimate(
            flops=2 * all_rows * width * count * HD, bytes_accessed=4 * MIB, transcendentals=0
        ),
        name="project",
    )(*heads, *weights)


def close_kernel(hidden_ref, gain_ref, *refs):
    *terms, residual_ref, normed_ref = refs
    total = hidden_ref[...].astype(WIDE)
    for term in terms:
        total = total + term[...].astype(WIDE)
    rounded = total.astype(jnp.bfloat16)
    residual_ref[...] = rounded
    total = rounded.astype(WIDE)
    factor = lax.rsqrt(jnp.mean(total * total, axis=1, keepdims=True) + EPSILON)
    normed_ref[...] = (total * factor * gain_ref[...]).astype(jnp.bfloat16)


def close(hidden, gain, terms):
    array = pl.BlockSpec(memory_space=pltpu.VMEM)
    return pl.pallas_call(
        close_kernel,
        out_shape=(jax.ShapeDtypeStruct(hidden.shape, jnp.bfloat16),) * 2,
        in_specs=[array] * (2 + len(terms)),
        out_specs=(array, array),
        compiler_params=pltpu.CompilerParams(vmem_limit_bytes=16 * MIB),
        name="close",
    )(hidden, gain[None, :], *terms)


def norm_kernel(hidden_ref, gain_ref, out_ref):
    values = hidden_ref[...].astype(WIDE)
    factor = lax.rsqrt(jnp.mean(values * values, axis=1, keepdims=True) + EPSILON)
    out_ref[...] = (values * factor * gain_ref[...]).astype(jnp.bfloat16)


def norm(hidden, gain):
    array = pl.BlockSpec(memory_space=pltpu.VMEM)
    return pl.pallas_call(
        norm_kernel,
        out_shape=jax.ShapeDtypeStruct(hidden.shape, jnp.bfloat16),
        in_specs=[array, array],
        out_specs=array,
        compiler_params=pltpu.CompilerParams(vmem_limit_bytes=16 * MIB),
        name="norm",
    )(hidden, gain[None, :])


def gather_blocks(rows, first):
    half = rows.shape[0] // 2
    from_x, from_y = swap(rows, 2), swap(rows, 4)
    beside = swap(after(rows, from_x), 1)
    x_1, y_2 = after((from_x[:half], from_y[half:]), *first)
    far = jnp.concatenate([swap(x_1, 4), swap(y_2, 2)], axis=0)
    near = jnp.concatenate([from_x, from_y], axis=0)
    near_beside = swap(near, 1)
    return (
        [[rows, beside], [near], [near_beside], [far, swap(far, 1)]],
        [[0, 1], [2, 4], [3, 5], [6, 7]],
    )


def gate_table(expert_ids, gates):
    req_count = lax.axis_size("req")
    exp_count = lax.axis_size("exp")
    experts = req_count * exp_count // SPLIT
    named = expert_ids.T[None] == jnp.arange(experts, dtype=jnp.int32)[:, None, None]
    table = jnp.sum(jnp.where(named, gates.T[None], 0.0), axis=1)
    near = jnp.stack([table, shift(table, 1)])
    near = jnp.concatenate([near, shift(near, 2)])
    bits = jnp.arange(0, exp_count, 2, dtype=jnp.int32)
    owner = lax.axis_index("req") * exp_count + (lax.axis_index("exp") ^ bits)
    chosen = (owner // SPLIT)[:, None] == jnp.arange(experts, dtype=jnp.int32)
    mine = jnp.sum(jnp.where(chosen[None, :, :, None], near[:, None], 0.0), axis=2)
    mine = jnp.pad(mine, ((0, 0), (0, -mine.shape[1] % 8), (0, 0)))
    marks = (mine > 0).astype(jnp.int32)
    return mine, jnp.cumsum(marks, axis=2) - marks


def deliver(buffer):
    result = lax.all_to_all(buffer, ("req", "exp"), split_axis=0, concat_axis=0, tiled=True)
    return result


def bring_back(buffer):
    result = lax.all_to_all(buffer, ("req", "exp"), split_axis=0, concat_axis=0, tiled=True)
    return result


def slots_of(choices, experts):
    return 2 * ((choices * 5 + 8 * experts - 1) // (8 * experts))


def sparse_experts(normed_moe, expert_ids, gates, w_in, w_down):
    local_rows, width = normed_moe.shape
    devices = lax.axis_size("req") * lax.axis_size("exp")
    experts = devices // SPLIT
    top = expert_ids.shape[1]
    capacity = slots_of(local_rows * top, experts)
    assigned = expert_ids.reshape(-1)
    count_all = assigned.shape[0]
    marks = (assigned[:, None] == jnp.arange(experts, dtype=jnp.int32)[None, :]).astype(jnp.int32)
    earlier = jnp.cumsum(marks, axis=0) - marks
    place = jnp.sum(earlier * marks, axis=1)
    target = assigned * capacity + place
    owner_rows = jnp.arange(count_all, dtype=jnp.int32) // top
    outgoing = (
        jnp.zeros((experts * capacity, width), jnp.bfloat16).at[target].set(normed_moe[owner_rows])
    )
    doubled = jnp.broadcast_to(
        outgoing.reshape(experts, 1, capacity, width), (experts, SPLIT, capacity, width)
    ).reshape(devices, capacity, width)
    arrived = deliver(doubled)
    piece_units = w_down.shape[1]
    inner = jnp.dot(
        arrived.reshape(devices * capacity, width), w_in[0], preferred_element_type=jnp.float32
    )
    activated = (jax.nn.silu(inner[:, :piece_units]) * inner[:, piece_units:]).astype(jnp.bfloat16)
    partial_value = (
        jnp.dot(activated, w_down[0], preferred_element_type=jnp.float32)
        .astype(jnp.bfloat16)
        .reshape(devices, capacity, width)
    )
    returned = bring_back(partial_value).reshape(devices * capacity, width)
    base_index = assigned * (SPLIT * capacity) + place
    lower_half = returned[base_index].astype(jnp.float32)
    upper_half = returned[base_index + capacity].astype(jnp.float32)
    weighted = (lower_half + upper_half) * gates.reshape(-1)[:, None]
    moe_out = jnp.sum(weighted.reshape(local_rows, top, width), axis=1)
    return moe_out


def body(
    hidden,
    attn_gain,
    w_query,
    w_keyval,
    k_pool,
    v_pool,
    dec_len,
    dec_pages,
    pre_pos,
    pre_pages,
    w_out,
    moe_gain,
    expert_ids,
    router_logits,
    w_in,
    w_down,
):
    local_rows, width = hidden.shape
    exp_count = lax.axis_size("exp")
    group_rows = local_rows * exp_count
    dec_count = dec_len.shape[0]
    quick = exp_count == 8
    experts = lax.axis_size("req") * exp_count // SPLIT
    capacity = slots_of(local_rows * expert_ids.shape[1], experts)
    normed_attn = norm(hidden, attn_gain)
    row_index = jnp.arange(group_rows, dtype=jnp.int32)
    own_positions = jnp.sum(
        jnp.where(row_index[:, None] == jnp.arange(dec_count), dec_len[None, :], 0), axis=1
    )
    positions = jnp.where(row_index < dec_count, own_positions, pre_pos[0] + row_index - dec_count)
    if quick:
        place = lax.axis_index("exp").reshape(1)
        gates = jax.nn.softmax(router_logits, axis=-1)
        near_gates, near_places = gate_table(expert_ids, gates)
        own_in, own_down = w_in[0], w_down[0]
        pair_in = swap(own_in, 1)
        groups, names = gather_blocks(normed_attn, (near_places, pair_in))
        far, late = groups[-1]
        own_out, late_down = after(w_out, far), after(own_down, late)
        out_blocks = [w_out] + [swap(own_out, bits) for bits in (2, 4, 6)]
        pieces = [(own_in, own_down), (pair_in, swap(late_down, 1))]
        earlier = near_places
    else:
        place = jnp.zeros((1,), jnp.int32)
        earlier = place
        blocks = jnp.split(lax.all_gather(normed_attn, "exp", axis=0, tiled=True), exp_count)
        groups = [blocks[at : at + 2] for at in range(0, exp_count, 2)]
        names = [[at, at + 1] for at in range(0, exp_count, 2)]
        out_blocks = jnp.split(lax.all_gather(w_out, "exp", axis=0, tiled=True), exp_count)
    attended, new_kv = attention(
        place,
        groups,
        names,
        (w_query, w_keyval),
        positions,
        (k_pool, v_pool),
        (pre_pos, dec_len, dec_pages, pre_pages),
        earlier,
    )
    if quick:
        attended = after(attended, pieces[1], out_blocks)
        pairs = jnp.split(attended, exp_count // 2)
        heads = [pairs[0]] + [swap(pairs[at], 2 * at) for at in range(1, exp_count // 2)]
        own, other = project(heads, out_blocks, local_rows)
        residual, normed_moe = close(hidden, moe_gain, [own, swap(other, 1)])
        mixed = plane_experts(
            normed_moe, residual, near_gates, near_places, pieces, capacity
        )
    else:
        heads = jnp.split(
            lax.all_to_all(attended, "exp", split_axis=0, concat_axis=0, tiled=True), exp_count
        )
        own, _ = project([jnp.tile(head, (2, 1)) for head in heads], out_blocks, local_rows)
        residual, normed_moe = close(hidden, moe_gain, [own])
        gates = jax.nn.softmax(router_logits, axis=-1)
        moe_out = sparse_experts(normed_moe, expert_ids, gates, w_in, w_down)
        mixed = (residual.astype(jnp.float32) + moe_out).astype(jnp.bfloat16)
    return (mixed, new_kv)


def solution(mesh):
    placed = (
        P(("req", "exp"), None),
        P(),
        P(None, "exp"),
        P(None, None, "exp"),
        P("req", None, "exp"),
        P("req", None, "exp"),
        P("req"),
        P("req", None),
        P("req"),
        P("req", None),
        P("exp", None),
        P(),
        P(("req", "exp"), None),
        P(("req", "exp"), None),
        P(("req", "exp"), None, None),
        P(("req", "exp"), None, None),
    )
    return jax.shard_map(
        body,
        mesh=mesh,
        in_specs=placed,
        out_specs=(P(("req", "exp"), None), P(None, "req", "exp")),
        check_vma=False,
    )
```

profile of v0, /device:TPU:0, one launch (start us, length us, event | category | flops | bytes accessed | tf_op | source)
XLA Modules:
  0.0 219.1 jit_solution(15311331916799978523)
XLA Ops:
  3.1 2.6 %collective-permute-start.4 = (bf16[128,2048]{1,0:T(8,128)(2,1)S(1)}, bf16[128,2048]{1,0:T(8,128)(2,1)S(1)}, u32[]{:S(2)}, u32[]{:S(2)}) collective-permute-start(bf16[128,2048]{1,0:T(8,128)(2,1)S(1)} %norm.1.refs_5_), channel_id=1, source_target_pairs={{0,4},{1,5},{2,6},{3,7},{4,0},{5,1},{6,2},{7,3},{8,12},{9,13},{10,... | collective-permute-start | bytes 1572872 | tf_op jit(solution)/shard_map/ppermute | solution.py:24
  5.7 1.5 collective-permute-start.2
  10.0 1.6 collective-permute-start
  11.7 3.9 %collective-permute-done = f32[16,128]{1,0:T(8,128)S(1)} collective-permute-done((f32[16,128]{1,0:T(8,128)S(1)}, f32[16,128]{1,0:T(8,128)S(1)}, u32[]{:S(2)}, u32[]{:S(2)}) %collective-permute-start) | collective-permute-done | bytes 8224 | tf_op jit(solution)/shard_map/ppermute | solution.py:29
  16.4 3.8 %collective-permute-done.1 = f32[2,16,128]{2,1,0:T(8,128)S(1)} collective-permute-done((f32[2,16,128]{2,1,0:T(8,128)S(1)}, f32[2,16,128]{2,1,0:T(8,128)S(1)}, u32[]{:S(2)}, u32[]{:S(2)}) %collective-permute-start.1) | collective-permute-done | bytes 16416 | tf_op jit(solution)/shard_map/ppermute | solution.py:29
  22.5 5.5 %collective-permute-done.7 = bf16[64,2048]{1,0:T(8,128)(2,1)S(1)} collective-permute-done((bf16[64,2048]{1,0:T(8,128)(2,1)S(1)}, bf16[64,2048]{1,0:T(8,128)(2,1)S(1)}, u32[]{:S(2)}, u32[]{:S(2)}) %collective-permute-start.7) | collective-permute-done | bytes 262176 | tf_op jit(solution)/shard_map/ppermute | solution.py:24
  28.6 1.9 collective-permute-done.9.refs_10_
  34.2 1.9 fusion
  36.1 1.7 collective-permute-start.13
  40.1 16.0 %attention.1 = (bf16[1024,128]{1,0:T(8,128)(2,1)S(1)}, bf16[2,1024,128]{2,1,0:T(8,128)(2,1)}) custom-call(s32[1]{0:T(128)} %bitcast.7.refs_0_, s32[1]{0:T(128)} %copy.20.refs_1_, s32[4]{0:T(128)S(1)} %copy-done.7, s32[4,32]{1,0:T(4,128)S(1)} %copy-done.6, s32[1,32]{1,0:T(1,128)S(1)} %copy-done.8, bf16[128,2048]{1,0:T(8,128)(2,1)S(1)} %norm.1.refs_5_, ...), custom_call_target="tpu_custom_call" | custom-call | flops 4294967296 | bytes 20971520 | tf_op jit(solution)/shard_map/attention/pallas_call | solution.py:438
  56.1 6.4 %collective-permute-done.12.refs_6_ = bf16[128,2048]{1,0:T(8,128)(2,1)S(1)} collective-permute-done((bf16[128,2048]{1,0:T(8,128)(2,1)S(1)}, bf16[128,2048]{1,0:T(8,128)(2,1)S(1)}, u32[]{:S(2)}, u32[]{:S(2)}) %collective-permute-start.12) | collective-permute-done | bytes 524320 | tf_op jit(solution)/shard_map/ppermute | solution.py:24
  62.6 1.6 collective-permute-start.16
  66.2 1.9 collective-permute-done.16.refs_3_
  70.4 1.9 collective-permute-done.17.refs_1_
  72.6 1.6 collective-permute-start.21
  74.3 1.4 pick.4
  77.6 1.6 collective-permute-start.20
  79.2 7.1 %collective-permute-done.18.refs_1_ = bf16[80,2048]{1,0:T(8,128)(2,1)S(1)} collective-permute-done((bf16[80,2048]{1,0:T(8,128)(2,1)S(1)}, bf16[80,2048]{1,0:T(8,128)(2,1)S(1)}, u32[]{:S(2)}, u32[]{:S(2)}) %collective-permute-start.18) | collective-permute-done | bytes 327712 | tf_op jit(solution)/shard_map/ppermute | solution.py:24
  86.7 5.9 %collective-permute-done.20.refs_3_ = bf16[80,2048]{1,0:T(8,128)(2,1)S(1)} collective-permute-done((bf16[80,2048]{1,0:T(8,128)(2,1)S(1)}, bf16[80,2048]{1,0:T(8,128)(2,1)S(1)}, u32[]{:S(2)}, u32[]{:S(2)}) %collective-permute-start.20) | collective-permute-done | bytes 327712 | tf_op jit(solution)/shard_map/ppermute | solution.py:24
  92.5 1.6 collective-permute-start.22
  94.1 1.4 pick.6
  95.5 1.5 collective-permute-start.26
  99.1 8.0 %collective-permute-done.22.rows_ref = bf16[128,2048]{1,0:T(8,128)(2,1)S(1)} collective-permute-done((bf16[128,2048]{1,0:T(8,128)(2,1)S(1)}, bf16[128,2048]{1,0:T(8,128)(2,1)S(1)}, u32[]{:S(2)}, u32[]{:S(2)}) %collective-permute-start.22) | collective-permute-done | bytes 524320 | tf_op jit(solution)/shard_map/ppermute | solution.py:29
  107.1 7.6 %experts.4 = (bf16[80,2048]{1,0:T(8,128)(2,1)S(1)}, bf16[80,2048]{1,0:T(8,128)(2,1)S(1)}, bf16[80,2048]{1,0:T(8,128)(2,1)S(1)}, bf16[80,2048]{1,0:T(8,128)(2,1)S(1)}) custom-call(bf16[80,2048]{1,0:T(8,128)(2,1)S(1)} %get-tuple-element.104.refs_0_, bf16[80,2048]{1,0:T(8,128)(2,1)S(1)} %collective-permute-done.18.refs_1_, ...), custom_call_target="tpu_custom_call" | custom-call | flops 4026531840 | bytes 16777216 | tf_op jit(solution)/shard_map/experts/pallas_call | solution.py:116
  114.7 1.4 pick.5
  118.0 1.6 collective-permute-start.25
  119.7 7.6 %experts.5 = (bf16[80,2048]{1,0:T(8,128)(2,1)S(1)}, bf16[80,2048]{1,0:T(8,128)(2,1)S(1)}, bf16[80,2048]{1,0:T(8,128)(2,1)S(1)}, bf16[80,2048]{1,0:T(8,128)(2,1)S(1)}) custom-call(bf16[80,2048]{1,0:T(8,128)(2,1)S(1)} %get-tuple-element.127.refs_0_, bf16[80,2048]{1,0:T(8,128)(2,1)S(1)} %collective-permute-done.26.refs_1_, ...), custom_call_target="tpu_custom_call" | custom-call | flops 4026531840 | bytes 16777216 | tf_op jit(solution)/shard_map/experts/pallas_call | solution.py:116
  127.5 4.0 %collective-permute-done.25.refs_3_ = bf16[80,2048]{1,0:T(8,128)(2,1)S(1)} collective-permute-done((bf16[80,2048]{1,0:T(8,128)(2,1)S(1)}, bf16[80,2048]{1,0:T(8,128)(2,1)S(1)}, u32[]{:S(2)}, u32[]{:S(2)}) %collective-permute-start.25) | collective-permute-done | bytes 327712 | tf_op jit(solution)/shard_map/ppermute | solution.py:24
  133.7 1.4 pick.7
  137.0 1.7 collective-permute-start.32
  138.7 7.7 %experts.6 = (bf16[80,2048]{1,0:T(8,128)(2,1)S(1)}, bf16[80,2048]{1,0:T(8,128)(2,1)S(1)}, bf16[80,2048]{1,0:T(8,128)(2,1)S(1)}, bf16[80,2048]{1,0:T(8,128)(2,1)S(1)}) custom-call(bf16[80,2048]{1,0:T(8,128)(2,1)S(1)} %get-tuple-element.135.refs_0_, bf16[80,2048]{1,0:T(8,128)(2,1)S(1)} %collective-permute-done.23.refs_1_, ...), custom_call_target="tpu_custom_call" | custom-call | flops 4026531840 | bytes 16777216 | tf_op jit(solution)/shard_map/experts/pallas_call | solution.py:116
  146.4 2.7 %collective-permute-done.30.refs_1_ = bf16[80,2048]{1,0:T(8,128)(2,1)S(1)} collective-permute-done((bf16[80,2048]{1,0:T(8,128)(2,1)S(1)}, bf16[80,2048]{1,0:T(8,128)(2,1)S(1)}, u32[]{:S(2)}, u32[]{:S(2)}) %collective-permute-start.30) | collective-permute-done | bytes 327712 | tf_op jit(solution)/shard_map/ppermute | solution.py:24
  149.1 1.7 collective-permute-start.41
  150.8 5.2 %collective-permute-done.32.refs_3_ = bf16[80,2048]{1,0:T(8,128)(2,1)S(1)} collective-permute-done((bf16[80,2048]{1,0:T(8,128)(2,1)S(1)}, bf16[80,2048]{1,0:T(8,128)(2,1)S(1)}, u32[]{:S(2)}, u32[]{:S(2)}) %collective-permute-start.32) | collective-permute-done | bytes 327712 | tf_op jit(solution)/shard_map/ppermute | solution.py:24
  156.0 7.6 %experts.7 = (bf16[80,2048]{1,0:T(8,128)(2,1)S(1)}, bf16[80,2048]{1,0:T(8,128)(2,1)S(1)}, bf16[80,2048]{1,0:T(8,128)(2,1)S(1)}, bf16[80,2048]{1,0:T(8,128)(2,1)S(1)}) custom-call(bf16[80,2048]{1,0:T(8,128)(2,1)S(1)} %get-tuple-element.159.refs_0_, bf16[80,2048]{1,0:T(8,128)(2,1)S(1)} %collective-permute-done.30.refs_1_, ...), custom_call_target="tpu_custom_call" | custom-call | flops 4026531840 | bytes 16777216 | tf_op jit(solution)/shard_map/experts/pallas_call | solution.py:116
  163.6 5.1 %collective-permute-start.44 = (bf16[80,2048]{1,0:T(8,128)(2,1)S(1)}, bf16[80,2048]{1,0:T(8,128)(2,1)S(1)}, u32[]{:S(2)}, u32[]{:S(2)}) collective-permute-start(bf16[80,2048]{1,0:T(8,128)(2,1)S(1)} %get-tuple-element.167), channel_id=1, source_target_pairs={{0,2},{1,3},{2,0},{3,1},{4,6},{5,7},{6,4},{7,5},{8,10},{9,11},{10,... | collective-permute-start | bytes 983048 | tf_op jit(solution)/shard_map/ppermute | solution.py:24
  170.3 1.9 collective-permute-start.33
  172.8 3.9 %collective-permute-done.44.refs_1_ = bf16[80,2048]{1,0:T(8,128)(2,1)S(1)} collective-permute-done((bf16[80,2048]{1,0:T(8,128)(2,1)S(1)}, bf16[80,2048]{1,0:T(8,128)(2,1)S(1)}, u32[]{:S(2)}, u32[]{:S(2)}) %collective-permute-start.44) | collective-permute-done | bytes 327712 | tf_op jit(solution)/shard_map/ppermute | solution.py:24
  177.7 1.8 merge.4
  179.5 2.1 collective-permute-done.45.refs_2_
  181.6 3.3 %collective-permute-start.42 = (bf16[128,2048]{1,0:T(8,128)(2,1)S(1)}, bf16[128,2048]{1,0:T(8,128)(2,1)S(1)}, u32[]{:S(2)}, u32[]{:S(2)}) collective-permute-start(bf16[128,2048]{1,0:T(8,128)(2,1)S(1)} %merge.4), channel_id=1, source_target_pairs={{0,24},{8,0},{16,8},{24,16},{1,25},{9,1},{17,9},{25,17},{2,26},{10... | collective-permute-start | bytes 1572872 | tf_op jit(solution)/shard_map/ppermute | solution.py:29
  184.9 1.8 merge.6
  187.8 6.0 %collective-permute-done.35.refs_3_ = bf16[80,2048]{1,0:T(8,128)(2,1)S(1)} collective-permute-done((bf16[80,2048]{1,0:T(8,128)(2,1)S(1)}, bf16[80,2048]{1,0:T(8,128)(2,1)S(1)}, u32[]{:S(2)}, u32[]{:S(2)}) %collective-permute-start.35) | collective-permute-done | bytes 327712 | tf_op jit(solution)/shard_map/ppermute | solution.py:24
  193.9 2.0 merge.5
  199.5 3.6 %collective-permute-done.36.refs_1_ = bf16[80,2048]{1,0:T(8,128)(2,1)S(1)} collective-permute-done((bf16[80,2048]{1,0:T(8,128)(2,1)S(1)}, bf16[80,2048]{1,0:T(8,128)(2,1)S(1)}, u32[]{:S(2)}, u32[]{:S(2)}) %collective-permute-start.36) | collective-permute-done | bytes 327712 | tf_op jit(solution)/shard_map/ppermute | solution.py:24
  203.1 4.5 %collective-permute-done.37.refs_2_ = bf16[80,2048]{1,0:T(8,128)(2,1)S(1)} collective-permute-done((bf16[80,2048]{1,0:T(8,128)(2,1)S(1)}, bf16[80,2048]{1,0:T(8,128)(2,1)S(1)}, u32[]{:S(2)}, u32[]{:S(2)}) %collective-permute-start.37) | collective-permute-done | bytes 327712 | tf_op jit(solution)/shard_map/ppermute | solution.py:24
  207.6 8.3 %collective-permute-done.43.refs_5_ = bf16[128,2048]{1,0:T(8,128)(2,1)S(1)} collective-permute-done((bf16[128,2048]{1,0:T(8,128)(2,1)S(1)}, bf16[128,2048]{1,0:T(8,128)(2,1)S(1)}, u32[]{:S(2)}, u32[]{:S(2)}) %collective-permute-start.43) | collective-permute-done | bytes 524320 | tf_op jit(solution)/shard_map/ppermute | solution.py:29
  216.0 2.9 %merge.7 = bf16[128,2048]{1,0:T(8,128)(2,1)} custom-call(f32[8,128]{1,0:T(8,128)S(1)} %get-tuple-element.183.gate_ref, s32[8,128]{1,0:T(8,128)S(1)} %get-tuple-element.179.place_ref, bf16[80,2048]{1,0:T(8,128)(2,1)S(1)} %get-tuple-element.108.refs_0_, bf16[80,2048]{1,0:T(8,128)(2,1)S(1)} %collective-permute-done.36.refs_1_, ...), custom_call_target="tpu_custom_call" | custom-call | flops 167772160 | bytes 1048576 | tf_op jit(solution)/shard_map/merge/pallas_call | solution.py:209
  (116 shorter events, 37.4 us)
Async XLA Ops:
  0.6 20.9 %collective-permute-start.6 = (bf16[2048,1024]{1,0:T(8,128)(2,1)}, bf16[2048,1024]{1,0:T(8,128)(2,1)}, u32[]{:S(2)}, u32[]{:S(2)}) collective-permute-start(bf16[2048,1024]{1,0:T(8,128)(2,1)} %bitcast.30), channel_id=1, source_target_pairs={{0,1},{1,0},{2,3},{3,2},{4,5},{5,4},{6,7},{7,6},{8,9},{9,8},{10,11... | collective-permute-start | bytes 12582920 | tf_op jit(solution)/shard_map/ppermute | solution.py:24
  3.1 18.4 %collective-permute-start.4 = (bf16[128,2048]{1,0:T(8,128)(2,1)S(1)}, bf16[128,2048]{1,0:T(8,128)(2,1)S(1)}, u32[]{:S(2)}, u32[]{:S(2)}) collective-permute-start(bf16[128,2048]{1,0:T(8,128)(2,1)S(1)} %norm.1.refs_5_), channel_id=1, source_target_pairs={{0,4},{1,5},{2,6},{3,7},{4,0},{5,1},{6,2},{7,3},{8,12},{9,13},{10,... | collective-permute-start | bytes 1572872 | tf_op jit(solution)/shard_map/ppermute | solution.py:24
  5.7 15.8 %collective-permute-start.2 = (bf16[128,2048]{1,0:T(8,128)(2,1)S(1)}, bf16[128,2048]{1,0:T(8,128)(2,1)S(1)}, u32[]{:S(2)}, u32[]{:S(2)}) collective-permute-start(bf16[128,2048]{1,0:T(8,128)(2,1)S(1)} %norm.1.refs_5_), channel_id=1, source_target_pairs={{0,2},{1,3},{2,0},{3,1},{4,6},{5,7},{6,4},{7,5},{8,10},{9,11},{10,... | collective-permute-start | bytes 1572872 | tf_op jit(solution)/shard_map/ppermute | solution.py:24
  10.0 5.5 %collective-permute-start = (f32[16,128]{1,0:T(8,128)S(1)}, f32[16,128]{1,0:T(8,128)S(1)}, u32[]{:S(2)}, u32[]{:S(2)}) collective-permute-start(f32[16,128]{1,0:T(8,128)S(1)} %select_reduce_fusion.1), channel_id=1, source_target_pairs={{0,8},{8,16},{16,24},{24,0},{1,9},{9,17},{17,25},{25,1},{2,10},{10... | collective-permute-start | bytes 24584 | tf_op jit(solution)/shard_map/ppermute | solution.py:29
  15.5 4.6 %collective-permute-start.1 = (f32[2,16,128]{2,1,0:T(8,128)S(1)}, f32[2,16,128]{2,1,0:T(8,128)S(1)}, u32[]{:S(2)}, u32[]{:S(2)}) collective-permute-start(f32[2,16,128]{2,1,0:T(8,128)S(1)} %pad_maximum_fusion.3), channel_id=1, source_target_pairs={{0,16},{8,24},{16,0},{24,8},{1,17},{9,25},{17,1},{25,9},{2,18},{10... | collective-permute-start | bytes 49160 | tf_op jit(solution)/shard_map/ppermute | solution.py:29
  21.6 6.4 %collective-permute-start.7 = (bf16[64,2048]{1,0:T(8,128)(2,1)S(1)}, bf16[64,2048]{1,0:T(8,128)(2,1)S(1)}, u32[]{:S(2)}, u32[]{:S(2)}) collective-permute-start(bf16[64,2048]{1,0:T(8,128)(2,1)S(1)} %slice.49), channel_id=1, source_target_pairs={{0,4},{1,5},{2,6},{3,7},{4,0},{5,1},{6,2},{7,3},{8,12},{9,13},{10,... | collective-permute-start | bytes 786440 | tf_op jit(solution)/shard_map/ppermute | solution.py:24
  22.2 6.4 %collective-permute-start.8 = (bf16[64,2048]{1,0:T(8,128)(2,1)S(1)}, bf16[64,2048]{1,0:T(8,128)(2,1)S(1)}, u32[]{:S(2)}, u32[]{:S(2)}) collective-permute-start(bf16[64,2048]{1,0:T(8,128)(2,1)S(1)} %slice.50), channel_id=1, source_target_pairs={{0,2},{1,3},{2,0},{3,1},{4,6},{5,7},{6,4},{7,5},{8,10},{9,11},{10,... | collective-permute-start | bytes 786440 | tf_op jit(solution)/shard_map/ppermute | solution.py:24
  28.6 2.0 collective-permute-start.9
  30.5 32.1 %collective-permute-start.10 = (bf16[512,2048]{1,0:T(8,128)(2,1)}, bf16[512,2048]{1,0:T(8,128)(2,1)S(1)}, u32[]{:S(2)}, u32[]{:S(2)}) collective-permute-start(bf16[512,2048]{1,0:T(8,128)(2,1)} %bitcast.35), channel_id=1, source_target_pairs={{0,1},{1,0},{2,3},{3,2},{4,5},{5,4},{6,7},{7,6},{8,9},{9,8},{10,11... | collective-permute-start | bytes 6291464 | tf_op jit(solution)/shard_map/ppermute | solution.py:24
  32.9 7.2 %collective-permute-start.5 = (bf16[256,2048]{1,0:T(8,128)(2,1)S(1)}, bf16[256,2048]{1,0:T(8,128)(2,1)S(1)}, u32[]{:S(2)}, u32[]{:S(2)}) collective-permute-start(bf16[256,2048]{1,0:T(8,128)(2,1)S(1)} %constant_dynamic-update-slice_fusion.refs_7_), channel_id=1, source_target_pairs={{0,1},{1,0},{2,3},{3,2},{4,5},{5,4},{6,7},{7,6},{8,9},{9,8},{10,11... | collective-permute-start | bytes 3145736 | tf_op jit(solution)/shard_map/ppermute | solution.py:24
  33.4 5.1 %collective-permute-start.3 = (bf16[128,2048]{1,0:T(8,128)(2,1)S(1)}, bf16[128,2048]{1,0:T(8,128)(2,1)S(1)}, u32[]{:S(2)}, u32[]{:S(2)}) collective-permute-start(bf16[128,2048]{1,0:T(8,128)(2,1)S(1)} %norm.1.refs_5_), channel_id=1, source_target_pairs={{0,1},{1,0},{2,3},{3,2},{4,5},{5,4},{6,7},{7,6},{8,9},{9,8},{10,11... | collective-permute-start | bytes 1572872 | tf_op jit(solution)/shard_map/ppermute | solution.py:24
  36.1 20.0 %collective-permute-start.13 = (bf16[128,2048]{1,0:T(8,128)(2,1)S(1)}, bf16[128,2048]{1,0:T(8,128)(2,1)S(1)}, u32[]{:S(2)}, u32[]{:S(2)}) collective-permute-start(bf16[128,2048]{1,0:T(8,128)(2,1)S(1)} %copy-done.3), channel_id=1, source_target_pairs={{0,6},{1,7},{2,4},{3,5},{4,2},{5,3},{6,0},{7,1},{8,14},{9,15},{10,... | collective-permute-start | bytes 1572872 | tf_op jit(solution)/shard_map/ppermute | solution.py:24
  37.8 24.7 %collective-permute-start.12 = (bf16[128,2048]{1,0:T(8,128)(2,1)S(1)}, bf16[128,2048]{1,0:T(8,128)(2,1)S(1)}, u32[]{:S(2)}, u32[]{:S(2)}) collective-permute-start(bf16[128,2048]{1,0:T(8,128)(2,1)S(1)} %copy-done.3), channel_id=1, source_target_pairs={{0,4},{1,5},{2,6},{3,7},{4,0},{5,1},{6,2},{7,3},{8,12},{9,13},{10,... | collective-permute-start | bytes 1572872 | tf_op jit(solution)/shard_map/ppermute | solution.py:24
  38.5 24.2 %collective-permute-start.11 = (bf16[128,2048]{1,0:T(8,128)(2,1)S(1)}, bf16[128,2048]{1,0:T(8,128)(2,1)S(1)}, u32[]{:S(2)}, u32[]{:S(2)}) collective-permute-start(bf16[128,2048]{1,0:T(8,128)(2,1)S(1)} %copy-done.3), channel_id=1, source_target_pairs={{0,2},{1,3},{2,0},{3,1},{4,6},{5,7},{6,4},{7,5},{8,10},{9,11},{10,... | collective-permute-start | bytes 1572872 | tf_op jit(solution)/shard_map/ppermute | solution.py:24
  62.6 5.4 %collective-permute-start.16 = (bf16[256,128]{1,0:T(8,128)(2,1)S(1)}, bf16[256,128]{1,0:T(8,128)(2,1)S(1)}, u32[]{:S(2)}, u32[]{:S(2)}) collective-permute-start(bf16[256,128]{1,0:T(8,128)(2,1)S(1)} %get-tuple-element.172), channel_id=1, source_target_pairs={{0,6},{1,7},{2,4},{3,5},{4,2},{5,3},{6,0},{7,1},{8,14},{9,15},{10,... | collective-permute-start | bytes 196616 | tf_op jit(solution)/shard_map/ppermute | solution.py:24
  64.2 4.7 %collective-permute-start.15 = (bf16[256,128]{1,0:T(8,128)(2,1)S(1)}, bf16[256,128]{1,0:T(8,128)(2,1)S(1)}, u32[]{:S(2)}, u32[]{:S(2)}) collective-permute-start(bf16[256,128]{1,0:T(8,128)(2,1)S(1)} %get-tuple-element.173), channel_id=1, source_target_pairs={{0,4},{1,5},{2,6},{3,7},{4,0},{5,1},{6,2},{7,3},{8,12},{9,13},{10,... | collective-permute-start | bytes 196616 | tf_op jit(solution)/shard_map/ppermute | solution.py:24
  64.9 4.3 %collective-permute-start.14 = (bf16[256,128]{1,0:T(8,128)(2,1)S(1)}, bf16[256,128]{1,0:T(8,128)(2,1)S(1)}, u32[]{:S(2)}, u32[]{:S(2)}) collective-permute-start(bf16[256,128]{1,0:T(8,128)(2,1)S(1)} %get-tuple-element.174), channel_id=1, source_target_pairs={{0,2},{1,3},{2,0},{3,1},{4,6},{5,7},{6,4},{7,5},{8,10},{9,11},{10,... | collective-permute-start | bytes 196616 | tf_op jit(solution)/shard_map/ppermute | solution.py:24
  70.3 2.0 collective-permute-start.17
  72.6 19.9 %collective-permute-start.21 = (bf16[128,2048]{1,0:T(8,128)(2,1)S(1)}, bf16[128,2048]{1,0:T(8,128)(2,1)S(1)}, u32[]{:S(2)}, u32[]{:S(2)}) collective-permute-start(bf16[128,2048]{1,0:T(8,128)(2,1)S(1)} %get-tuple-element.96.rows_ref), channel_id=1, source_target_pairs={{0,8},{8,16},{16,24},{24,0},{1,9},{9,17},{17,25},{25,1},{2,10},{10... | collective-permute-start | bytes 1572872 | tf_op jit(solution)/shard_map/ppermute | solution.py:29
  75.7 10.7 %collective-permute-start.18 = (bf16[80,2048]{1,0:T(8,128)(2,1)S(1)}, bf16[80,2048]{1,0:T(8,128)(2,1)S(1)}, u32[]{:S(2)}, u32[]{:S(2)}) collective-permute-start(bf16[80,2048]{1,0:T(8,128)(2,1)S(1)} %get-tuple-element.101), channel_id=1, source_target_pairs={{0,2},{1,3},{2,0},{3,1},{4,6},{5,7},{6,4},{7,5},{8,10},{9,11},{10,... | collective-permute-start | bytes 983048 | tf_op jit(solution)/shard_map/ppermute | solution.py:24
  76.3 10.3 %collective-permute-start.19 = (bf16[80,2048]{1,0:T(8,128)(2,1)S(1)}, bf16[80,2048]{1,0:T(8,128)(2,1)S(1)}, u32[]{:S(2)}, u32[]{:S(2)}) collective-permute-start(bf16[80,2048]{1,0:T(8,128)(2,1)S(1)} %get-tuple-element.102), channel_id=1, source_target_pairs={{0,4},{1,5},{2,6},{3,7},{4,0},{5,1},{6,2},{7,3},{8,12},{9,13},{10,... | collective-permute-start | bytes 983048 | tf_op jit(solution)/shard_map/ppermute | solution.py:24
  77.6 14.9 %collective-permute-start.20 = (bf16[80,2048]{1,0:T(8,128)(2,1)S(1)}, bf16[80,2048]{1,0:T(8,128)(2,1)S(1)}, u32[]{:S(2)}, u32[]{:S(2)}) collective-permute-start(bf16[80,2048]{1,0:T(8,128)(2,1)S(1)} %get-tuple-element.103), channel_id=1, source_target_pairs={{0,6},{1,7},{2,4},{3,5},{4,2},{5,3},{6,0},{7,1},{8,14},{9,15},{10,... | collective-permute-start | bytes 983048 | tf_op jit(solution)/shard_map/ppermute | solution.py:24
  92.5 14.6 %collective-permute-start.22 = (bf16[128,2048]{1,0:T(8,128)(2,1)S(1)}, bf16[128,2048]{1,0:T(8,128)(2,1)S(1)}, u32[]{:S(2)}, u32[]{:S(2)}) collective-permute-start(bf16[128,2048]{1,0:T(8,128)(2,1)S(1)} %collective-permute-done.21.rows_ref), channel_id=1, source_target_pairs={{0,8},{8,16},{16,24},{24,0},{1,9},{9,17},{17,25},{25,1},{2,10},{10... | collective-permute-start | bytes 1572872 | tf_op jit(solution)/shard_map/ppermute | solution.py:29
  95.5 19.2 %collective-permute-start.26 = (bf16[80,2048]{1,0:T(8,128)(2,1)S(1)}, bf16[80,2048]{1,0:T(8,128)(2,1)S(1)}, u32[]{:S(2)}, u32[]{:S(2)}) collective-permute-start(bf16[80,2048]{1,0:T(8,128)(2,1)S(1)} %get-tuple-element.124), channel_id=1, source_target_pairs={{0,2},{1,3},{2,0},{3,1},{4,6},{5,7},{6,4},{7,5},{8,10},{9,11},{10,... | collective-permute-start | bytes 983048 | tf_op jit(solution)/shard_map/ppermute | solution.py:24
  97.0 17.7 %collective-permute-start.27 = (bf16[80,2048]{1,0:T(8,128)(2,1)S(1)}, bf16[80,2048]{1,0:T(8,128)(2,1)S(1)}, u32[]{:S(2)}, u32[]{:S(2)}) collective-permute-start(bf16[80,2048]{1,0:T(8,128)(2,1)S(1)} %get-tuple-element.125), channel_id=1, source_target_pairs={{0,4},{1,5},{2,6},{3,7},{4,0},{5,1},{6,2},{7,3},{8,12},{9,13},{10,... | collective-permute-start | bytes 983048 | tf_op jit(solution)/shard_map/ppermute | solution.py:24
  97.8 16.9 %collective-permute-start.28 = (bf16[80,2048]{1,0:T(8,128)(2,1)S(1)}, bf16[80,2048]{1,0:T(8,128)(2,1)S(1)}, u32[]{:S(2)}, u32[]{:S(2)}) collective-permute-start(bf16[80,2048]{1,0:T(8,128)(2,1)S(1)} %get-tuple-element.126), channel_id=1, source_target_pairs={{0,6},{1,7},{2,4},{3,5},{4,2},{5,3},{6,0},{7,1},{8,14},{9,15},{10,... | collective-permute-start | bytes 983048 | tf_op jit(solution)/shard_map/ppermute | solution.py:24
  107.1 26.7 %collective-permute-start.29 = (bf16[128,2048]{1,0:T(8,128)(2,1)S(1)}, bf16[128,2048]{1,0:T(8,128)(2,1)S(1)}, u32[]{:S(2)}, u32[]{:S(2)}) collective-permute-start(bf16[128,2048]{1,0:T(8,128)(2,1)S(1)} %collective-permute-done.22.rows_ref), channel_id=1, source_target_pairs={{0,8},{8,16},{16,24},{24,0},{1,9},{9,17},{17,25},{25,1},{2,10},{10... | collective-permute-start | bytes 1572872 | tf_op jit(solution)/shard_map/ppermute | solution.py:29
  116.1 11.1 %collective-permute-start.23 = (bf16[80,2048]{1,0:T(8,128)(2,1)S(1)}, bf16[80,2048]{1,0:T(8,128)(2,1)S(1)}, u32[]{:S(2)}, u32[]{:S(2)}) collective-permute-start(bf16[80,2048]{1,0:T(8,128)(2,1)S(1)} %get-tuple-element.117), channel_id=1, source_target_pairs={{0,2},{1,3},{2,0},{3,1},{4,6},{5,7},{6,4},{7,5},{8,10},{9,11},{10,... | collective-permute-start | bytes 983048 | tf_op jit(solution)/shard_map/ppermute | solution.py:24
  117.3 10.2 %collective-permute-start.24 = (bf16[80,2048]{1,0:T(8,128)(2,1)S(1)}, bf16[80,2048]{1,0:T(8,128)(2,1)S(1)}, u32[]{:S(2)}, u32[]{:S(2)}) collective-permute-start(bf16[80,2048]{1,0:T(8,128)(2,1)S(1)} %get-tuple-element.118), channel_id=1, source_target_pairs={{0,4},{1,5},{2,6},{3,7},{4,0},{5,1},{6,2},{7,3},{8,12},{9,13},{10,... | collective-permute-start | bytes 983048 | tf_op jit(solution)/shard_map/ppermute | solution.py:24
  118.0 13.4 %collective-permute-start.25 = (bf16[80,2048]{1,0:T(8,128)(2,1)S(1)}, bf16[80,2048]{1,0:T(8,128)(2,1)S(1)}, u32[]{:S(2)}, u32[]{:S(2)}) collective-permute-start(bf16[80,2048]{1,0:T(8,128)(2,1)S(1)} %get-tuple-element.119), channel_id=1, source_target_pairs={{0,6},{1,7},{2,4},{3,5},{4,2},{5,3},{6,0},{7,1},{8,14},{9,15},{10,... | collective-permute-start | bytes 983048 | tf_op jit(solution)/shard_map/ppermute | solution.py:24
  131.5 32.1 %collective-permute-start.39 = (bf16[80,2048]{1,0:T(8,128)(2,1)S(1)}, bf16[80,2048]{1,0:T(8,128)(2,1)S(1)}, u32[]{:S(2)}, u32[]{:S(2)}) collective-permute-start(bf16[80,2048]{1,0:T(8,128)(2,1)S(1)} %get-tuple-element.154), channel_id=1, source_target_pairs={{0,2},{1,3},{2,0},{3,1},{4,6},{5,7},{6,4},{7,5},{8,10},{9,11},{10,... | collective-permute-start | bytes 983048 | tf_op jit(solution)/shard_map/ppermute | solution.py:24
  132.6 31.0 %collective-permute-start.40 = (bf16[80,2048]{1,0:T(8,128)(2,1)S(1)}, bf16[80,2048]{1,0:T(8,128)(2,1)S(1)}, u32[]{:S(2)}, u32[]{:S(2)}) collective-permute-start(bf16[80,2048]{1,0:T(8,128)(2,1)S(1)} %get-tuple-element.155), channel_id=1, source_target_pairs={{0,4},{1,5},{2,6},{3,7},{4,0},{5,1},{6,2},{7,3},{8,12},{9,13},{10,... | collective-permute-start | bytes 983048 | tf_op jit(solution)/shard_map/ppermute | solution.py:24
  135.1 14.0 %collective-permute-start.30 = (bf16[80,2048]{1,0:T(8,128)(2,1)S(1)}, bf16[80,2048]{1,0:T(8,128)(2,1)S(1)}, u32[]{:S(2)}, u32[]{:S(2)}) collective-permute-start(bf16[80,2048]{1,0:T(8,128)(2,1)S(1)} %get-tuple-element.145), channel_id=1, source_target_pairs={{0,2},{1,3},{2,0},{3,1},{4,6},{5,7},{6,4},{7,5},{8,10},{9,11},{10,... | collective-permute-start | bytes 983048 | tf_op jit(solution)/shard_map/ppermute | solution.py:24
  135.8 15.1 %collective-permute-start.31 = (bf16[80,2048]{1,0:T(8,128)(2,1)S(1)}, bf16[80,2048]{1,0:T(8,128)(2,1)S(1)}, u32[]{:S(2)}, u32[]{:S(2)}) collective-permute-start(bf16[80,2048]{1,0:T(8,128)(2,1)S(1)} %get-tuple-element.146), channel_id=1, source_target_pairs={{0,4},{1,5},{2,6},{3,7},{4,0},{5,1},{6,2},{7,3},{8,12},{9,13},{10,... | collective-permute-start | bytes 983048 | tf_op jit(solution)/shard_map/ppermute | solution.py:24
  137.0 19.0 %collective-permute-start.32 = (bf16[80,2048]{1,0:T(8,128)(2,1)S(1)}, bf16[80,2048]{1,0:T(8,128)(2,1)S(1)}, u32[]{:S(2)}, u32[]{:S(2)}) collective-permute-start(bf16[80,2048]{1,0:T(8,128)(2,1)S(1)} %get-tuple-element.147), channel_id=1, source_target_pairs={{0,6},{1,7},{2,4},{3,5},{4,2},{5,3},{6,0},{7,1},{8,14},{9,15},{10,... | collective-permute-start | bytes 983048 | tf_op jit(solution)/shard_map/ppermute | solution.py:24
  149.1 14.5 %collective-permute-start.41 = (bf16[80,2048]{1,0:T(8,128)(2,1)S(1)}, bf16[80,2048]{1,0:T(8,128)(2,1)S(1)}, u32[]{:S(2)}, u32[]{:S(2)}) collective-permute-start(bf16[80,2048]{1,0:T(8,128)(2,1)S(1)} %get-tuple-element.156), channel_id=1, source_target_pairs={{0,6},{1,7},{2,4},{3,5},{4,2},{5,3},{6,0},{7,1},{8,14},{9,15},{10,... | collective-permute-start | bytes 983048 | tf_op jit(solution)/shard_map/ppermute | solution.py:24
  163.6 13.1 %collective-permute-start.44 = (bf16[80,2048]{1,0:T(8,128)(2,1)S(1)}, bf16[80,2048]{1,0:T(8,128)(2,1)S(1)}, u32[]{:S(2)}, u32[]{:S(2)}) collective-permute-start(bf16[80,2048]{1,0:T(8,128)(2,1)S(1)} %get-tuple-element.167), channel_id=1, source_target_pairs={{0,2},{1,3},{2,0},{3,1},{4,6},{5,7},{6,4},{7,5},{8,10},{9,11},{10,... | collective-permute-start | bytes 983048 | tf_op jit(solution)/shard_map/ppermute | solution.py:24
  168.7 12.9 %collective-permute-start.45 = (bf16[80,2048]{1,0:T(8,128)(2,1)S(1)}, bf16[80,2048]{1,0:T(8,128)(2,1)S(1)}, u32[]{:S(2)}, u32[]{:S(2)}) collective-permute-start(bf16[80,2048]{1,0:T(8,128)(2,1)S(1)} %get-tuple-element.168), channel_id=1, source_target_pairs={{0,4},{1,5},{2,6},{3,7},{4,0},{5,1},{6,2},{7,3},{8,12},{9,13},{10,... | collective-permute-start | bytes 983048 | tf_op jit(solution)/shard_map/ppermute | solution.py:24
  169.3 15.6 %collective-permute-start.46 = (bf16[80,2048]{1,0:T(8,128)(2,1)S(1)}, bf16[80,2048]{1,0:T(8,128)(2,1)S(1)}, u32[]{:S(2)}, u32[]{:S(2)}) collective-permute-start(bf16[80,2048]{1,0:T(8,128)(2,1)S(1)} %get-tuple-element.169), channel_id=1, source_target_pairs={{0,6},{1,7},{2,4},{3,5},{4,2},{5,3},{6,0},{7,1},{8,14},{9,15},{10,... | collective-permute-start | bytes 983048 | tf_op jit(solution)/shard_map/ppermute | solution.py:24
  170.3 16.5 %collective-permute-start.33 = (bf16[80,2048]{1,0:T(8,128)(2,1)S(1)}, bf16[80,2048]{1,0:T(8,128)(2,1)S(1)}, u32[]{:S(2)}, u32[]{:S(2)}) collective-permute-start(bf16[80,2048]{1,0:T(8,128)(2,1)S(1)} %get-tuple-element.148), channel_id=1, source_target_pairs={{0,2},{1,3},{2,0},{3,1},{4,6},{5,7},{6,4},{7,5},{8,10},{9,11},{10,... | collective-permute-start | bytes 983048 | tf_op jit(solution)/shard_map/ppermute | solution.py:24
  172.2 15.6 %collective-permute-start.34 = (bf16[80,2048]{1,0:T(8,128)(2,1)S(1)}, bf16[80,2048]{1,0:T(8,128)(2,1)S(1)}, u32[]{:S(2)}, u32[]{:S(2)}) collective-permute-start(bf16[80,2048]{1,0:T(8,128)(2,1)S(1)} %get-tuple-element.149), channel_id=1, source_target_pairs={{0,4},{1,5},{2,6},{3,7},{4,0},{5,1},{6,2},{7,3},{8,12},{9,13},{10,... | collective-permute-start | bytes 983048 | tf_op jit(solution)/shard_map/ppermute | solution.py:24
  176.7 17.2 %collective-permute-start.35 = (bf16[80,2048]{1,0:T(8,128)(2,1)S(1)}, bf16[80,2048]{1,0:T(8,128)(2,1)S(1)}, u32[]{:S(2)}, u32[]{:S(2)}) collective-permute-start(bf16[80,2048]{1,0:T(8,128)(2,1)S(1)} %get-tuple-element.150), channel_id=1, source_target_pairs={{0,6},{1,7},{2,4},{3,5},{4,2},{5,3},{6,0},{7,1},{8,14},{9,15},{10,... | collective-permute-start | bytes 983048 | tf_op jit(solution)/shard_map/ppermute | solution.py:24
  181.6 16.6 %collective-permute-start.42 = (bf16[128,2048]{1,0:T(8,128)(2,1)S(1)}, bf16[128,2048]{1,0:T(8,128)(2,1)S(1)}, u32[]{:S(2)}, u32[]{:S(2)}) collective-permute-start(bf16[128,2048]{1,0:T(8,128)(2,1)S(1)} %merge.4), channel_id=1, source_target_pairs={{0,24},{8,0},{16,8},{24,16},{1,25},{9,1},{17,9},{25,17},{2,26},{10... | collective-permute-start | bytes 1572872 | tf_op jit(solution)/shard_map/ppermute | solution.py:29
  186.7 20.9 %collective-permute-start.47 = (bf16[128,2048]{1,0:T(8,128)(2,1)S(1)}, bf16[128,2048]{1,0:T(8,128)(2,1)S(1)}, u32[]{:S(2)}, u32[]{:S(2)}) collective-permute-start(bf16[128,2048]{1,0:T(8,128)(2,1)S(1)} %merge.6), channel_id=1, source_target_pairs={{0,8},{8,16},{16,24},{24,0},{1,9},{9,17},{17,25},{25,1},{2,10},{10... | collective-permute-start | bytes 1572872 | tf_op jit(solution)/shard_map/ppermute | solution.py:29
  195.9 20.1 %collective-permute-start.43 = (bf16[128,2048]{1,0:T(8,128)(2,1)S(1)}, bf16[128,2048]{1,0:T(8,128)(2,1)S(1)}, u32[]{:S(2)}, u32[]{:S(2)}) collective-permute-start(bf16[128,2048]{1,0:T(8,128)(2,1)S(1)} %merge.5), channel_id=1, source_target_pairs={{0,16},{8,24},{16,0},{24,8},{1,17},{9,25},{17,1},{25,9},{2,18},{10... | collective-permute-start | bytes 1572872 | tf_op jit(solution)/shard_map/ppermute | solution.py:29
  196.0 7.1 %collective-permute-start.36 = (bf16[80,2048]{1,0:T(8,128)(2,1)S(1)}, bf16[80,2048]{1,0:T(8,128)(2,1)S(1)}, u32[]{:S(2)}, u32[]{:S(2)}) collective-permute-start(bf16[80,2048]{1,0:T(8,128)(2,1)S(1)} %get-tuple-element.151), channel_id=1, source_target_pairs={{0,2},{1,3},{2,0},{3,1},{4,6},{5,7},{6,4},{7,5},{8,10},{9,11},{10,... | collective-permute-start | bytes 983048 | tf_op jit(solution)/shard_map/ppermute | solution.py:24
  197.0 10.6 %collective-permute-start.37 = (bf16[80,2048]{1,0:T(8,128)(2,1)S(1)}, bf16[80,2048]{1,0:T(8,128)(2,1)S(1)}, u32[]{:S(2)}, u32[]{:S(2)}) collective-permute-start(bf16[80,2048]{1,0:T(8,128)(2,1)S(1)} %get-tuple-element.152), channel_id=1, source_target_pairs={{0,4},{1,5},{2,6},{3,7},{4,0},{5,1},{6,2},{7,3},{8,12},{9,13},{10,... | collective-permute-start | bytes 983048 | tf_op jit(solution)/shard_map/ppermute | solution.py:24
  198.2 9.4 %collective-permute-start.38 = (bf16[80,2048]{1,0:T(8,128)(2,1)S(1)}, bf16[80,2048]{1,0:T(8,128)(2,1)S(1)}, u32[]{:S(2)}, u32[]{:S(2)}) collective-permute-start(bf16[80,2048]{1,0:T(8,128)(2,1)S(1)} %get-tuple-element.153), channel_id=1, source_target_pairs={{0,6},{1,7},{2,4},{3,5},{4,2},{5,3},{6,0},{7,1},{8,14},{9,15},{10,... | collective-permute-start | bytes 983048 | tf_op jit(solution)/shard_map/ppermute | solution.py:24
  (13 other events, 307.8 us)
where the time goes:
time: 223 us; the launch traced here: 219 us
  waiting for transfers between devices  89.8 us (40%)
  Pallas kernels  62.3 us (28%)
  starting transfers between devices  54.5 us (24%)
  other arithmetic  6.5 us (3%)
  local copies, waits for them, and re-layouts  4.06 us (2%)
    ppermute x40, waiting for transfers between devices, swap(): return lax.ppermute(values, 'exp', [(d, d ^ bits) for d in range(count)])  65.8 us
    ppermute x40, starting transfers between devices, swap(): return lax.ppermute(values, 'exp', [(d, d ^ bits) for d in range(count)])  45.4 us
    pallas_call x4, Pallas kernels, expert_rows(): pl.pallas_call(functools.partial(experts_kernel, part, wide), out_shape=[...  30.5 us
    ppermute x8, waiting for transfers between devices, shift(): lax.ppermute(values, 'req', [(d, (d + steps) % count) for d in range(coun...  24 us
    pallas_call x1, Pallas kernels, attention(): pl.pallas_call(functools.partial(attention_kernel, layout, block_rows, ti...  16 us
    ppermute x8, starting transfers between devices, shift(): lax.ppermute(values, 'req', [(d, (d + steps) % count) for d in range(coun...  9.06 us
    pallas_call x4, Pallas kernels, merge(): pl.pallas_call(functools.partial(merge_kernel, count), out_shape=jax.Shap...  8.58 us
    pallas_call x4, Pallas kernels, pick(): pl.pallas_call(pick_kernel, out_shape=[jax.ShapeDtypeStruct((capacity, wi...  5.55 us
  transfers between devices with their start and end apart: 48, of which 26 were waited for; matrix products, arithmetic and copies ran while one was open for 4% of the time, Pallas kernels for 26%

commit v1 on v0

--- a/solution.py
+++ b/solution.py
@@ -228,27 +228,34 @@
 def plane_experts(normed_moe, residual, gates, places, pieces, capacity):
     steps = lax.axis_size("req")
     count = lax.axis_size("exp") // 2
-    rounds = []
-
-    def exchange(parts):
+    def exchange(parts, *earlier):
         mine, *others = parts
-        others = after(tuple(others), *rounds[-2:-1])
-        rounds.append(tuple(swap(part, 2 * at) for at, part in enumerate(others, 1)))
-        return [mine, *rounds[-1]]
-
-    moved, came = normed_moe, []
-    for step in range(steps):
-        following = shift(moved, 1) if step + 1 < steps else None
-        came.append(exchange(pick(moved, gates[step], places[step], count, capacity)))
-        moved = following if step else after(following, rounds[0])
-    made = []
-    for step in range(steps):
-        made.append(expert_rows(after(came[step], *made[-1:]), pieces))
-    sums = []
+        others = after(tuple(others), *earlier)
+        return [mine, *(swap(part, 2 * at) for at, part in enumerate(others, 1))]
+
+    def use(step):
+        return pick(moved[step], gates[step], places[step], count, capacity)
+
+    moved = [normed_moe]
+    came = [exchange(use(0))]
+    made, back, chain = [], [], []
     for step in range(1, steps):
-        sums.append(merge(exchange(made[step]), gates[step], places[step], []))
-    terms = [shift(total, -step) for step, total in enumerate(sums, 1)]
-    return merge(exchange(made[0]), gates[0], places[0], [*terms, residual])
+        moved.append(shift(moved[-1], 1))
+        if step == 1:
+            moved[1] = after(moved[1], came[0])
+    for step in range(1, steps):
+        made.append(expert_rows(after(came[step - 1], *made[-1:]), pieces))
+        if step > 2:
+            back.append(exchange(made[step - 2]))
+        came.append(exchange(use(step), *came[step - 2 : step - 1]))
+    made.append(expert_rows(after(came[-1], made[-1]), pieces))
+    for step in range(1, steps):
+        if step >= len(back) + 1:
+            back.append(exchange(made[step], *back[step - 2 : step - 1]))
+        chain = [merge(back[step - 1], gates[step], places[step], chain)]
+        chain = [shift(chain[0], 1)]
+    last = exchange(made[0], *back[-2:-1])
+    return merge(last, gates[0], places[0], [*chain, residual])
 
 
 LOW = -1e30

time: 223 us -> 214 us (0.960)
  waiting for transfers between devices: 89.8 us -> 82 us
    ppermute x8, waiting for transfers between devices: 24 us -> 7.65 us  [shift(): lax.ppermute(values, 'req', [(d, (d + steps) % count) for d in range(coun...]
    ppermute x40, waiting for transfers between devices: 65.8 us -> 74.3 us  [swap(): return lax.ppermute(values, 'exp', [(d, d ^ bits) for d in range(count)])]
    ppermute x40, starting transfers between devices: 45.4 us -> 42.8 us  [swap(): return lax.ppermute(values, 'exp', [(d, d ^ bits) for d in range(count)])]
  transfers between devices with their start and end apart: 48 -> 48, of which waited for: 26 -> 25; matrix products, arithmetic and copies ran while one was open for 4% -> 4% of each run, Pallas kernels for 26% -> 26%
where the time goes in v1:
time: 214 us; the launch traced here: 210 us
  waiting for transfers between devices  82 us (38%)
  Pallas kernels  62.1 us (29%)
  starting transfers between devices  53.3 us (25%)
  other arithmetic  6.5 us (3%)
  local copies, waits for them, and re-layouts  4.06 us (2%)
    ppermute x40, waiting for transfers between devices, swap(): return lax.ppermute(values, 'exp', [(d, d ^ bits) for d in range(count)])  74.3 us
    ppermute x40, starting transfers between devices, swap(): return lax.ppermute(values, 'exp', [(d, d ^ bits) for d in range(count)])  42.8 us
    pallas_call x4, Pallas kernels, expert_rows(): pl.pallas_call(functools.partial(experts_kernel, part, wide), out_shape=[...  30.8 us
    pallas_call x1, Pallas kernels, attention(): pl.pallas_call(functools.partial(attention_kernel, layout, block_rows, ti...  15.9 us
    ppermute x8, starting transfers between devices, shift(): lax.ppermute(values, 'req', [(d, (d + steps) % count) for d in range(coun...  10.4 us
    pallas_call x4, Pallas kernels, merge(): pl.pallas_call(functools.partial(merge_kernel, count), out_shape=jax.Shap...  8.26 us
    ppermute x8, waiting for transfers between devices, shift(): lax.ppermute(values, 'req', [(d, (d + steps) % count) for d in range(coun...  7.65 us
    pallas_call x4, Pallas kernels, pick(): pl.pallas_call(pick_kernel, out_shape=[jax.ShapeDtypeStruct((capacity, wi...  5.56 us
  transfers between devices with their start and end apart: 48, of which 25 were waited for; matrix products, arithmetic and copies ran while one was open for 4% of the time, Pallas kernels for 26%

profile of v1, /device:TPU:0, one launch (start us, length us, event | category | flops | bytes accessed | tf_op | source)
XLA Modules:
  0.0 209.8 jit_solution(534467107550580245)
XLA Ops:
  3.1 2.6 %collective-permute-start.4 = (bf16[128,2048]{1,0:T(8,128)(2,1)S(1)}, bf16[128,2048]{1,0:T(8,128)(2,1)S(1)}, u32[]{:S(2)}, u32[]{:S(2)}) collective-permute-start(bf16[128,2048]{1,0:T(8,128)(2,1)S(1)} %norm.1.refs_5_), channel_id=1, source_target_pairs={{0,4},{1,5},{2,6},{3,7},{4,0},{5,1},{6,2},{7,3},{8,12},{9,13},{10,... | collective-permute-start | bytes 1572872 | tf_op jit(solution)/shard_map/ppermute | solution.py:24
  5.7 1.5 collective-permute-start.2
  10.0 1.6 collective-permute-start
  11.7 3.9 %collective-permute-done = f32[16,128]{1,0:T(8,128)S(1)} collective-permute-done((f32[16,128]{1,0:T(8,128)S(1)}, f32[16,128]{1,0:T(8,128)S(1)}, u32[]{:S(2)}, u32[]{:S(2)}) %collective-permute-start) | collective-permute-done | bytes 8224 | tf_op jit(solution)/shard_map/ppermute | solution.py:29
  16.4 3.8 %collective-permute-done.1 = f32[2,16,128]{2,1,0:T(8,128)S(1)} collective-permute-done((f32[2,16,128]{2,1,0:T(8,128)S(1)}, f32[2,16,128]{2,1,0:T(8,128)S(1)}, u32[]{:S(2)}, u32[]{:S(2)}) %collective-permute-start.1) | collective-permute-done | bytes 16416 | tf_op jit(solution)/shard_map/ppermute | solution.py:29
  22.5 5.5 %collective-permute-done.7 = bf16[64,2048]{1,0:T(8,128)(2,1)S(1)} collective-permute-done((bf16[64,2048]{1,0:T(8,128)(2,1)S(1)}, bf16[64,2048]{1,0:T(8,128)(2,1)S(1)}, u32[]{:S(2)}, u32[]{:S(2)}) %collective-permute-start.7) | collective-permute-done | bytes 262176 | tf_op jit(solution)/shard_map/ppermute | solution.py:24
  28.6 1.9 collective-permute-done.9.refs_10_
  34.2 1.9 fusion
  36.1 1.7 collective-permute-start.13
  40.1 15.9 %attention.1 = (bf16[1024,128]{1,0:T(8,128)(2,1)S(1)}, bf16[2,1024,128]{2,1,0:T(8,128)(2,1)}) custom-call(s32[1]{0:T(128)} %bitcast.7.refs_0_, s32[1]{0:T(128)} %copy.20.refs_1_, s32[4]{0:T(128)S(1)} %copy-done.7, s32[4,32]{1,0:T(4,128)S(1)} %copy-done.6, s32[1,32]{1,0:T(1,128)S(1)} %copy-done.8, bf16[128,2048]{1,0:T(8,128)(2,1)S(1)} %norm.1.refs_5_, ...), custom_call_target="tpu_custom_call" | custom-call | flops 4294967296 | bytes 20971520 | tf_op jit(solution)/shard_map/attention/pallas_call | solution.py:445
  56.1 6.4 %collective-permute-done.12.refs_6_ = bf16[128,2048]{1,0:T(8,128)(2,1)S(1)} collective-permute-done((bf16[128,2048]{1,0:T(8,128)(2,1)S(1)}, bf16[128,2048]{1,0:T(8,128)(2,1)S(1)}, u32[]{:S(2)}, u32[]{:S(2)}) %collective-permute-start.12) | collective-permute-done | bytes 524320 | tf_op jit(solution)/shard_map/ppermute | solution.py:24
  62.6 1.6 collective-permute-start.16
  66.2 1.9 collective-permute-done.16.refs_3_
  70.2 1.9 collective-permute-done.17.refs_1_
  72.4 1.6 collective-permute-start.21
  77.4 1.6 collective-permute-start.20
  79.0 7.1 %collective-permute-done.18.refs_1_ = bf16[80,2048]{1,0:T(8,128)(2,1)S(1)} collective-permute-done((bf16[80,2048]{1,0:T(8,128)(2,1)S(1)}, bf16[80,2048]{1,0:T(8,128)(2,1)S(1)}, u32[]{:S(2)}, u32[]{:S(2)}) %collective-permute-start.18) | collective-permute-done | bytes 327712 | tf_op jit(solution)/shard_map/ppermute | solution.py:24
  86.5 5.9 %collective-permute-done.20.refs_3_ = bf16[80,2048]{1,0:T(8,128)(2,1)S(1)} collective-permute-done((bf16[80,2048]{1,0:T(8,128)(2,1)S(1)}, bf16[80,2048]{1,0:T(8,128)(2,1)S(1)}, u32[]{:S(2)}, u32[]{:S(2)}) %collective-permute-start.20) | collective-permute-done | bytes 327712 | tf_op jit(solution)/shard_map/ppermute | solution.py:24
  92.3 1.6 collective-permute-start.22
  93.9 1.4 pick.6
  95.3 1.5 collective-permute-start.26
  98.9 7.6 %experts.4 = (bf16[80,2048]{1,0:T(8,128)(2,1)S(1)}, bf16[80,2048]{1,0:T(8,128)(2,1)S(1)}, bf16[80,2048]{1,0:T(8,128)(2,1)S(1)}, bf16[80,2048]{1,0:T(8,128)(2,1)S(1)}) custom-call(bf16[80,2048]{1,0:T(8,128)(2,1)S(1)} %get-tuple-element.104.refs_0_, bf16[80,2048]{1,0:T(8,128)(2,1)S(1)} %collective-permute-done.18.refs_1_, ...), custom_call_target="tpu_custom_call" | custom-call | flops 4026531840 | bytes 16777216 | tf_op jit(solution)/shard_map/experts/pallas_call | solution.py:116
  106.5 5.0 %collective-permute-done.27.refs_2_ = bf16[80,2048]{1,0:T(8,128)(2,1)S(1)} collective-permute-done((bf16[80,2048]{1,0:T(8,128)(2,1)S(1)}, bf16[80,2048]{1,0:T(8,128)(2,1)S(1)}, u32[]{:S(2)}, u32[]{:S(2)}) %collective-permute-start.27) | collective-permute-done | bytes 327712 | tf_op jit(solution)/shard_map/ppermute | solution.py:24
  111.5 1.4 pick.5
  116.5 7.6 %experts.5 = (bf16[80,2048]{1,0:T(8,128)(2,1)S(1)}, bf16[80,2048]{1,0:T(8,128)(2,1)S(1)}, bf16[80,2048]{1,0:T(8,128)(2,1)S(1)}, bf16[80,2048]{1,0:T(8,128)(2,1)S(1)}) custom-call(bf16[80,2048]{1,0:T(8,128)(2,1)S(1)} %get-tuple-element.127.refs_0_, bf16[80,2048]{1,0:T(8,128)(2,1)S(1)} %collective-permute-done.26.refs_1_, ...), custom_call_target="tpu_custom_call" | custom-call | flops 4026531840 | bytes 16777216 | tf_op jit(solution)/shard_map/experts/pallas_call | solution.py:116
  127.6 1.6 collective-permute-start.38
  129.2 1.6 collective-permute-done.25.refs_3_
  130.8 8.0 %experts.6 = (bf16[80,2048]{1,0:T(8,128)(2,1)S(1)}, bf16[80,2048]{1,0:T(8,128)(2,1)S(1)}, bf16[80,2048]{1,0:T(8,128)(2,1)S(1)}, bf16[80,2048]{1,0:T(8,128)(2,1)S(1)}) custom-call(bf16[80,2048]{1,0:T(8,128)(2,1)S(1)} %get-tuple-element.135.refs_0_, bf16[80,2048]{1,0:T(8,128)(2,1)S(1)} %collective-permute-done.23.refs_1_, ...), custom_call_target="tpu_custom_call" | custom-call | flops 4026531840 | bytes 16777216 | tf_op jit(solution)/shard_map/experts/pallas_call | solution.py:116
  138.8 3.3 %collective-permute-done.30.refs_2_ = bf16[80,2048]{1,0:T(8,128)(2,1)S(1)} collective-permute-done((bf16[80,2048]{1,0:T(8,128)(2,1)S(1)}, bf16[80,2048]{1,0:T(8,128)(2,1)S(1)}, u32[]{:S(2)}, u32[]{:S(2)}) %collective-permute-start.30) | collective-permute-done | bytes 327712 | tf_op jit(solution)/shard_map/ppermute | solution.py:24
  144.0 1.8 merge.4
  145.8 1.6 collective-permute-start.45
  147.4 1.6 collective-permute-start.34
  149.1 1.4 pick.7
  153.7 4.4 %collective-permute-done.33.refs_2_ = bf16[80,2048]{1,0:T(8,128)(2,1)S(1)} collective-permute-done((bf16[80,2048]{1,0:T(8,128)(2,1)S(1)}, bf16[80,2048]{1,0:T(8,128)(2,1)S(1)}, u32[]{:S(2)}, u32[]{:S(2)}) %collective-permute-start.33) | collective-permute-done | bytes 327712 | tf_op jit(solution)/shard_map/ppermute | solution.py:24
  158.1 2.4 %collective-permute-start.41 = (bf16[80,2048]{1,0:T(8,128)(2,1)S(1)}, bf16[80,2048]{1,0:T(8,128)(2,1)S(1)}, u32[]{:S(2)}, u32[]{:S(2)}) collective-permute-start(bf16[80,2048]{1,0:T(8,128)(2,1)S(1)} %get-tuple-element.158), channel_id=1, source_target_pairs={{0,6},{1,7},{2,4},{3,5},{4,2},{5,3},{6,0},{7,1},{8,14},{9,15},{10,... | collective-permute-start | bytes 983048 | tf_op jit(solution)/shard_map/ppermute | solution.py:24
  160.5 1.9 merge.5
  162.3 1.6 collective-permute-start.46
  163.9 2.4 %collective-permute-done.39.refs_1_ = bf16[80,2048]{1,0:T(8,128)(2,1)S(1)} collective-permute-done((bf16[80,2048]{1,0:T(8,128)(2,1)S(1)}, bf16[80,2048]{1,0:T(8,128)(2,1)S(1)}, u32[]{:S(2)}, u32[]{:S(2)}) %collective-permute-start.39) | collective-permute-done | bytes 327712 | tf_op jit(solution)/shard_map/ppermute | solution.py:24
  166.3 4.2 %collective-permute-done.40.refs_2_ = bf16[80,2048]{1,0:T(8,128)(2,1)S(1)} collective-permute-done((bf16[80,2048]{1,0:T(8,128)(2,1)S(1)}, bf16[80,2048]{1,0:T(8,128)(2,1)S(1)}, u32[]{:S(2)}, u32[]{:S(2)}) %collective-permute-start.40) | collective-permute-done | bytes 327712 | tf_op jit(solution)/shard_map/ppermute | solution.py:24
  170.5 7.7 %experts.7 = (bf16[80,2048]{1,0:T(8,128)(2,1)S(1)}, bf16[80,2048]{1,0:T(8,128)(2,1)S(1)}, bf16[80,2048]{1,0:T(8,128)(2,1)S(1)}, bf16[80,2048]{1,0:T(8,128)(2,1)S(1)}) custom-call(bf16[80,2048]{1,0:T(8,128)(2,1)S(1)} %get-tuple-element.159.refs_0_, bf16[80,2048]{1,0:T(8,128)(2,1)S(1)} %collective-permute-done.39.refs_1_, ...), custom_call_target="tpu_custom_call" | custom-call | flops 4026531840 | bytes 16777216 | tf_op jit(solution)/shard_map/experts/pallas_call | solution.py:116
  178.3 1.6 collective-permute-start.42
  181.8 5.9 %collective-permute-done.42.refs_1_ = bf16[80,2048]{1,0:T(8,128)(2,1)S(1)} collective-permute-done((bf16[80,2048]{1,0:T(8,128)(2,1)S(1)}, bf16[80,2048]{1,0:T(8,128)(2,1)S(1)}, u32[]{:S(2)}, u32[]{:S(2)}) %collective-permute-start.42) | collective-permute-done | bytes 327712 | tf_op jit(solution)/shard_map/ppermute | solution.py:24
  187.8 4.9 %collective-permute-done.43.refs_2_ = bf16[80,2048]{1,0:T(8,128)(2,1)S(1)} collective-permute-done((bf16[80,2048]{1,0:T(8,128)(2,1)S(1)}, bf16[80,2048]{1,0:T(8,128)(2,1)S(1)}, u32[]{:S(2)}, u32[]{:S(2)}) %collective-permute-start.43) | collective-permute-done | bytes 327712 | tf_op jit(solution)/shard_map/ppermute | solution.py:24
  192.7 1.8 merge.6
  196.5 1.7 collective-permute-start.37
  198.2 3.8 %collective-permute-done.35.refs_1_ = bf16[80,2048]{1,0:T(8,128)(2,1)S(1)} collective-permute-done((bf16[80,2048]{1,0:T(8,128)(2,1)S(1)}, bf16[80,2048]{1,0:T(8,128)(2,1)S(1)}, u32[]{:S(2)}, u32[]{:S(2)}) %collective-permute-start.35) | collective-permute-done | bytes 327712 | tf_op jit(solution)/shard_map/ppermute | solution.py:24
  202.0 4.9 %collective-permute-done.36.refs_2_ = bf16[80,2048]{1,0:T(8,128)(2,1)S(1)} collective-permute-done((bf16[80,2048]{1,0:T(8,128)(2,1)S(1)}, bf16[80,2048]{1,0:T(8,128)(2,1)S(1)}, u32[]{:S(2)}, u32[]{:S(2)}) %collective-permute-start.36) | collective-permute-done | bytes 327712 | tf_op jit(solution)/shard_map/ppermute | solution.py:24
  206.9 2.7 %merge.7 = bf16[128,2048]{1,0:T(8,128)(2,1)} custom-call(f32[8,128]{1,0:T(8,128)S(1)} %get-tuple-element.183.gate_ref, s32[8,128]{1,0:T(8,128)S(1)} %get-tuple-element.179.place_ref, bf16[80,2048]{1,0:T(8,128)(2,1)S(1)} %get-tuple-element.108.refs_0_, bf16[80,2048]{1,0:T(8,128)(2,1)S(1)} %collective-permute-done.35.refs_1_, ...), custom_call_target="tpu_custom_call" | custom-call | flops 167772160 | bytes 1048576 | tf_op jit(solution)/shard_map/merge/pallas_call | solution.py:209
  (116 shorter events, 40.6 us)
Async XLA Ops:
  0.6 20.9 %collective-permute-start.6 = (bf16[2048,1024]{1,0:T(8,128)(2,1)}, bf16[2048,1024]{1,0:T(8,128)(2,1)}, u32[]{:S(2)}, u32[]{:S(2)}) collective-permute-start(bf16[2048,1024]{1,0:T(8,128)(2,1)} %bitcast.30), channel_id=1, source_target_pairs={{0,1},{1,0},{2,3},{3,2},{4,5},{5,4},{6,7},{7,6},{8,9},{9,8},{10,11... | collective-permute-start | bytes 12582920 | tf_op jit(solution)/shard_map/ppermute | solution.py:24
  3.1 18.4 %collective-permute-start.4 = (bf16[128,2048]{1,0:T(8,128)(2,1)S(1)}, bf16[128,2048]{1,0:T(8,128)(2,1)S(1)}, u32[]{:S(2)}, u32[]{:S(2)}) collective-permute-start(bf16[128,2048]{1,0:T(8,128)(2,1)S(1)} %norm.1.refs_5_), channel_id=1, source_target_pairs={{0,4},{1,5},{2,6},{3,7},{4,0},{5,1},{6,2},{7,3},{8,12},{9,13},{10,... | collective-permute-start | bytes 1572872 | tf_op jit(solution)/shard_map/ppermute | solution.py:24
  5.7 15.8 %collective-permute-start.2 = (bf16[128,2048]{1,0:T(8,128)(2,1)S(1)}, bf16[128,2048]{1,0:T(8,128)(2,1)S(1)}, u32[]{:S(2)}, u32[]{:S(2)}) collective-permute-start(bf16[128,2048]{1,0:T(8,128)(2,1)S(1)} %norm.1.refs_5_), channel_id=1, source_target_pairs={{0,2},{1,3},{2,0},{3,1},{4,6},{5,7},{6,4},{7,5},{8,10},{9,11},{10,... | collective-permute-start | bytes 1572872 | tf_op jit(solution)/shard_map/ppermute | solution.py:24
  10.0 5.5 %collective-permute-start = (f32[16,128]{1,0:T(8,128)S(1)}, f32[16,128]{1,0:T(8,128)S(1)}, u32[]{:S(2)}, u32[]{:S(2)}) collective-permute-start(f32[16,128]{1,0:T(8,128)S(1)} %select_reduce_fusion.1), channel_id=1, source_target_pairs={{0,8},{8,16},{16,24},{24,0},{1,9},{9,17},{17,25},{25,1},{2,10},{10... | collective-permute-start | bytes 24584 | tf_op jit(solution)/shard_map/ppermute | solution.py:29
  15.5 4.6 %collective-permute-start.1 = (f32[2,16,128]{2,1,0:T(8,128)S(1)}, f32[2,16,128]{2,1,0:T(8,128)S(1)}, u32[]{:S(2)}, u32[]{:S(2)}) collective-permute-start(f32[2,16,128]{2,1,0:T(8,128)S(1)} %pad_maximum_fusion.3), channel_id=1, source_target_pairs={{0,16},{8,24},{16,0},{24,8},{1,17},{9,25},{17,1},{25,9},{2,18},{10... | collective-permute-start | bytes 49160 | tf_op jit(solution)/shard_map/ppermute | solution.py:29
  21.6 6.4 %collective-permute-start.7 = (bf16[64,2048]{1,0:T(8,128)(2,1)S(1)}, bf16[64,2048]{1,0:T(8,128)(2,1)S(1)}, u32[]{:S(2)}, u32[]{:S(2)}) collective-permute-start(bf16[64,2048]{1,0:T(8,128)(2,1)S(1)} %slice.49), channel_id=1, source_target_pairs={{0,4},{1,5},{2,6},{3,7},{4,0},{5,1},{6,2},{7,3},{8,12},{9,13},{10,... | collective-permute-start | bytes 786440 | tf_op jit(solution)/shard_map/ppermute | solution.py:24
  22.2 6.4 %collective-permute-start.8 = (bf16[64,2048]{1,0:T(8,128)(2,1)S(1)}, bf16[64,2048]{1,0:T(8,128)(2,1)S(1)}, u32[]{:S(2)}, u32[]{:S(2)}) collective-permute-start(bf16[64,2048]{1,0:T(8,128)(2,1)S(1)} %slice.50), channel_id=1, source_target_pairs={{0,2},{1,3},{2,0},{3,1},{4,6},{5,7},{6,4},{7,5},{8,10},{9,11},{10,... | collective-permute-start | bytes 786440 | tf_op jit(solution)/shard_map/ppermute | solution.py:24
  28.6 2.0 collective-permute-start.9
  30.5 32.1 %collective-permute-start.10 = (bf16[512,2048]{1,0:T(8,128)(2,1)}, bf16[512,2048]{1,0:T(8,128)(2,1)S(1)}, u32[]{:S(2)}, u32[]{:S(2)}) collective-permute-start(bf16[512,2048]{1,0:T(8,128)(2,1)} %bitcast.35), channel_id=1, source_target_pairs={{0,1},{1,0},{2,3},{3,2},{4,5},{5,4},{6,7},{7,6},{8,9},{9,8},{10,11... | collective-permute-start | bytes 6291464 | tf_op jit(solution)/shard_map/ppermute | solution.py:24
  32.9 7.2 %collective-permute-start.5 = (bf16[256,2048]{1,0:T(8,128)(2,1)S(1)}, bf16[256,2048]{1,0:T(8,128)(2,1)S(1)}, u32[]{:S(2)}, u32[]{:S(2)}) collective-permute-start(bf16[256,2048]{1,0:T(8,128)(2,1)S(1)} %constant_dynamic-update-slice_fusion.refs_7_), channel_id=1, source_target_pairs={{0,1},{1,0},{2,3},{3,2},{4,5},{5,4},{6,7},{7,6},{8,9},{9,8},{10,11... | collective-permute-start | bytes 3145736 | tf_op jit(solution)/shard_map/ppermute | solution.py:24
  33.4 5.1 %collective-permute-start.3 = (bf16[128,2048]{1,0:T(8,128)(2,1)S(1)}, bf16[128,2048]{1,0:T(8,128)(2,1)S(1)}, u32[]{:S(2)}, u32[]{:S(2)}) collective-permute-start(bf16[128,2048]{1,0:T(8,128)(2,1)S(1)} %norm.1.refs_5_), channel_id=1, source_target_pairs={{0,1},{1,0},{2,3},{3,2},{4,5},{5,4},{6,7},{7,6},{8,9},{9,8},{10,11... | collective-permute-start | bytes 1572872 | tf_op jit(solution)/shard_map/ppermute | solution.py:24
  36.1 20.0 %collective-permute-start.13 = (bf16[128,2048]{1,0:T(8,128)(2,1)S(1)}, bf16[128,2048]{1,0:T(8,128)(2,1)S(1)}, u32[]{:S(2)}, u32[]{:S(2)}) collective-permute-start(bf16[128,2048]{1,0:T(8,128)(2,1)S(1)} %copy-done.3), channel_id=1, source_target_pairs={{0,6},{1,7},{2,4},{3,5},{4,2},{5,3},{6,0},{7,1},{8,14},{9,15},{10,... | collective-permute-start | bytes 1572872 | tf_op jit(solution)/shard_map/ppermute | solution.py:24
  37.8 24.7 %collective-permute-start.12 = (bf16[128,2048]{1,0:T(8,128)(2,1)S(1)}, bf16[128,2048]{1,0:T(8,128)(2,1)S(1)}, u32[]{:S(2)}, u32[]{:S(2)}) collective-permute-start(bf16[128,2048]{1,0:T(8,128)(2,1)S(1)} %copy-done.3), channel_id=1, source_target_pairs={{0,4},{1,5},{2,6},{3,7},{4,0},{5,1},{6,2},{7,3},{8,12},{9,13},{10,... | collective-permute-start | bytes 1572872 | tf_op jit(solution)/shard_map/ppermute | solution.py:24
  38.5 24.2 %collective-permute-start.11 = (bf16[128,2048]{1,0:T(8,128)(2,1)S(1)}, bf16[128,2048]{1,0:T(8,128)(2,1)S(1)}, u32[]{:S(2)}, u32[]{:S(2)}) collective-permute-start(bf16[128,2048]{1,0:T(8,128)(2,1)S(1)} %copy-done.3), channel_id=1, source_target_pairs={{0,2},{1,3},{2,0},{3,1},{4,6},{5,7},{6,4},{7,5},{8,10},{9,11},{10,... | collective-permute-start | bytes 1572872 | tf_op jit(solution)/shard_map/ppermute | solution.py:24
  62.6 5.4 %collective-permute-start.16 = (bf16[256,128]{1,0:T(8,128)(2,1)S(1)}, bf16[256,128]{1,0:T(8,128)(2,1)S(1)}, u32[]{:S(2)}, u32[]{:S(2)}) collective-permute-start(bf16[256,128]{1,0:T(8,128)(2,1)S(1)} %get-tuple-element.172), channel_id=1, source_target_pairs={{0,6},{1,7},{2,4},{3,5},{4,2},{5,3},{6,0},{7,1},{8,14},{9,15},{10,... | collective-permute-start | bytes 196616 | tf_op jit(solution)/shard_map/ppermute | solution.py:24
  64.2 4.7 %collective-permute-start.15 = (bf16[256,128]{1,0:T(8,128)(2,1)S(1)}, bf16[256,128]{1,0:T(8,128)(2,1)S(1)}, u32[]{:S(2)}, u32[]{:S(2)}) collective-permute-start(bf16[256,128]{1,0:T(8,128)(2,1)S(1)} %get-tuple-element.173), channel_id=1, source_target_pairs={{0,4},{1,5},{2,6},{3,7},{4,0},{5,1},{6,2},{7,3},{8,12},{9,13},{10,... | collective-permute-start | bytes 196616 | tf_op jit(solution)/shard_map/ppermute | solution.py:24
  64.9 4.3 %collective-permute-start.14 = (bf16[256,128]{1,0:T(8,128)(2,1)S(1)}, bf16[256,128]{1,0:T(8,128)(2,1)S(1)}, u32[]{:S(2)}, u32[]{:S(2)}) collective-permute-start(bf16[256,128]{1,0:T(8,128)(2,1)S(1)} %get-tuple-element.174), channel_id=1, source_target_pairs={{0,2},{1,3},{2,0},{3,1},{4,6},{5,7},{6,4},{7,5},{8,10},{9,11},{10,... | collective-permute-start | bytes 196616 | tf_op jit(solution)/shard_map/ppermute | solution.py:24
  70.1 2.0 collective-permute-start.17
  72.4 19.9 %collective-permute-start.21 = (bf16[128,2048]{1,0:T(8,128)(2,1)S(1)}, bf16[128,2048]{1,0:T(8,128)(2,1)S(1)}, u32[]{:S(2)}, u32[]{:S(2)}) collective-permute-start(bf16[128,2048]{1,0:T(8,128)(2,1)S(1)} %get-tuple-element.96.rows_ref), channel_id=1, source_target_pairs={{0,8},{8,16},{16,24},{24,0},{1,9},{9,17},{17,25},{25,1},{2,10},{10... | collective-permute-start | bytes 1572872 | tf_op jit(solution)/shard_map/ppermute | solution.py:29
  75.5 10.7 %collective-permute-start.18 = (bf16[80,2048]{1,0:T(8,128)(2,1)S(1)}, bf16[80,2048]{1,0:T(8,128)(2,1)S(1)}, u32[]{:S(2)}, u32[]{:S(2)}) collective-permute-start(bf16[80,2048]{1,0:T(8,128)(2,1)S(1)} %get-tuple-element.101), channel_id=1, source_target_pairs={{0,2},{1,3},{2,0},{3,1},{4,6},{5,7},{6,4},{7,5},{8,10},{9,11},{10,... | collective-permute-start | bytes 983048 | tf_op jit(solution)/shard_map/ppermute | solution.py:24
  76.1 10.3 %collective-permute-start.19 = (bf16[80,2048]{1,0:T(8,128)(2,1)S(1)}, bf16[80,2048]{1,0:T(8,128)(2,1)S(1)}, u32[]{:S(2)}, u32[]{:S(2)}) collective-permute-start(bf16[80,2048]{1,0:T(8,128)(2,1)S(1)} %get-tuple-element.102), channel_id=1, source_target_pairs={{0,4},{1,5},{2,6},{3,7},{4,0},{5,1},{6,2},{7,3},{8,12},{9,13},{10,... | collective-permute-start | bytes 983048 | tf_op jit(solution)/shard_map/ppermute | solution.py:24
  77.4 14.9 %collective-permute-start.20 = (bf16[80,2048]{1,0:T(8,128)(2,1)S(1)}, bf16[80,2048]{1,0:T(8,128)(2,1)S(1)}, u32[]{:S(2)}, u32[]{:S(2)}) collective-permute-start(bf16[80,2048]{1,0:T(8,128)(2,1)S(1)} %get-tuple-element.103), channel_id=1, source_target_pairs={{0,6},{1,7},{2,4},{3,5},{4,2},{5,3},{6,0},{7,1},{8,14},{9,15},{10,... | collective-permute-start | bytes 983048 | tf_op jit(solution)/shard_map/ppermute | solution.py:24
  92.3 19.2 %collective-permute-start.22 = (bf16[128,2048]{1,0:T(8,128)(2,1)S(1)}, bf16[128,2048]{1,0:T(8,128)(2,1)S(1)}, u32[]{:S(2)}, u32[]{:S(2)}) collective-permute-start(bf16[128,2048]{1,0:T(8,128)(2,1)S(1)} %collective-permute-done.21.rows_ref), channel_id=1, source_target_pairs={{0,8},{8,16},{16,24},{24,0},{1,9},{9,17},{17,25},{25,1},{2,10},{10... | collective-permute-start | bytes 1572872 | tf_op jit(solution)/shard_map/ppermute | solution.py:29
  95.3 11.1 %collective-permute-start.26 = (bf16[80,2048]{1,0:T(8,128)(2,1)S(1)}, bf16[80,2048]{1,0:T(8,128)(2,1)S(1)}, u32[]{:S(2)}, u32[]{:S(2)}) collective-permute-start(bf16[80,2048]{1,0:T(8,128)(2,1)S(1)} %get-tuple-element.124), channel_id=1, source_target_pairs={{0,2},{1,3},{2,0},{3,1},{4,6},{5,7},{6,4},{7,5},{8,10},{9,11},{10,... | collective-permute-start | bytes 983048 | tf_op jit(solution)/shard_map/ppermute | solution.py:24
  96.8 14.7 %collective-permute-start.27 = (bf16[80,2048]{1,0:T(8,128)(2,1)S(1)}, bf16[80,2048]{1,0:T(8,128)(2,1)S(1)}, u32[]{:S(2)}, u32[]{:S(2)}) collective-permute-start(bf16[80,2048]{1,0:T(8,128)(2,1)S(1)} %get-tuple-element.125), channel_id=1, source_target_pairs={{0,4},{1,5},{2,6},{3,7},{4,0},{5,1},{6,2},{7,3},{8,12},{9,13},{10,... | collective-permute-start | bytes 983048 | tf_op jit(solution)/shard_map/ppermute | solution.py:24
  97.6 13.9 %collective-permute-start.28 = (bf16[80,2048]{1,0:T(8,128)(2,1)S(1)}, bf16[80,2048]{1,0:T(8,128)(2,1)S(1)}, u32[]{:S(2)}, u32[]{:S(2)}) collective-permute-start(bf16[80,2048]{1,0:T(8,128)(2,1)S(1)} %get-tuple-element.126), channel_id=1, source_target_pairs={{0,6},{1,7},{2,4},{3,5},{4,2},{5,3},{6,0},{7,1},{8,14},{9,15},{10,... | collective-permute-start | bytes 983048 | tf_op jit(solution)/shard_map/ppermute | solution.py:24
  112.9 13.4 %collective-permute-start.23 = (bf16[80,2048]{1,0:T(8,128)(2,1)S(1)}, bf16[80,2048]{1,0:T(8,128)(2,1)S(1)}, u32[]{:S(2)}, u32[]{:S(2)}) collective-permute-start(bf16[80,2048]{1,0:T(8,128)(2,1)S(1)} %get-tuple-element.117), channel_id=1, source_target_pairs={{0,2},{1,3},{2,0},{3,1},{4,6},{5,7},{6,4},{7,5},{8,10},{9,11},{10,... | collective-permute-start | bytes 983048 | tf_op jit(solution)/shard_map/ppermute | solution.py:24
  113.9 13.7 %collective-permute-start.24 = (bf16[80,2048]{1,0:T(8,128)(2,1)S(1)}, bf16[80,2048]{1,0:T(8,128)(2,1)S(1)}, u32[]{:S(2)}, u32[]{:S(2)}) collective-permute-start(bf16[80,2048]{1,0:T(8,128)(2,1)S(1)} %get-tuple-element.118), channel_id=1, source_target_pairs={{0,4},{1,5},{2,6},{3,7},{4,0},{5,1},{6,2},{7,3},{8,12},{9,13},{10,... | collective-permute-start | bytes 983048 | tf_op jit(solution)/shard_map/ppermute | solution.py:24
  115.1 15.7 %collective-permute-start.25 = (bf16[80,2048]{1,0:T(8,128)(2,1)S(1)}, bf16[80,2048]{1,0:T(8,128)(2,1)S(1)}, u32[]{:S(2)}, u32[]{:S(2)}) collective-permute-start(bf16[80,2048]{1,0:T(8,128)(2,1)S(1)} %get-tuple-element.119), channel_id=1, source_target_pairs={{0,6},{1,7},{2,4},{3,5},{4,2},{5,3},{6,0},{7,1},{8,14},{9,15},{10,... | collective-permute-start | bytes 983048 | tf_op jit(solution)/shard_map/ppermute | solution.py:24
  124.1 14.7 %collective-permute-start.29 = (bf16[80,2048]{1,0:T(8,128)(2,1)S(1)}, bf16[80,2048]{1,0:T(8,128)(2,1)S(1)}, u32[]{:S(2)}, u32[]{:S(2)}) collective-permute-start(bf16[80,2048]{1,0:T(8,128)(2,1)S(1)} %get-tuple-element.143), channel_id=1, source_target_pairs={{0,2},{1,3},{2,0},{3,1},{4,6},{5,7},{6,4},{7,5},{8,10},{9,11},{10,... | collective-permute-start | bytes 983048 | tf_op jit(solution)/shard_map/ppermute | solution.py:24
  125.0 17.0 %collective-permute-start.30 = (bf16[80,2048]{1,0:T(8,128)(2,1)S(1)}, bf16[80,2048]{1,0:T(8,128)(2,1)S(1)}, u32[]{:S(2)}, u32[]{:S(2)}) collective-permute-start(bf16[80,2048]{1,0:T(8,128)(2,1)S(1)} %get-tuple-element.144), channel_id=1, source_target_pairs={{0,4},{1,5},{2,6},{3,7},{4,0},{5,1},{6,2},{7,3},{8,12},{9,13},{10,... | collective-permute-start | bytes 983048 | tf_op jit(solution)/shard_map/ppermute | solution.py:24
  126.3 15.8 %collective-permute-start.31 = (bf16[80,2048]{1,0:T(8,128)(2,1)S(1)}, bf16[80,2048]{1,0:T(8,128)(2,1)S(1)}, u32[]{:S(2)}, u32[]{:S(2)}) collective-permute-start(bf16[80,2048]{1,0:T(8,128)(2,1)S(1)} %get-tuple-element.145), channel_id=1, source_target_pairs={{0,6},{1,7},{2,4},{3,5},{4,2},{5,3},{6,0},{7,1},{8,14},{9,15},{10,... | collective-permute-start | bytes 983048 | tf_op jit(solution)/shard_map/ppermute | solution.py:24
  127.6 21.4 %collective-permute-start.38 = (bf16[128,2048]{1,0:T(8,128)(2,1)S(1)}, bf16[128,2048]{1,0:T(8,128)(2,1)S(1)}, u32[]{:S(2)}, u32[]{:S(2)}) collective-permute-start(bf16[128,2048]{1,0:T(8,128)(2,1)S(1)} %collective-permute-done.22.rows_ref), channel_id=1, source_target_pairs={{0,8},{8,16},{16,24},{24,0},{1,9},{9,17},{17,25},{25,1},{2,10},{10... | collective-permute-start | bytes 1572872 | tf_op jit(solution)/shard_map/ppermute | solution.py:29
  142.1 10.5 %collective-permute-start.32 = (bf16[80,2048]{1,0:T(8,128)(2,1)S(1)}, bf16[80,2048]{1,0:T(8,128)(2,1)S(1)}, u32[]{:S(2)}, u32[]{:S(2)}) collective-permute-start(bf16[80,2048]{1,0:T(8,128)(2,1)S(1)} %get-tuple-element.146), channel_id=1, source_target_pairs={{0,2},{1,3},{2,0},{3,1},{4,6},{5,7},{6,4},{7,5},{8,10},{9,11},{10,... | collective-permute-start | bytes 983048 | tf_op jit(solution)/shard_map/ppermute | solution.py:24
  143.1 15.0 %collective-permute-start.33 = (bf16[80,2048]{1,0:T(8,128)(2,1)S(1)}, bf16[80,2048]{1,0:T(8,128)(2,1)S(1)}, u32[]{:S(2)}, u32[]{:S(2)}) collective-permute-start(bf16[80,2048]{1,0:T(8,128)(2,1)S(1)} %get-tuple-element.147), channel_id=1, source_target_pairs={{0,4},{1,5},{2,6},{3,7},{4,0},{5,1},{6,2},{7,3},{8,12},{9,13},{10,... | collective-permute-start | bytes 983048 | tf_op jit(solution)/shard_map/ppermute | solution.py:24
  145.8 14.7 %collective-permute-start.45 = (bf16[128,2048]{1,0:T(8,128)(2,1)S(1)}, bf16[128,2048]{1,0:T(8,128)(2,1)S(1)}, u32[]{:S(2)}, u32[]{:S(2)}) collective-permute-start(bf16[128,2048]{1,0:T(8,128)(2,1)S(1)} %merge.4), channel_id=1, source_target_pairs={{0,8},{8,16},{16,24},{24,0},{1,9},{9,17},{17,25},{25,1},{2,10},{10... | collective-permute-start | bytes 1572872 | tf_op jit(solution)/shard_map/ppermute | solution.py:29
  147.4 13.1 %collective-permute-start.34 = (bf16[80,2048]{1,0:T(8,128)(2,1)S(1)}, bf16[80,2048]{1,0:T(8,128)(2,1)S(1)}, u32[]{:S(2)}, u32[]{:S(2)}) collective-permute-start(bf16[80,2048]{1,0:T(8,128)(2,1)S(1)} %get-tuple-element.148), channel_id=1, source_target_pairs={{0,6},{1,7},{2,4},{3,5},{4,2},{5,3},{6,0},{7,1},{8,14},{9,15},{10,... | collective-permute-start | bytes 983048 | tf_op jit(solution)/shard_map/ppermute | solution.py:24
  150.4 15.8 %collective-permute-start.39 = (bf16[80,2048]{1,0:T(8,128)(2,1)S(1)}, bf16[80,2048]{1,0:T(8,128)(2,1)S(1)}, u32[]{:S(2)}, u32[]{:S(2)}) collective-permute-start(bf16[80,2048]{1,0:T(8,128)(2,1)S(1)} %get-tuple-element.156), channel_id=1, source_target_pairs={{0,2},{1,3},{2,0},{3,1},{4,6},{5,7},{6,4},{7,5},{8,10},{9,11},{10,... | collective-permute-start | bytes 983048 | tf_op jit(solution)/shard_map/ppermute | solution.py:24
  152.6 18.0 %collective-permute-start.40 = (bf16[80,2048]{1,0:T(8,128)(2,1)S(1)}, bf16[80,2048]{1,0:T(8,128)(2,1)S(1)}, u32[]{:S(2)}, u32[]{:S(2)}) collective-permute-start(bf16[80,2048]{1,0:T(8,128)(2,1)S(1)} %get-tuple-element.157), channel_id=1, source_target_pairs={{0,4},{1,5},{2,6},{3,7},{4,0},{5,1},{6,2},{7,3},{8,12},{9,13},{10,... | collective-permute-start | bytes 983048 | tf_op jit(solution)/shard_map/ppermute | solution.py:24
  158.1 12.5 %collective-permute-start.41 = (bf16[80,2048]{1,0:T(8,128)(2,1)S(1)}, bf16[80,2048]{1,0:T(8,128)(2,1)S(1)}, u32[]{:S(2)}, u32[]{:S(2)}) collective-permute-start(bf16[80,2048]{1,0:T(8,128)(2,1)S(1)} %get-tuple-element.158), channel_id=1, source_target_pairs={{0,6},{1,7},{2,4},{3,5},{4,2},{5,3},{6,0},{7,1},{8,14},{9,15},{10,... | collective-permute-start | bytes 983048 | tf_op jit(solution)/shard_map/ppermute | solution.py:24
  162.3 30.4 %collective-permute-start.46 = (bf16[128,2048]{1,0:T(8,128)(2,1)S(1)}, bf16[128,2048]{1,0:T(8,128)(2,1)S(1)}, u32[]{:S(2)}, u32[]{:S(2)}) collective-permute-start(bf16[128,2048]{1,0:T(8,128)(2,1)S(1)} %merge.5), channel_id=1, source_target_pairs={{0,8},{8,16},{16,24},{24,0},{1,9},{9,17},{17,25},{25,1},{2,10},{10... | collective-permute-start | bytes 1572872 | tf_op jit(solution)/shard_map/ppermute | solution.py:29
  178.3 9.5 %collective-permute-start.42 = (bf16[80,2048]{1,0:T(8,128)(2,1)S(1)}, bf16[80,2048]{1,0:T(8,128)(2,1)S(1)}, u32[]{:S(2)}, u32[]{:S(2)}) collective-permute-start(bf16[80,2048]{1,0:T(8,128)(2,1)S(1)} %get-tuple-element.167), channel_id=1, source_target_pairs={{0,2},{1,3},{2,0},{3,1},{4,6},{5,7},{6,4},{7,5},{8,10},{9,11},{10,... | collective-permute-start | bytes 983048 | tf_op jit(solution)/shard_map/ppermute | solution.py:24
  179.9 12.8 %collective-permute-start.43 = (bf16[80,2048]{1,0:T(8,128)(2,1)S(1)}, bf16[80,2048]{1,0:T(8,128)(2,1)S(1)}, u32[]{:S(2)}, u32[]{:S(2)}) collective-permute-start(bf16[80,2048]{1,0:T(8,128)(2,1)S(1)} %get-tuple-element.168), channel_id=1, source_target_pairs={{0,4},{1,5},{2,6},{3,7},{4,0},{5,1},{6,2},{7,3},{8,12},{9,13},{10,... | collective-permute-start | bytes 983048 | tf_op jit(solution)/shard_map/ppermute | solution.py:24
  180.9 11.8 %collective-permute-start.44 = (bf16[80,2048]{1,0:T(8,128)(2,1)S(1)}, bf16[80,2048]{1,0:T(8,128)(2,1)S(1)}, u32[]{:S(2)}, u32[]{:S(2)}) collective-permute-start(bf16[80,2048]{1,0:T(8,128)(2,1)S(1)} %get-tuple-element.169), channel_id=1, source_target_pairs={{0,6},{1,7},{2,4},{3,5},{4,2},{5,3},{6,0},{7,1},{8,14},{9,15},{10,... | collective-permute-start | bytes 983048 | tf_op jit(solution)/shard_map/ppermute | solution.py:24
  194.5 12.4 %collective-permute-start.47 = (bf16[128,2048]{1,0:T(8,128)(2,1)S(1)}, bf16[128,2048]{1,0:T(8,128)(2,1)S(1)}, u32[]{:S(2)}, u32[]{:S(2)}) collective-permute-start(bf16[128,2048]{1,0:T(8,128)(2,1)S(1)} %merge.6), channel_id=1, source_target_pairs={{0,8},{8,16},{16,24},{24,0},{1,9},{9,17},{17,25},{25,1},{2,10},{10... | collective-permute-start | bytes 1572872 | tf_op jit(solution)/shard_map/ppermute | solution.py:29
  194.6 7.4 %collective-permute-start.35 = (bf16[80,2048]{1,0:T(8,128)(2,1)S(1)}, bf16[80,2048]{1,0:T(8,128)(2,1)S(1)}, u32[]{:S(2)}, u32[]{:S(2)}) collective-permute-start(bf16[80,2048]{1,0:T(8,128)(2,1)S(1)} %get-tuple-element.149), channel_id=1, source_target_pairs={{0,2},{1,3},{2,0},{3,1},{4,6},{5,7},{6,4},{7,5},{8,10},{9,11},{10,... | collective-permute-start | bytes 983048 | tf_op jit(solution)/shard_map/ppermute | solution.py:24
  195.4 11.5 %collective-permute-start.36 = (bf16[80,2048]{1,0:T(8,128)(2,1)S(1)}, bf16[80,2048]{1,0:T(8,128)(2,1)S(1)}, u32[]{:S(2)}, u32[]{:S(2)}) collective-permute-start(bf16[80,2048]{1,0:T(8,128)(2,1)S(1)} %get-tuple-element.150), channel_id=1, source_target_pairs={{0,4},{1,5},{2,6},{3,7},{4,0},{5,1},{6,2},{7,3},{8,12},{9,13},{10,... | collective-permute-start | bytes 983048 | tf_op jit(solution)/shard_map/ppermute | solution.py:24
  196.5 10.4 %collective-permute-start.37 = (bf16[80,2048]{1,0:T(8,128)(2,1)S(1)}, bf16[80,2048]{1,0:T(8,128)(2,1)S(1)}, u32[]{:S(2)}, u32[]{:S(2)}) collective-permute-start(bf16[80,2048]{1,0:T(8,128)(2,1)S(1)} %get-tuple-element.151), channel_id=1, source_target_pairs={{0,6},{1,7},{2,4},{3,5},{4,2},{5,3},{6,0},{7,1},{8,14},{9,15},{10,... | collective-permute-start | bytes 983048 | tf_op jit(solution)/shard_map/ppermute | solution.py:24
  (13 other events, 291.0 us)

commit v2 on v1

--- a/solution.py
+++ b/solution.py
@@ -711,7 +711,7 @@
         earlier,
     )
     if quick:
-        attended = after(attended, pieces[1], out_blocks)
+        attended = after(attended, pieces[1])
         pairs = jnp.split(attended, exp_count // 2)
         heads = [pairs[0]] + [swap(pairs[at], 2 * at) for at in range(1, exp_count // 2)]
         own, other = project(heads, out_blocks, local_rows)

time: 214 us -> 209 us (0.977)
  starting transfers between devices: 53.3 us -> 50.9 us
    ppermute x40, starting transfers between devices: 42.8 us -> 40.7 us  [swap(): return lax.ppermute(values, 'exp', [(d, d ^ bits) for d in range(count)])]
  transfers between devices with their start and end apart: 48 -> 48, of which waited for: 25 -> 24; matrix products, arithmetic and copies ran while one was open for 4% -> 4% of each run, Pallas kernels for 26% -> 26%
where the time goes in v2:
time: 209 us; the launch traced here: 205 us
  waiting for transfers between devices  81.3 us (39%)
  Pallas kernels  61.6 us (29%)
  starting transfers between devices  50.9 us (24%)
  other arithmetic  6.5 us (3%)
  local copies, waits for them, and re-layouts  3.01 us (1%)
    ppermute x40, waiting for transfers between devices, swap(): return lax.ppermute(values, 'exp', [(d, d ^ bits) for d in range(count)])  73.6 us
    ppermute x40, starting transfers between devices, swap(): return lax.ppermute(values, 'exp', [(d, d ^ bits) for d in range(count)])  40.7 us
    pallas_call x4, Pallas kernels, expert_rows(): pl.pallas_call(functools.partial(experts_kernel, part, wide), out_shape=[...  30.3 us
    pallas_call x1, Pallas kernels, attention(): pl.pallas_call(functools.partial(attention_kernel, layout, block_rows, ti...  16 us
    ppermute x8, starting transfers between devices, shift(): lax.ppermute(values, 'req', [(d, (d + steps) % count) for d in range(coun...  10.2 us
    pallas_call x4, Pallas kernels, merge(): pl.pallas_call(functools.partial(merge_kernel, count), out_shape=jax.Shap...  8.25 us
    ppermute x8, waiting for transfers between devices, shift(): lax.ppermute(values, 'req', [(d, (d + steps) % count) for d in range(coun...  7.65 us
    pallas_call x4, Pallas kernels, pick(): pl.pallas_call(pick_kernel, out_shape=[jax.ShapeDtypeStruct((capacity, wi...  5.56 us
  transfers between devices with their start and end apart: 48, of which 24 were waited for; matrix products, arithmetic and copies ran while one was open for 4% of the time, Pallas kernels for 26%

profile of v2, /device:TPU:0, one launch (start us, length us, event | category | flops | bytes accessed | tf_op | source)
XLA Modules:
  0.0 205.2 jit_solution(17162830414797232518)
XLA Ops:
  3.1 2.6 %collective-permute-start.4 = (bf16[128,2048]{1,0:T(8,128)(2,1)S(1)}, bf16[128,2048]{1,0:T(8,128)(2,1)S(1)}, u32[]{:S(2)}, u32[]{:S(2)}) collective-permute-start(bf16[128,2048]{1,0:T(8,128)(2,1)S(1)} %norm.1.refs_5_), channel_id=1, source_target_pairs={{0,4},{1,5},{2,6},{3,7},{4,0},{5,1},{6,2},{7,3},{8,12},{9,13},{10,... | collective-permute-start | bytes 1572872 | tf_op jit(solution)/shard_map/ppermute | solution.py:24
  5.7 1.5 collective-permute-start.2
  10.0 1.6 collective-permute-start
  11.7 3.9 %collective-permute-done = f32[16,128]{1,0:T(8,128)S(1)} collective-permute-done((f32[16,128]{1,0:T(8,128)S(1)}, f32[16,128]{1,0:T(8,128)S(1)}, u32[]{:S(2)}, u32[]{:S(2)}) %collective-permute-start) | collective-permute-done | bytes 8224 | tf_op jit(solution)/shard_map/ppermute | solution.py:29
  16.4 3.8 %collective-permute-done.1 = f32[2,16,128]{2,1,0:T(8,128)S(1)} collective-permute-done((f32[2,16,128]{2,1,0:T(8,128)S(1)}, f32[2,16,128]{2,1,0:T(8,128)S(1)}, u32[]{:S(2)}, u32[]{:S(2)}) %collective-permute-start.1) | collective-permute-done | bytes 16416 | tf_op jit(solution)/shard_map/ppermute | solution.py:29
  22.5 5.5 %collective-permute-done.7 = bf16[64,2048]{1,0:T(8,128)(2,1)S(1)} collective-permute-done((bf16[64,2048]{1,0:T(8,128)(2,1)S(1)}, bf16[64,2048]{1,0:T(8,128)(2,1)S(1)}, u32[]{:S(2)}, u32[]{:S(2)}) %collective-permute-start.7) | collective-permute-done | bytes 262176 | tf_op jit(solution)/shard_map/ppermute | solution.py:24
  28.6 1.9 collective-permute-done.9.refs_10_
  33.1 1.9 fusion
  35.4 1.7 collective-permute-start.16
  39.0 16.0 %attention.1 = (bf16[1024,128]{1,0:T(8,128)(2,1)S(1)}, bf16[2,1024,128]{2,1,0:T(8,128)(2,1)}) custom-call(s32[1]{0:T(128)} %bitcast.7.refs_0_, s32[1]{0:T(128)} %copy.20.refs_1_, s32[4]{0:T(128)S(1)} %copy-done.7, s32[4,32]{1,0:T(4,128)S(1)} %copy-done.6, s32[1,32]{1,0:T(1,128)S(1)} %copy-done.8, bf16[128,2048]{1,0:T(8,128)(2,1)S(1)} %norm.1.refs_5_, ...), custom_call_target="tpu_custom_call" | custom-call | flops 4294967296 | bytes 20971520 | tf_op jit(solution)/shard_map/attention/pallas_call | solution.py:445
  55.1 1.7 collective-permute-start.13
  58.6 3.8 %collective-permute-done.15.refs_6_ = bf16[128,2048]{1,0:T(8,128)(2,1)S(1)} collective-permute-done((bf16[128,2048]{1,0:T(8,128)(2,1)S(1)}, bf16[128,2048]{1,0:T(8,128)(2,1)S(1)}, u32[]{:S(2)}, u32[]{:S(2)}) %collective-permute-start.15) | collective-permute-done | bytes 524320 | tf_op jit(solution)/shard_map/ppermute | solution.py:24
  65.8 1.9 collective-permute-done.17.refs_1_
  68.9 1.4 pick.4
  70.3 1.6 collective-permute-start.18
  73.8 7.1 %collective-permute-done.18.refs_1_ = bf16[80,2048]{1,0:T(8,128)(2,1)S(1)} collective-permute-done((bf16[80,2048]{1,0:T(8,128)(2,1)S(1)}, bf16[80,2048]{1,0:T(8,128)(2,1)S(1)}, u32[]{:S(2)}, u32[]{:S(2)}) %collective-permute-start.18) | collective-permute-done | bytes 327712 | tf_op jit(solution)/shard_map/ppermute | solution.py:24
  80.9 7.1 %collective-permute-done.19.refs_2_ = bf16[80,2048]{1,0:T(8,128)(2,1)S(1)} collective-permute-done((bf16[80,2048]{1,0:T(8,128)(2,1)S(1)}, bf16[80,2048]{1,0:T(8,128)(2,1)S(1)}, u32[]{:S(2)}, u32[]{:S(2)}) %collective-permute-start.19) | collective-permute-done | bytes 327712 | tf_op jit(solution)/shard_map/ppermute | solution.py:24
  88.0 1.6 collective-permute-start.22
  89.6 1.4 pick.6
  91.6 1.4 collective-permute-start.27
  93.0 1.6 collective-permute-start.28
  94.6 7.5 %experts.4 = (bf16[80,2048]{1,0:T(8,128)(2,1)S(1)}, bf16[80,2048]{1,0:T(8,128)(2,1)S(1)}, bf16[80,2048]{1,0:T(8,128)(2,1)S(1)}, bf16[80,2048]{1,0:T(8,128)(2,1)S(1)}) custom-call(bf16[80,2048]{1,0:T(8,128)(2,1)S(1)} %get-tuple-element.104.refs_0_, bf16[80,2048]{1,0:T(8,128)(2,1)S(1)} %collective-permute-done.18.refs_1_, ...), custom_call_target="tpu_custom_call" | custom-call | flops 4026531840 | bytes 16777216 | tf_op jit(solution)/shard_map/experts/pallas_call | solution.py:116
  102.0 4.6 %collective-permute-done.27.refs_2_ = bf16[80,2048]{1,0:T(8,128)(2,1)S(1)} collective-permute-done((bf16[80,2048]{1,0:T(8,128)(2,1)S(1)}, bf16[80,2048]{1,0:T(8,128)(2,1)S(1)}, u32[]{:S(2)}, u32[]{:S(2)}) %collective-permute-start.27) | collective-permute-done | bytes 327712 | tf_op jit(solution)/shard_map/ppermute | solution.py:24
  106.7 1.4 pick.5
  109.9 1.7 collective-permute-start.25
  111.6 7.5 %experts.5 = (bf16[80,2048]{1,0:T(8,128)(2,1)S(1)}, bf16[80,2048]{1,0:T(8,128)(2,1)S(1)}, bf16[80,2048]{1,0:T(8,128)(2,1)S(1)}, bf16[80,2048]{1,0:T(8,128)(2,1)S(1)}) custom-call(bf16[80,2048]{1,0:T(8,128)(2,1)S(1)} %get-tuple-element.127.refs_0_, bf16[80,2048]{1,0:T(8,128)(2,1)S(1)} %collective-permute-done.26.refs_1_, ...), custom_call_target="tpu_custom_call" | custom-call | flops 4026531840 | bytes 16777216 | tf_op jit(solution)/shard_map/experts/pallas_call | solution.py:116
  120.9 1.7 collective-permute-start.31
  122.7 1.6 collective-permute-start.38
  124.2 2.2 %collective-permute-done.25.refs_3_ = bf16[80,2048]{1,0:T(8,128)(2,1)S(1)} collective-permute-done((bf16[80,2048]{1,0:T(8,128)(2,1)S(1)}, bf16[80,2048]{1,0:T(8,128)(2,1)S(1)}, u32[]{:S(2)}, u32[]{:S(2)}) %collective-permute-start.25) | collective-permute-done | bytes 327712 | tf_op jit(solution)/shard_map/ppermute | solution.py:24
  126.4 7.8 %experts.6 = (bf16[80,2048]{1,0:T(8,128)(2,1)S(1)}, bf16[80,2048]{1,0:T(8,128)(2,1)S(1)}, bf16[80,2048]{1,0:T(8,128)(2,1)S(1)}, bf16[80,2048]{1,0:T(8,128)(2,1)S(1)}) custom-call(bf16[80,2048]{1,0:T(8,128)(2,1)S(1)} %get-tuple-element.135.refs_0_, bf16[80,2048]{1,0:T(8,128)(2,1)S(1)} %collective-permute-done.23.refs_1_, ...), custom_call_target="tpu_custom_call" | custom-call | flops 4026531840 | bytes 16777216 | tf_op jit(solution)/shard_map/experts/pallas_call | solution.py:116
  134.3 3.0 %collective-permute-done.30.refs_2_ = bf16[80,2048]{1,0:T(8,128)(2,1)S(1)} collective-permute-done((bf16[80,2048]{1,0:T(8,128)(2,1)S(1)}, bf16[80,2048]{1,0:T(8,128)(2,1)S(1)}, u32[]{:S(2)}, u32[]{:S(2)}) %collective-permute-start.30) | collective-permute-done | bytes 327712 | tf_op jit(solution)/shard_map/ppermute | solution.py:24
  139.5 1.8 merge.4
  141.3 1.7 collective-permute-start.45
  144.3 1.4 pick.7
  148.4 6.1 %collective-permute-done.33.refs_2_ = bf16[80,2048]{1,0:T(8,128)(2,1)S(1)} collective-permute-done((bf16[80,2048]{1,0:T(8,128)(2,1)S(1)}, bf16[80,2048]{1,0:T(8,128)(2,1)S(1)}, u32[]{:S(2)}, u32[]{:S(2)}) %collective-permute-start.33) | collective-permute-done | bytes 327712 | tf_op jit(solution)/shard_map/ppermute | solution.py:24
  154.8 1.9 merge.5
  156.7 2.1 %collective-permute-start.46 = (bf16[128,2048]{1,0:T(8,128)(2,1)S(1)}, bf16[128,2048]{1,0:T(8,128)(2,1)S(1)}, u32[]{:S(2)}, u32[]{:S(2)}) collective-permute-start(bf16[128,2048]{1,0:T(8,128)(2,1)S(1)} %merge.5), channel_id=1, source_target_pairs={{0,8},{8,16},{16,24},{24,0},{1,9},{9,17},{17,25},{25,1},{2,10},{10... | collective-permute-start | bytes 1572872 | tf_op jit(solution)/shard_map/ppermute | solution.py:29
  158.8 2.8 %collective-permute-done.39.refs_1_ = bf16[80,2048]{1,0:T(8,128)(2,1)S(1)} collective-permute-done((bf16[80,2048]{1,0:T(8,128)(2,1)S(1)}, bf16[80,2048]{1,0:T(8,128)(2,1)S(1)}, u32[]{:S(2)}, u32[]{:S(2)}) %collective-permute-start.39) | collective-permute-done | bytes 327712 | tf_op jit(solution)/shard_map/ppermute | solution.py:24
  161.5 4.8 %collective-permute-done.40.refs_2_ = bf16[80,2048]{1,0:T(8,128)(2,1)S(1)} collective-permute-done((bf16[80,2048]{1,0:T(8,128)(2,1)S(1)}, bf16[80,2048]{1,0:T(8,128)(2,1)S(1)}, u32[]{:S(2)}, u32[]{:S(2)}) %collective-permute-start.40) | collective-permute-done | bytes 327712 | tf_op jit(solution)/shard_map/ppermute | solution.py:24
  166.4 7.6 %experts.7 = (bf16[80,2048]{1,0:T(8,128)(2,1)S(1)}, bf16[80,2048]{1,0:T(8,128)(2,1)S(1)}, bf16[80,2048]{1,0:T(8,128)(2,1)S(1)}, bf16[80,2048]{1,0:T(8,128)(2,1)S(1)}) custom-call(bf16[80,2048]{1,0:T(8,128)(2,1)S(1)} %get-tuple-element.159.refs_0_, bf16[80,2048]{1,0:T(8,128)(2,1)S(1)} %collective-permute-done.39.refs_1_, ...), custom_call_target="tpu_custom_call" | custom-call | flops 4026531840 | bytes 16777216 | tf_op jit(solution)/shard_map/experts/pallas_call | solution.py:116
  175.5 2.0 collective-permute-start.44
  177.5 6.1 %collective-permute-done.42.refs_1_ = bf16[80,2048]{1,0:T(8,128)(2,1)S(1)} collective-permute-done((bf16[80,2048]{1,0:T(8,128)(2,1)S(1)}, bf16[80,2048]{1,0:T(8,128)(2,1)S(1)}, u32[]{:S(2)}, u32[]{:S(2)}) %collective-permute-start.42) | collective-permute-done | bytes 327712 | tf_op jit(solution)/shard_map/ppermute | solution.py:24
  184.1 3.5 %collective-permute-done.44.refs_3_ = bf16[80,2048]{1,0:T(8,128)(2,1)S(1)} collective-permute-done((bf16[80,2048]{1,0:T(8,128)(2,1)S(1)}, bf16[80,2048]{1,0:T(8,128)(2,1)S(1)}, u32[]{:S(2)}, u32[]{:S(2)}) %collective-permute-start.44) | collective-permute-done | bytes 327712 | tf_op jit(solution)/shard_map/ppermute | solution.py:24
  187.6 1.8 merge.6
  189.5 1.4 collective-permute-start.35
  193.1 4.8 %collective-permute-done.35.refs_1_ = bf16[80,2048]{1,0:T(8,128)(2,1)S(1)} collective-permute-done((bf16[80,2048]{1,0:T(8,128)(2,1)S(1)}, bf16[80,2048]{1,0:T(8,128)(2,1)S(1)}, u32[]{:S(2)}, u32[]{:S(2)}) %collective-permute-start.35) | collective-permute-done | bytes 327712 | tf_op jit(solution)/shard_map/ppermute | solution.py:24
  197.9 4.4 %collective-permute-done.36.refs_2_ = bf16[80,2048]{1,0:T(8,128)(2,1)S(1)} collective-permute-done((bf16[80,2048]{1,0:T(8,128)(2,1)S(1)}, bf16[80,2048]{1,0:T(8,128)(2,1)S(1)}, u32[]{:S(2)}, u32[]{:S(2)}) %collective-permute-start.36) | collective-permute-done | bytes 327712 | tf_op jit(solution)/shard_map/ppermute | solution.py:24
  202.3 2.7 %merge.7 = bf16[128,2048]{1,0:T(8,128)(2,1)} custom-call(f32[8,128]{1,0:T(8,128)S(1)} %get-tuple-element.183.gate_ref, s32[8,128]{1,0:T(8,128)S(1)} %get-tuple-element.179.place_ref, bf16[80,2048]{1,0:T(8,128)(2,1)S(1)} %get-tuple-element.108.refs_0_, bf16[80,2048]{1,0:T(8,128)(2,1)S(1)} %collective-permute-done.35.refs_1_, ...), custom_call_target="tpu_custom_call" | custom-call | flops 167772160 | bytes 1048576 | tf_op jit(solution)/shard_map/merge/pallas_call | solution.py:209
  (114 shorter events, 36.7 us)
Async XLA Ops:
  0.6 20.9 %collective-permute-start.6 = (bf16[2048,1024]{1,0:T(8,128)(2,1)}, bf16[2048,1024]{1,0:T(8,128)(2,1)}, u32[]{:S(2)}, u32[]{:S(2)}) collective-permute-start(bf16[2048,1024]{1,0:T(8,128)(2,1)} %bitcast.30), channel_id=1, source_target_pairs={{0,1},{1,0},{2,3},{3,2},{4,5},{5,4},{6,7},{7,6},{8,9},{9,8},{10,11... | collective-permute-start | bytes 12582920 | tf_op jit(solution)/shard_map/ppermute | solution.py:24
  3.1 18.4 %collective-permute-start.4 = (bf16[128,2048]{1,0:T(8,128)(2,1)S(1)}, bf16[128,2048]{1,0:T(8,128)(2,1)S(1)}, u32[]{:S(2)}, u32[]{:S(2)}) collective-permute-start(bf16[128,2048]{1,0:T(8,128)(2,1)S(1)} %norm.1.refs_5_), channel_id=1, source_target_pairs={{0,4},{1,5},{2,6},{3,7},{4,0},{5,1},{6,2},{7,3},{8,12},{9,13},{10,... | collective-permute-start | bytes 1572872 | tf_op jit(solution)/shard_map/ppermute | solution.py:24
  5.7 15.8 %collective-permute-start.2 = (bf16[128,2048]{1,0:T(8,128)(2,1)S(1)}, bf16[128,2048]{1,0:T(8,128)(2,1)S(1)}, u32[]{:S(2)}, u32[]{:S(2)}) collective-permute-start(bf16[128,2048]{1,0:T(8,128)(2,1)S(1)} %norm.1.refs_5_), channel_id=1, source_target_pairs={{0,2},{1,3},{2,0},{3,1},{4,6},{5,7},{6,4},{7,5},{8,10},{9,11},{10,... | collective-permute-start | bytes 1572872 | tf_op jit(solution)/shard_map/ppermute | solution.py:24
  10.0 5.5 %collective-permute-start = (f32[16,128]{1,0:T(8,128)S(1)}, f32[16,128]{1,0:T(8,128)S(1)}, u32[]{:S(2)}, u32[]{:S(2)}) collective-permute-start(f32[16,128]{1,0:T(8,128)S(1)} %select_reduce_fusion.1), channel_id=1, source_target_pairs={{0,8},{8,16},{16,24},{24,0},{1,9},{9,17},{17,25},{25,1},{2,10},{10... | collective-permute-start | bytes 24584 | tf_op jit(solution)/shard_map/ppermute | solution.py:29
  15.5 4.6 %collective-permute-start.1 = (f32[2,16,128]{2,1,0:T(8,128)S(1)}, f32[2,16,128]{2,1,0:T(8,128)S(1)}, u32[]{:S(2)}, u32[]{:S(2)}) collective-permute-start(f32[2,16,128]{2,1,0:T(8,128)S(1)} %pad_maximum_fusion.3), channel_id=1, source_target_pairs={{0,16},{8,24},{16,0},{24,8},{1,17},{9,25},{17,1},{25,9},{2,18},{10... | collective-permute-start | bytes 49160 | tf_op jit(solution)/shard_map/ppermute | solution.py:29
  21.6 6.4 %collective-permute-start.7 = (bf16[64,2048]{1,0:T(8,128)(2,1)S(1)}, bf16[64,2048]{1,0:T(8,128)(2,1)S(1)}, u32[]{:S(2)}, u32[]{:S(2)}) collective-permute-start(bf16[64,2048]{1,0:T(8,128)(2,1)S(1)} %slice.49), channel_id=1, source_target_pairs={{0,4},{1,5},{2,6},{3,7},{4,0},{5,1},{6,2},{7,3},{8,12},{9,13},{10,... | collective-permute-start | bytes 786440 | tf_op jit(solution)/shard_map/ppermute | solution.py:24
  22.2 6.4 %collective-permute-start.8 = (bf16[64,2048]{1,0:T(8,128)(2,1)S(1)}, bf16[64,2048]{1,0:T(8,128)(2,1)S(1)}, u32[]{:S(2)}, u32[]{:S(2)}) collective-permute-start(bf16[64,2048]{1,0:T(8,128)(2,1)S(1)} %slice.50), channel_id=1, source_target_pairs={{0,2},{1,3},{2,0},{3,1},{4,6},{5,7},{6,4},{7,5},{8,10},{9,11},{10,... | collective-permute-start | bytes 786440 | tf_op jit(solution)/shard_map/ppermute | solution.py:24
  28.6 2.0 collective-permute-start.9
  30.5 24.5 %collective-permute-start.10 = (bf16[512,2048]{1,0:T(8,128)(2,1)}, bf16[512,2048]{1,0:T(8,128)(2,1)S(1)}, u32[]{:S(2)}, u32[]{:S(2)}) collective-permute-start(bf16[512,2048]{1,0:T(8,128)(2,1)} %bitcast.35), channel_id=1, source_target_pairs={{0,1},{1,0},{2,3},{3,2},{4,5},{5,4},{6,7},{7,6},{8,9},{9,8},{10,11... | collective-permute-start | bytes 6291464 | tf_op jit(solution)/shard_map/ppermute | solution.py:24
  31.8 7.2 %collective-permute-start.5 = (bf16[256,2048]{1,0:T(8,128)(2,1)S(1)}, bf16[256,2048]{1,0:T(8,128)(2,1)S(1)}, u32[]{:S(2)}, u32[]{:S(2)}) collective-permute-start(bf16[256,2048]{1,0:T(8,128)(2,1)S(1)} %constant_dynamic-update-slice_fusion.refs_7_), channel_id=1, source_target_pairs={{0,1},{1,0},{2,3},{3,2},{4,5},{5,4},{6,7},{7,6},{8,9},{9,8},{10,11... | collective-permute-start | bytes 3145736 | tf_op jit(solution)/shard_map/ppermute | solution.py:24
  33.0 4.8 %collective-permute-start.3 = (bf16[128,2048]{1,0:T(8,128)(2,1)S(1)}, bf16[128,2048]{1,0:T(8,128)(2,1)S(1)}, u32[]{:S(2)}, u32[]{:S(2)}) collective-permute-start(bf16[128,2048]{1,0:T(8,128)(2,1)S(1)} %norm.1.refs_5_), channel_id=1, source_target_pairs={{0,1},{1,0},{2,3},{3,2},{4,5},{5,4},{6,7},{7,6},{8,9},{9,8},{10,11... | collective-permute-start | bytes 1572872 | tf_op jit(solution)/shard_map/ppermute | solution.py:24
  35.4 22.0 %collective-permute-start.16 = (bf16[128,2048]{1,0:T(8,128)(2,1)S(1)}, bf16[128,2048]{1,0:T(8,128)(2,1)S(1)}, u32[]{:S(2)}, u32[]{:S(2)}) collective-permute-start(bf16[128,2048]{1,0:T(8,128)(2,1)S(1)} %copy-done.3), channel_id=1, source_target_pairs={{0,6},{1,7},{2,4},{3,5},{4,2},{5,3},{6,0},{7,1},{8,14},{9,15},{10,... | collective-permute-start | bytes 1572872 | tf_op jit(solution)/shard_map/ppermute | solution.py:24
  37.1 25.4 %collective-permute-start.15 = (bf16[128,2048]{1,0:T(8,128)(2,1)S(1)}, bf16[128,2048]{1,0:T(8,128)(2,1)S(1)}, u32[]{:S(2)}, u32[]{:S(2)}) collective-permute-start(bf16[128,2048]{1,0:T(8,128)(2,1)S(1)} %copy-done.3), channel_id=1, source_target_pairs={{0,4},{1,5},{2,6},{3,7},{4,0},{5,1},{6,2},{7,3},{8,12},{9,13},{10,... | collective-permute-start | bytes 1572872 | tf_op jit(solution)/shard_map/ppermute | solution.py:24
  37.7 24.7 %collective-permute-start.14 = (bf16[128,2048]{1,0:T(8,128)(2,1)S(1)}, bf16[128,2048]{1,0:T(8,128)(2,1)S(1)}, u32[]{:S(2)}, u32[]{:S(2)}) collective-permute-start(bf16[128,2048]{1,0:T(8,128)(2,1)S(1)} %copy-done.3), channel_id=1, source_target_pairs={{0,2},{1,3},{2,0},{3,1},{4,6},{5,7},{6,4},{7,5},{8,10},{9,11},{10,... | collective-permute-start | bytes 1572872 | tf_op jit(solution)/shard_map/ppermute | solution.py:24
  55.1 8.8 %collective-permute-start.13 = (bf16[256,128]{1,0:T(8,128)(2,1)S(1)}, bf16[256,128]{1,0:T(8,128)(2,1)S(1)}, u32[]{:S(2)}, u32[]{:S(2)}) collective-permute-start(bf16[256,128]{1,0:T(8,128)(2,1)S(1)} %get-tuple-element.172), channel_id=1, source_target_pairs={{0,6},{1,7},{2,4},{3,5},{4,2},{5,3},{6,0},{7,1},{8,14},{9,15},{10,... | collective-permute-start | bytes 196616 | tf_op jit(solution)/shard_map/ppermute | solution.py:24
  56.7 7.9 %collective-permute-start.12 = (bf16[256,128]{1,0:T(8,128)(2,1)S(1)}, bf16[256,128]{1,0:T(8,128)(2,1)S(1)}, u32[]{:S(2)}, u32[]{:S(2)}) collective-permute-start(bf16[256,128]{1,0:T(8,128)(2,1)S(1)} %get-tuple-element.173), channel_id=1, source_target_pairs={{0,4},{1,5},{2,6},{3,7},{4,0},{5,1},{6,2},{7,3},{8,12},{9,13},{10,... | collective-permute-start | bytes 196616 | tf_op jit(solution)/shard_map/ppermute | solution.py:24
  57.4 7.4 %collective-permute-start.11 = (bf16[256,128]{1,0:T(8,128)(2,1)S(1)}, bf16[256,128]{1,0:T(8,128)(2,1)S(1)}, u32[]{:S(2)}, u32[]{:S(2)}) collective-permute-start(bf16[256,128]{1,0:T(8,128)(2,1)S(1)} %get-tuple-element.174), channel_id=1, source_target_pairs={{0,2},{1,3},{2,0},{3,1},{4,6},{5,7},{6,4},{7,5},{8,10},{9,11},{10,... | collective-permute-start | bytes 196616 | tf_op jit(solution)/shard_map/ppermute | solution.py:24
  65.7 2.0 collective-permute-start.17
  68.0 20.0 %collective-permute-start.21 = (bf16[128,2048]{1,0:T(8,128)(2,1)S(1)}, bf16[128,2048]{1,0:T(8,128)(2,1)S(1)}, u32[]{:S(2)}, u32[]{:S(2)}) collective-permute-start(bf16[128,2048]{1,0:T(8,128)(2,1)S(1)} %get-tuple-element.96.rows_ref), channel_id=1, source_target_pairs={{0,8},{8,16},{16,24},{24,0},{1,9},{9,17},{17,25},{25,1},{2,10},{10... | collective-permute-start | bytes 1572872 | tf_op jit(solution)/shard_map/ppermute | solution.py:29
  70.3 10.7 %collective-permute-start.18 = (bf16[80,2048]{1,0:T(8,128)(2,1)S(1)}, bf16[80,2048]{1,0:T(8,128)(2,1)S(1)}, u32[]{:S(2)}, u32[]{:S(2)}) collective-permute-start(bf16[80,2048]{1,0:T(8,128)(2,1)S(1)} %get-tuple-element.101), channel_id=1, source_target_pairs={{0,2},{1,3},{2,0},{3,1},{4,6},{5,7},{6,4},{7,5},{8,10},{9,11},{10,... | collective-permute-start | bytes 983048 | tf_op jit(solution)/shard_map/ppermute | solution.py:24
  71.8 16.2 %collective-permute-start.19 = (bf16[80,2048]{1,0:T(8,128)(2,1)S(1)}, bf16[80,2048]{1,0:T(8,128)(2,1)S(1)}, u32[]{:S(2)}, u32[]{:S(2)}) collective-permute-start(bf16[80,2048]{1,0:T(8,128)(2,1)S(1)} %get-tuple-element.102), channel_id=1, source_target_pairs={{0,4},{1,5},{2,6},{3,7},{4,0},{5,1},{6,2},{7,3},{8,12},{9,13},{10,... | collective-permute-start | bytes 983048 | tf_op jit(solution)/shard_map/ppermute | solution.py:24
  72.6 15.4 %collective-permute-start.20 = (bf16[80,2048]{1,0:T(8,128)(2,1)S(1)}, bf16[80,2048]{1,0:T(8,128)(2,1)S(1)}, u32[]{:S(2)}, u32[]{:S(2)}) collective-permute-start(bf16[80,2048]{1,0:T(8,128)(2,1)S(1)} %get-tuple-element.103), channel_id=1, source_target_pairs={{0,6},{1,7},{2,4},{3,5},{4,2},{5,3},{6,0},{7,1},{8,14},{9,15},{10,... | collective-permute-start | bytes 983048 | tf_op jit(solution)/shard_map/ppermute | solution.py:24
  88.0 18.6 %collective-permute-start.22 = (bf16[128,2048]{1,0:T(8,128)(2,1)S(1)}, bf16[128,2048]{1,0:T(8,128)(2,1)S(1)}, u32[]{:S(2)}, u32[]{:S(2)}) collective-permute-start(bf16[128,2048]{1,0:T(8,128)(2,1)S(1)} %collective-permute-done.21.rows_ref), channel_id=1, source_target_pairs={{0,8},{8,16},{16,24},{24,0},{1,9},{9,17},{17,25},{25,1},{2,10},{10... | collective-permute-start | bytes 1572872 | tf_op jit(solution)/shard_map/ppermute | solution.py:29
  91.0 11.0 %collective-permute-start.26 = (bf16[80,2048]{1,0:T(8,128)(2,1)S(1)}, bf16[80,2048]{1,0:T(8,128)(2,1)S(1)}, u32[]{:S(2)}, u32[]{:S(2)}) collective-permute-start(bf16[80,2048]{1,0:T(8,128)(2,1)S(1)} %get-tuple-element.124), channel_id=1, source_target_pairs={{0,2},{1,3},{2,0},{3,1},{4,6},{5,7},{6,4},{7,5},{8,10},{9,11},{10,... | collective-permute-start | bytes 983048 | tf_op jit(solution)/shard_map/ppermute | solution.py:24
  91.6 15.1 %collective-permute-start.27 = (bf16[80,2048]{1,0:T(8,128)(2,1)S(1)}, bf16[80,2048]{1,0:T(8,128)(2,1)S(1)}, u32[]{:S(2)}, u32[]{:S(2)}) collective-permute-start(bf16[80,2048]{1,0:T(8,128)(2,1)S(1)} %get-tuple-element.125), channel_id=1, source_target_pairs={{0,4},{1,5},{2,6},{3,7},{4,0},{5,1},{6,2},{7,3},{8,12},{9,13},{10,... | collective-permute-start | bytes 983048 | tf_op jit(solution)/shard_map/ppermute | solution.py:24
  93.0 13.7 %collective-permute-start.28 = (bf16[80,2048]{1,0:T(8,128)(2,1)S(1)}, bf16[80,2048]{1,0:T(8,128)(2,1)S(1)}, u32[]{:S(2)}, u32[]{:S(2)}) collective-permute-start(bf16[80,2048]{1,0:T(8,128)(2,1)S(1)} %get-tuple-element.126), channel_id=1, source_target_pairs={{0,6},{1,7},{2,4},{3,5},{4,2},{5,3},{6,0},{7,1},{8,14},{9,15},{10,... | collective-permute-start | bytes 983048 | tf_op jit(solution)/shard_map/ppermute | solution.py:24
  108.1 12.9 %collective-permute-start.23 = (bf16[80,2048]{1,0:T(8,128)(2,1)S(1)}, bf16[80,2048]{1,0:T(8,128)(2,1)S(1)}, u32[]{:S(2)}, u32[]{:S(2)}) collective-permute-start(bf16[80,2048]{1,0:T(8,128)(2,1)S(1)} %get-tuple-element.117), channel_id=1, source_target_pairs={{0,2},{1,3},{2,0},{3,1},{4,6},{5,7},{6,4},{7,5},{8,10},{9,11},{10,... | collective-permute-start | bytes 983048 | tf_op jit(solution)/shard_map/ppermute | solution.py:24
  109.3 13.4 %collective-permute-start.24 = (bf16[80,2048]{1,0:T(8,128)(2,1)S(1)}, bf16[80,2048]{1,0:T(8,128)(2,1)S(1)}, u32[]{:S(2)}, u32[]{:S(2)}) collective-permute-start(bf16[80,2048]{1,0:T(8,128)(2,1)S(1)} %get-tuple-element.118), channel_id=1, source_target_pairs={{0,4},{1,5},{2,6},{3,7},{4,0},{5,1},{6,2},{7,3},{8,12},{9,13},{10,... | collective-permute-start | bytes 983048 | tf_op jit(solution)/shard_map/ppermute | solution.py:24
  109.9 16.5 %collective-permute-start.25 = (bf16[80,2048]{1,0:T(8,128)(2,1)S(1)}, bf16[80,2048]{1,0:T(8,128)(2,1)S(1)}, u32[]{:S(2)}, u32[]{:S(2)}) collective-permute-start(bf16[80,2048]{1,0:T(8,128)(2,1)S(1)} %get-tuple-element.119), channel_id=1, source_target_pairs={{0,6},{1,7},{2,4},{3,5},{4,2},{5,3},{6,0},{7,1},{8,14},{9,15},{10,... | collective-permute-start | bytes 983048 | tf_op jit(solution)/shard_map/ppermute | solution.py:24
  119.1 15.2 %collective-permute-start.29 = (bf16[80,2048]{1,0:T(8,128)(2,1)S(1)}, bf16[80,2048]{1,0:T(8,128)(2,1)S(1)}, u32[]{:S(2)}, u32[]{:S(2)}) collective-permute-start(bf16[80,2048]{1,0:T(8,128)(2,1)S(1)} %get-tuple-element.143), channel_id=1, source_target_pairs={{0,2},{1,3},{2,0},{3,1},{4,6},{5,7},{6,4},{7,5},{8,10},{9,11},{10,... | collective-permute-start | bytes 983048 | tf_op jit(solution)/shard_map/ppermute | solution.py:24
  120.3 17.0 %collective-permute-start.30 = (bf16[80,2048]{1,0:T(8,128)(2,1)S(1)}, bf16[80,2048]{1,0:T(8,128)(2,1)S(1)}, u32[]{:S(2)}, u32[]{:S(2)}) collective-permute-start(bf16[80,2048]{1,0:T(8,128)(2,1)S(1)} %get-tuple-element.144), channel_id=1, source_target_pairs={{0,4},{1,5},{2,6},{3,7},{4,0},{5,1},{6,2},{7,3},{8,12},{9,13},{10,... | collective-permute-start | bytes 983048 | tf_op jit(solution)/shard_map/ppermute | solution.py:24
  120.9 16.3 %collective-permute-start.31 = (bf16[80,2048]{1,0:T(8,128)(2,1)S(1)}, bf16[80,2048]{1,0:T(8,128)(2,1)S(1)}, u32[]{:S(2)}, u32[]{:S(2)}) collective-permute-start(bf16[80,2048]{1,0:T(8,128)(2,1)S(1)} %get-tuple-element.145), channel_id=1, source_target_pairs={{0,6},{1,7},{2,4},{3,5},{4,2},{5,3},{6,0},{7,1},{8,14},{9,15},{10,... | collective-permute-start | bytes 983048 | tf_op jit(solution)/shard_map/ppermute | solution.py:24
  122.7 21.6 %collective-permute-start.38 = (bf16[128,2048]{1,0:T(8,128)(2,1)S(1)}, bf16[128,2048]{1,0:T(8,128)(2,1)S(1)}, u32[]{:S(2)}, u32[]{:S(2)}) collective-permute-start(bf16[128,2048]{1,0:T(8,128)(2,1)S(1)} %collective-permute-done.22.rows_ref), channel_id=1, source_target_pairs={{0,8},{8,16},{16,24},{24,0},{1,9},{9,17},{17,25},{25,1},{2,10},{10... | collective-permute-start | bytes 1572872 | tf_op jit(solution)/shard_map/ppermute | solution.py:29
  137.3 10.2 %collective-permute-start.32 = (bf16[80,2048]{1,0:T(8,128)(2,1)S(1)}, bf16[80,2048]{1,0:T(8,128)(2,1)S(1)}, u32[]{:S(2)}, u32[]{:S(2)}) collective-permute-start(bf16[80,2048]{1,0:T(8,128)(2,1)S(1)} %get-tuple-element.146), channel_id=1, source_target_pairs={{0,2},{1,3},{2,0},{3,1},{4,6},{5,7},{6,4},{7,5},{8,10},{9,11},{10,... | collective-permute-start | bytes 983048 | tf_op jit(solution)/shard_map/ppermute | solution.py:24
  138.4 16.1 %collective-permute-start.33 = (bf16[80,2048]{1,0:T(8,128)(2,1)S(1)}, bf16[80,2048]{1,0:T(8,128)(2,1)S(1)}, u32[]{:S(2)}, u32[]{:S(2)}) collective-permute-start(bf16[80,2048]{1,0:T(8,128)(2,1)S(1)} %get-tuple-element.147), channel_id=1, source_target_pairs={{0,4},{1,5},{2,6},{3,7},{4,0},{5,1},{6,2},{7,3},{8,12},{9,13},{10,... | collective-permute-start | bytes 983048 | tf_op jit(solution)/shard_map/ppermute | solution.py:24
  141.3 13.5 %collective-permute-start.45 = (bf16[128,2048]{1,0:T(8,128)(2,1)S(1)}, bf16[128,2048]{1,0:T(8,128)(2,1)S(1)}, u32[]{:S(2)}, u32[]{:S(2)}) collective-permute-start(bf16[128,2048]{1,0:T(8,128)(2,1)S(1)} %merge.4), channel_id=1, source_target_pairs={{0,8},{8,16},{16,24},{24,0},{1,9},{9,17},{17,25},{25,1},{2,10},{10... | collective-permute-start | bytes 1572872 | tf_op jit(solution)/shard_map/ppermute | solution.py:29
  142.9 11.9 %collective-permute-start.34 = (bf16[80,2048]{1,0:T(8,128)(2,1)S(1)}, bf16[80,2048]{1,0:T(8,128)(2,1)S(1)}, u32[]{:S(2)}, u32[]{:S(2)}) collective-permute-start(bf16[80,2048]{1,0:T(8,128)(2,1)S(1)} %get-tuple-element.148), channel_id=1, source_target_pairs={{0,6},{1,7},{2,4},{3,5},{4,2},{5,3},{6,0},{7,1},{8,14},{9,15},{10,... | collective-permute-start | bytes 983048 | tf_op jit(solution)/shard_map/ppermute | solution.py:24
  145.7 15.8 %collective-permute-start.39 = (bf16[80,2048]{1,0:T(8,128)(2,1)S(1)}, bf16[80,2048]{1,0:T(8,128)(2,1)S(1)}, u32[]{:S(2)}, u32[]{:S(2)}) collective-permute-start(bf16[80,2048]{1,0:T(8,128)(2,1)S(1)} %get-tuple-element.156), channel_id=1, source_target_pairs={{0,2},{1,3},{2,0},{3,1},{4,6},{5,7},{6,4},{7,5},{8,10},{9,11},{10,... | collective-permute-start | bytes 983048 | tf_op jit(solution)/shard_map/ppermute | solution.py:24
  147.5 18.9 %collective-permute-start.40 = (bf16[80,2048]{1,0:T(8,128)(2,1)S(1)}, bf16[80,2048]{1,0:T(8,128)(2,1)S(1)}, u32[]{:S(2)}, u32[]{:S(2)}) collective-permute-start(bf16[80,2048]{1,0:T(8,128)(2,1)S(1)} %get-tuple-element.157), channel_id=1, source_target_pairs={{0,4},{1,5},{2,6},{3,7},{4,0},{5,1},{6,2},{7,3},{8,12},{9,13},{10,... | collective-permute-start | bytes 983048 | tf_op jit(solution)/shard_map/ppermute | solution.py:24
  154.4 11.9 %collective-permute-start.41 = (bf16[80,2048]{1,0:T(8,128)(2,1)S(1)}, bf16[80,2048]{1,0:T(8,128)(2,1)S(1)}, u32[]{:S(2)}, u32[]{:S(2)}) collective-permute-start(bf16[80,2048]{1,0:T(8,128)(2,1)S(1)} %get-tuple-element.158), channel_id=1, source_target_pairs={{0,6},{1,7},{2,4},{3,5},{4,2},{5,3},{6,0},{7,1},{8,14},{9,15},{10,... | collective-permute-start | bytes 983048 | tf_op jit(solution)/shard_map/ppermute | solution.py:24
  156.7 30.9 %collective-permute-start.46 = (bf16[128,2048]{1,0:T(8,128)(2,1)S(1)}, bf16[128,2048]{1,0:T(8,128)(2,1)S(1)}, u32[]{:S(2)}, u32[]{:S(2)}) collective-permute-start(bf16[128,2048]{1,0:T(8,128)(2,1)S(1)} %merge.5), channel_id=1, source_target_pairs={{0,8},{8,16},{16,24},{24,0},{1,9},{9,17},{17,25},{25,1},{2,10},{10... | collective-permute-start | bytes 1572872 | tf_op jit(solution)/shard_map/ppermute | solution.py:29
  174.0 9.6 %collective-permute-start.42 = (bf16[80,2048]{1,0:T(8,128)(2,1)S(1)}, bf16[80,2048]{1,0:T(8,128)(2,1)S(1)}, u32[]{:S(2)}, u32[]{:S(2)}) collective-permute-start(bf16[80,2048]{1,0:T(8,128)(2,1)S(1)} %get-tuple-element.167), channel_id=1, source_target_pairs={{0,2},{1,3},{2,0},{3,1},{4,6},{5,7},{6,4},{7,5},{8,10},{9,11},{10,... | collective-permute-start | bytes 983048 | tf_op jit(solution)/shard_map/ppermute | solution.py:24
  174.5 9.6 %collective-permute-start.43 = (bf16[80,2048]{1,0:T(8,128)(2,1)S(1)}, bf16[80,2048]{1,0:T(8,128)(2,1)S(1)}, u32[]{:S(2)}, u32[]{:S(2)}) collective-permute-start(bf16[80,2048]{1,0:T(8,128)(2,1)S(1)} %get-tuple-element.168), channel_id=1, source_target_pairs={{0,4},{1,5},{2,6},{3,7},{4,0},{5,1},{6,2},{7,3},{8,12},{9,13},{10,... | collective-permute-start | bytes 983048 | tf_op jit(solution)/shard_map/ppermute | solution.py:24
  175.5 12.1 %collective-permute-start.44 = (bf16[80,2048]{1,0:T(8,128)(2,1)S(1)}, bf16[80,2048]{1,0:T(8,128)(2,1)S(1)}, u32[]{:S(2)}, u32[]{:S(2)}) collective-permute-start(bf16[80,2048]{1,0:T(8,128)(2,1)S(1)} %get-tuple-element.169), channel_id=1, source_target_pairs={{0,6},{1,7},{2,4},{3,5},{4,2},{5,3},{6,0},{7,1},{8,14},{9,15},{10,... | collective-permute-start | bytes 983048 | tf_op jit(solution)/shard_map/ppermute | solution.py:24
  189.4 12.8 %collective-permute-start.47 = (bf16[128,2048]{1,0:T(8,128)(2,1)S(1)}, bf16[128,2048]{1,0:T(8,128)(2,1)S(1)}, u32[]{:S(2)}, u32[]{:S(2)}) collective-permute-start(bf16[128,2048]{1,0:T(8,128)(2,1)S(1)} %merge.6), channel_id=1, source_target_pairs={{0,8},{8,16},{16,24},{24,0},{1,9},{9,17},{17,25},{25,1},{2,10},{10... | collective-permute-start | bytes 1572872 | tf_op jit(solution)/shard_map/ppermute | solution.py:29
  189.5 8.4 %collective-permute-start.35 = (bf16[80,2048]{1,0:T(8,128)(2,1)S(1)}, bf16[80,2048]{1,0:T(8,128)(2,1)S(1)}, u32[]{:S(2)}, u32[]{:S(2)}) collective-permute-start(bf16[80,2048]{1,0:T(8,128)(2,1)S(1)} %get-tuple-element.149), channel_id=1, source_target_pairs={{0,2},{1,3},{2,0},{3,1},{4,6},{5,7},{6,4},{7,5},{8,10},{9,11},{10,... | collective-permute-start | bytes 983048 | tf_op jit(solution)/shard_map/ppermute | solution.py:24
  190.9 11.4 %collective-permute-start.36 = (bf16[80,2048]{1,0:T(8,128)(2,1)S(1)}, bf16[80,2048]{1,0:T(8,128)(2,1)S(1)}, u32[]{:S(2)}, u32[]{:S(2)}) collective-permute-start(bf16[80,2048]{1,0:T(8,128)(2,1)S(1)} %get-tuple-element.150), channel_id=1, source_target_pairs={{0,4},{1,5},{2,6},{3,7},{4,0},{5,1},{6,2},{7,3},{8,12},{9,13},{10,... | collective-permute-start | bytes 983048 | tf_op jit(solution)/shard_map/ppermute | solution.py:24
  191.9 10.4 %collective-permute-start.37 = (bf16[80,2048]{1,0:T(8,128)(2,1)S(1)}, bf16[80,2048]{1,0:T(8,128)(2,1)S(1)}, u32[]{:S(2)}, u32[]{:S(2)}) collective-permute-start(bf16[80,2048]{1,0:T(8,128)(2,1)S(1)} %get-tuple-element.151), channel_id=1, source_target_pairs={{0,6},{1,7},{2,4},{3,5},{4,2},{5,3},{6,0},{7,1},{8,14},{9,15},{10,... | collective-permute-start | bytes 983048 | tf_op jit(solution)/shard_map/ppermute | solution.py:24
  (12 other events, 245.9 us)

commit v3 on v2

--- a/solution.py
+++ b/solution.py
@@ -566,7 +566,7 @@
     )(hidden, gain[None, :])
 
 
-def gather_blocks(rows, first):
+def gather_blocks(rows, first, second):
     half = rows.shape[0] // 2
     from_x, from_y = swap(rows, 2), swap(rows, 4)
     beside = swap(after(rows, from_x), 1)
@@ -575,7 +575,7 @@
     near = jnp.concatenate([from_x, from_y], axis=0)
     near_beside = swap(near, 1)
     return (
-        [[rows, beside], [near], [near_beside], [far, swap(far, 1)]],
+        [[rows, beside], [near], [near_beside], [far, swap(after(far, second), 1)]],
         [[0, 1], [2, 4], [3, 5], [6, 7]],
     )
 
@@ -687,7 +687,7 @@
         near_gates, near_places = gate_table(expert_ids, gates)
         own_in, own_down = w_in[0], w_down[0]
         pair_in = swap(own_in, 1)
-        groups, names = gather_blocks(normed_attn, (near_places, pair_in))
+        groups, names = gather_blocks(normed_attn, (pair_in,), near_places)
         far, late = groups[-1]
         own_out, late_down = after(w_out, far), after(own_down, late)
         out_blocks = [w_out] + [swap(own_out, bits) for bits in (2, 4, 6)]

time: 209 us -> 209 us (level)
  starting transfers between devices: 50.9 us -> 53.8 us
  waiting for transfers between devices: 81.3 us -> 78.9 us
    ppermute x40, waiting for transfers between devices: 73.6 us -> 71.3 us  [swap(): return lax.ppermute(values, 'exp', [(d, d ^ bits) for d in range(count)])]
    ppermute x40, starting transfers between devices: 40.7 us -> 42.8 us  [swap(): return lax.ppermute(values, 'exp', [(d, d ^ bits) for d in range(count)])]
  transfers between devices with their start and end apart: 48 -> 48, of which waited for: 24 -> 24; matrix products, arithmetic and copies ran while one was open for 4% -> 3% of each run, Pallas kernels for 26% -> 27%
where the time goes in v3:
time: 209 us; the launch traced here: 205 us
  waiting for transfers between devices  78.9 us (38%)
  Pallas kernels  62.1 us (30%)
  starting transfers between devices  53.8 us (26%)
  other arithmetic  6.48 us (3%)
    ppermute x40, waiting for transfers between devices, swap(): return lax.ppermute(values, 'exp', [(d, d ^ bits) for d in range(count)])  71.3 us
    ppermute x40, starting transfers between devices, swap(): return lax.ppermute(values, 'exp', [(d, d ^ bits) for d in range(count)])  42.8 us
    pallas_call x4, Pallas kernels, expert_rows(): pl.pallas_call(functools.partial(experts_kernel, part, wide), out_shape=[...  30.8 us
    pallas_call x1, Pallas kernels, attention(): pl.pallas_call(functools.partial(attention_kernel, layout, block_rows, ti...  15.9 us
    ppermute x8, starting transfers between devices, shift(): lax.ppermute(values, 'req', [(d, (d + steps) % count) for d in range(coun...  11 us
    pallas_call x4, Pallas kernels, merge(): pl.pallas_call(functools.partial(merge_kernel, count), out_shape=jax.Shap...  8.25 us
    ppermute x8, waiting for transfers between devices, shift(): lax.ppermute(values, 'req', [(d, (d + steps) % count) for d in range(coun...  7.65 us
    pallas_call x4, Pallas kernels, pick(): pl.pallas_call(pick_kernel, out_shape=[jax.ShapeDtypeStruct((capacity, wi...  5.56 us
  transfers between devices with their start and end apart: 48, of which 24 were waited for; matrix products, arithmetic and copies ran while one was open for 3% of the time, Pallas kernels for 27%

profile of v3, /device:TPU:0, one launch (start us, length us, event | category | flops | bytes accessed | tf_op | source)
XLA Modules:
  0.0 205.2 jit_solution(9323053538067206848)
XLA Ops:
  3.1 2.6 %collective-permute-start.4 = (bf16[128,2048]{1,0:T(8,128)(2,1)S(1)}, bf16[128,2048]{1,0:T(8,128)(2,1)S(1)}, u32[]{:S(2)}, u32[]{:S(2)}) collective-permute-start(bf16[128,2048]{1,0:T(8,128)(2,1)S(1)} %norm.1.refs_5_), channel_id=1, source_target_pairs={{0,4},{1,5},{2,6},{3,7},{4,0},{5,1},{6,2},{7,3},{8,12},{9,13},{10,... | collective-permute-start | bytes 1572872 | tf_op jit(solution)/shard_map/ppermute | solution.py:24
  5.7 1.5 collective-permute-start.2
  10.0 1.6 collective-permute-start
  11.7 3.9 %collective-permute-done = f32[16,128]{1,0:T(8,128)S(1)} collective-permute-done((f32[16,128]{1,0:T(8,128)S(1)}, f32[16,128]{1,0:T(8,128)S(1)}, u32[]{:S(2)}, u32[]{:S(2)}) %collective-permute-start) | collective-permute-done | bytes 8224 | tf_op jit(solution)/shard_map/ppermute | solution.py:29
  16.4 3.8 %collective-permute-done.1 = f32[2,16,128]{2,1,0:T(8,128)S(1)} collective-permute-done((f32[2,16,128]{2,1,0:T(8,128)S(1)}, f32[2,16,128]{2,1,0:T(8,128)S(1)}, u32[]{:S(2)}, u32[]{:S(2)}) %collective-permute-start.1) | collective-permute-done | bytes 16416 | tf_op jit(solution)/shard_map/ppermute | solution.py:29
  23.0 4.4 %collective-permute-done.7 = bf16[64,2048]{1,0:T(8,128)(2,1)S(1)} collective-permute-done((bf16[64,2048]{1,0:T(8,128)(2,1)S(1)}, bf16[64,2048]{1,0:T(8,128)(2,1)S(1)}, u32[]{:S(2)}, u32[]{:S(2)}) %collective-permute-start.7) | collective-permute-done | bytes 262176 | tf_op jit(solution)/shard_map/ppermute | solution.py:24
  27.5 1.6 collective-permute-done.8
  29.1 1.9 collective-permute-done.9.refs_10_
  32.6 1.9 fusion
  34.9 2.4 %collective-permute-start.16 = (bf16[128,2048]{1,0:T(8,128)(2,1)S(1)}, bf16[128,2048]{1,0:T(8,128)(2,1)S(1)}, u32[]{:S(2)}, u32[]{:S(2)}) collective-permute-start(bf16[128,2048]{1,0:T(8,128)(2,1)S(1)} %copy-done.3), channel_id=1, source_target_pairs={{0,6},{1,7},{2,4},{3,5},{4,2},{5,3},{6,0},{7,1},{8,14},{9,15},{10,... | collective-permute-start | bytes 1572872 | tf_op jit(solution)/shard_map/ppermute | solution.py:24
  38.9 15.9 %attention.1 = (bf16[1024,128]{1,0:T(8,128)(2,1)S(1)}, bf16[2,1024,128]{2,1,0:T(8,128)(2,1)}) custom-call(s32[1]{0:T(128)} %bitcast.7.refs_0_, s32[1]{0:T(128)} %copy.20.refs_1_, s32[4]{0:T(128)S(1)} %copy-done.7, s32[4,32]{1,0:T(4,128)S(1)} %copy-done.6, s32[1,32]{1,0:T(1,128)S(1)} %copy-done.8, bf16[128,2048]{1,0:T(8,128)(2,1)S(1)} %norm.1.refs_5_, ...), custom_call_target="tpu_custom_call" | custom-call | flops 4294967296 | bytes 20971520 | tf_op jit(solution)/shard_map/attention/pallas_call | solution.py:445
  55.0 1.9 collective-permute-start.13
  58.5 3.4 %collective-permute-done.15.refs_6_ = bf16[128,2048]{1,0:T(8,128)(2,1)S(1)} collective-permute-done((bf16[128,2048]{1,0:T(8,128)(2,1)S(1)}, bf16[128,2048]{1,0:T(8,128)(2,1)S(1)}, u32[]{:S(2)}, u32[]{:S(2)}) %collective-permute-start.15) | collective-permute-done | bytes 524320 | tf_op jit(solution)/shard_map/ppermute | solution.py:24
  65.1 1.9 collective-permute-done.17.refs_1_
  67.4 1.6 collective-permute-start.21
  70.4 1.5 collective-permute-start.18
  73.9 7.1 %collective-permute-done.18.refs_1_ = bf16[80,2048]{1,0:T(8,128)(2,1)S(1)} collective-permute-done((bf16[80,2048]{1,0:T(8,128)(2,1)S(1)}, bf16[80,2048]{1,0:T(8,128)(2,1)S(1)}, u32[]{:S(2)}, u32[]{:S(2)}) %collective-permute-start.18) | collective-permute-done | bytes 327712 | tf_op jit(solution)/shard_map/ppermute | solution.py:24
  81.1 7.1 %collective-permute-done.19.refs_2_ = bf16[80,2048]{1,0:T(8,128)(2,1)S(1)} collective-permute-done((bf16[80,2048]{1,0:T(8,128)(2,1)S(1)}, bf16[80,2048]{1,0:T(8,128)(2,1)S(1)}, u32[]{:S(2)}, u32[]{:S(2)}) %collective-permute-start.19) | collective-permute-done | bytes 327712 | tf_op jit(solution)/shard_map/ppermute | solution.py:24
  88.2 1.6 collective-permute-start.22
  93.1 1.6 collective-permute-start.28
  94.7 7.6 %experts.4 = (bf16[80,2048]{1,0:T(8,128)(2,1)S(1)}, bf16[80,2048]{1,0:T(8,128)(2,1)S(1)}, bf16[80,2048]{1,0:T(8,128)(2,1)S(1)}, bf16[80,2048]{1,0:T(8,128)(2,1)S(1)}) custom-call(bf16[80,2048]{1,0:T(8,128)(2,1)S(1)} %get-tuple-element.106.refs_0_, bf16[80,2048]{1,0:T(8,128)(2,1)S(1)} %collective-permute-done.18.refs_1_, ...), custom_call_target="tpu_custom_call" | custom-call | flops 4026531840 | bytes 16777216 | tf_op jit(solution)/shard_map/experts/pallas_call | solution.py:116
  102.3 4.5 %collective-permute-done.27.refs_2_ = bf16[80,2048]{1,0:T(8,128)(2,1)S(1)} collective-permute-done((bf16[80,2048]{1,0:T(8,128)(2,1)S(1)}, bf16[80,2048]{1,0:T(8,128)(2,1)S(1)}, u32[]{:S(2)}, u32[]{:S(2)}) %collective-permute-start.27) | collective-permute-done | bytes 327712 | tf_op jit(solution)/shard_map/ppermute | solution.py:24
  106.8 1.4 pick.5
  110.1 1.7 collective-permute-start.25
  111.8 7.6 %experts.5 = (bf16[80,2048]{1,0:T(8,128)(2,1)S(1)}, bf16[80,2048]{1,0:T(8,128)(2,1)S(1)}, bf16[80,2048]{1,0:T(8,128)(2,1)S(1)}, bf16[80,2048]{1,0:T(8,128)(2,1)S(1)}) custom-call(bf16[80,2048]{1,0:T(8,128)(2,1)S(1)} %get-tuple-element.129.refs_0_, bf16[80,2048]{1,0:T(8,128)(2,1)S(1)} %collective-permute-done.26.refs_1_, ...), custom_call_target="tpu_custom_call" | custom-call | flops 4026531840 | bytes 16777216 | tf_op jit(solution)/shard_map/experts/pallas_call | solution.py:116
  121.2 1.7 collective-permute-start.31
  122.9 1.6 collective-permute-start.38
  124.5 2.0 collective-permute-done.25.refs_3_
  126.5 8.0 %experts.6 = (bf16[80,2048]{1,0:T(8,128)(2,1)S(1)}, bf16[80,2048]{1,0:T(8,128)(2,1)S(1)}, bf16[80,2048]{1,0:T(8,128)(2,1)S(1)}, bf16[80,2048]{1,0:T(8,128)(2,1)S(1)}) custom-call(bf16[80,2048]{1,0:T(8,128)(2,1)S(1)} %get-tuple-element.137.refs_0_, bf16[80,2048]{1,0:T(8,128)(2,1)S(1)} %collective-permute-done.23.refs_1_, ...), custom_call_target="tpu_custom_call" | custom-call | flops 4026531840 | bytes 16777216 | tf_op jit(solution)/shard_map/experts/pallas_call | solution.py:116
  134.5 2.8 %collective-permute-done.30.refs_2_ = bf16[80,2048]{1,0:T(8,128)(2,1)S(1)} collective-permute-done((bf16[80,2048]{1,0:T(8,128)(2,1)S(1)}, bf16[80,2048]{1,0:T(8,128)(2,1)S(1)}, u32[]{:S(2)}, u32[]{:S(2)}) %collective-permute-start.30) | collective-permute-done | bytes 327712 | tf_op jit(solution)/shard_map/ppermute | solution.py:24
  139.6 1.8 merge.4
  141.4 1.6 collective-permute-start.45
  143.0 1.7 collective-permute-start.34
  144.8 1.4 pick.7
  148.8 5.2 %collective-permute-done.33.refs_2_ = bf16[80,2048]{1,0:T(8,128)(2,1)S(1)} collective-permute-done((bf16[80,2048]{1,0:T(8,128)(2,1)S(1)}, bf16[80,2048]{1,0:T(8,128)(2,1)S(1)}, u32[]{:S(2)}, u32[]{:S(2)}) %collective-permute-start.33) | collective-permute-done | bytes 327712 | tf_op jit(solution)/shard_map/ppermute | solution.py:24
  155.3 1.9 merge.5
  157.2 2.1 %collective-permute-start.46 = (bf16[128,2048]{1,0:T(8,128)(2,1)S(1)}, bf16[128,2048]{1,0:T(8,128)(2,1)S(1)}, u32[]{:S(2)}, u32[]{:S(2)}) collective-permute-start(bf16[128,2048]{1,0:T(8,128)(2,1)S(1)} %merge.5), channel_id=1, source_target_pairs={{0,8},{8,16},{16,24},{24,0},{1,9},{9,17},{17,25},{25,1},{2,10},{10... | collective-permute-start | bytes 1572872 | tf_op jit(solution)/shard_map/ppermute | solution.py:29
  159.3 2.5 %collective-permute-done.39.refs_1_ = bf16[80,2048]{1,0:T(8,128)(2,1)S(1)} collective-permute-done((bf16[80,2048]{1,0:T(8,128)(2,1)S(1)}, bf16[80,2048]{1,0:T(8,128)(2,1)S(1)}, u32[]{:S(2)}, u32[]{:S(2)}) %collective-permute-start.39) | collective-permute-done | bytes 327712 | tf_op jit(solution)/shard_map/ppermute | solution.py:24
  161.8 4.5 %collective-permute-done.40.refs_2_ = bf16[80,2048]{1,0:T(8,128)(2,1)S(1)} collective-permute-done((bf16[80,2048]{1,0:T(8,128)(2,1)S(1)}, bf16[80,2048]{1,0:T(8,128)(2,1)S(1)}, u32[]{:S(2)}, u32[]{:S(2)}) %collective-permute-start.40) | collective-permute-done | bytes 327712 | tf_op jit(solution)/shard_map/ppermute | solution.py:24
  166.4 7.7 %experts.7 = (bf16[80,2048]{1,0:T(8,128)(2,1)S(1)}, bf16[80,2048]{1,0:T(8,128)(2,1)S(1)}, bf16[80,2048]{1,0:T(8,128)(2,1)S(1)}, bf16[80,2048]{1,0:T(8,128)(2,1)S(1)}) custom-call(bf16[80,2048]{1,0:T(8,128)(2,1)S(1)} %get-tuple-element.161.refs_0_, bf16[80,2048]{1,0:T(8,128)(2,1)S(1)} %collective-permute-done.39.refs_1_, ...), custom_call_target="tpu_custom_call" | custom-call | flops 4026531840 | bytes 16777216 | tf_op jit(solution)/shard_map/experts/pallas_call | solution.py:116
  175.8 1.9 collective-permute-start.44
  177.6 5.9 %collective-permute-done.42.refs_1_ = bf16[80,2048]{1,0:T(8,128)(2,1)S(1)} collective-permute-done((bf16[80,2048]{1,0:T(8,128)(2,1)S(1)}, bf16[80,2048]{1,0:T(8,128)(2,1)S(1)}, u32[]{:S(2)}, u32[]{:S(2)}) %collective-permute-start.42) | collective-permute-done | bytes 327712 | tf_op jit(solution)/shard_map/ppermute | solution.py:24
  184.3 3.7 %collective-permute-done.44.refs_3_ = bf16[80,2048]{1,0:T(8,128)(2,1)S(1)} collective-permute-done((bf16[80,2048]{1,0:T(8,128)(2,1)S(1)}, bf16[80,2048]{1,0:T(8,128)(2,1)S(1)}, u32[]{:S(2)}, u32[]{:S(2)}) %collective-permute-start.44) | collective-permute-done | bytes 327712 | tf_op jit(solution)/shard_map/ppermute | solution.py:24
  188.0 1.9 merge.6
  190.8 1.5 collective-permute-start.36
  193.5 4.7 %collective-permute-done.35.refs_1_ = bf16[80,2048]{1,0:T(8,128)(2,1)S(1)} collective-permute-done((bf16[80,2048]{1,0:T(8,128)(2,1)S(1)}, bf16[80,2048]{1,0:T(8,128)(2,1)S(1)}, u32[]{:S(2)}, u32[]{:S(2)}) %collective-permute-start.35) | collective-permute-done | bytes 327712 | tf_op jit(solution)/shard_map/ppermute | solution.py:24
  198.2 4.1 %collective-permute-done.36.refs_2_ = bf16[80,2048]{1,0:T(8,128)(2,1)S(1)} collective-permute-done((bf16[80,2048]{1,0:T(8,128)(2,1)S(1)}, bf16[80,2048]{1,0:T(8,128)(2,1)S(1)}, u32[]{:S(2)}, u32[]{:S(2)}) %collective-permute-start.36) | collective-permute-done | bytes 327712 | tf_op jit(solution)/shard_map/ppermute | solution.py:24
  202.3 2.7 %merge.7 = bf16[128,2048]{1,0:T(8,128)(2,1)} custom-call(f32[8,128]{1,0:T(8,128)S(1)} %get-tuple-element.185.gate_ref, s32[8,128]{1,0:T(8,128)S(1)} %get-tuple-element.181.place_ref, bf16[80,2048]{1,0:T(8,128)(2,1)S(1)} %get-tuple-element.110.refs_0_, bf16[80,2048]{1,0:T(8,128)(2,1)S(1)} %collective-permute-done.35.refs_1_, ...), custom_call_target="tpu_custom_call" | custom-call | flops 167772160 | bytes 1048576 | tf_op jit(solution)/shard_map/merge/pallas_call | solution.py:209
  (112 shorter events, 38.6 us)
Async XLA Ops:
  0.6 19.8 %collective-permute-start.6 = (bf16[2048,1024]{1,0:T(8,128)(2,1)}, bf16[2048,1024]{1,0:T(8,128)(2,1)}, u32[]{:S(2)}, u32[]{:S(2)}) collective-permute-start(bf16[2048,1024]{1,0:T(8,128)(2,1)} %bitcast.30), channel_id=1, source_target_pairs={{0,1},{1,0},{2,3},{3,2},{4,5},{5,4},{6,7},{7,6},{8,9},{9,8},{10,11... | collective-permute-start | bytes 12582920 | tf_op jit(solution)/shard_map/ppermute | solution.py:24
  3.1 17.2 %collective-permute-start.4 = (bf16[128,2048]{1,0:T(8,128)(2,1)S(1)}, bf16[128,2048]{1,0:T(8,128)(2,1)S(1)}, u32[]{:S(2)}, u32[]{:S(2)}) collective-permute-start(bf16[128,2048]{1,0:T(8,128)(2,1)S(1)} %norm.1.refs_5_), channel_id=1, source_target_pairs={{0,4},{1,5},{2,6},{3,7},{4,0},{5,1},{6,2},{7,3},{8,12},{9,13},{10,... | collective-permute-start | bytes 1572872 | tf_op jit(solution)/shard_map/ppermute | solution.py:24
  5.7 14.7 %collective-permute-start.2 = (bf16[128,2048]{1,0:T(8,128)(2,1)S(1)}, bf16[128,2048]{1,0:T(8,128)(2,1)S(1)}, u32[]{:S(2)}, u32[]{:S(2)}) collective-permute-start(bf16[128,2048]{1,0:T(8,128)(2,1)S(1)} %norm.1.refs_5_), channel_id=1, source_target_pairs={{0,2},{1,3},{2,0},{3,1},{4,6},{5,7},{6,4},{7,5},{8,10},{9,11},{10,... | collective-permute-start | bytes 1572872 | tf_op jit(solution)/shard_map/ppermute | solution.py:24
  10.0 5.5 %collective-permute-start = (f32[16,128]{1,0:T(8,128)S(1)}, f32[16,128]{1,0:T(8,128)S(1)}, u32[]{:S(2)}, u32[]{:S(2)}) collective-permute-start(f32[16,128]{1,0:T(8,128)S(1)} %select_reduce_fusion.1), channel_id=1, source_target_pairs={{0,8},{8,16},{16,24},{24,0},{1,9},{9,17},{17,25},{25,1},{2,10},{10... | collective-permute-start | bytes 24584 | tf_op jit(solution)/shard_map/ppermute | solution.py:29
  15.5 4.6 %collective-permute-start.1 = (f32[2,16,128]{2,1,0:T(8,128)S(1)}, f32[2,16,128]{2,1,0:T(8,128)S(1)}, u32[]{:S(2)}, u32[]{:S(2)}) collective-permute-start(f32[2,16,128]{2,1,0:T(8,128)S(1)} %pad_maximum_fusion.3), channel_id=1, source_target_pairs={{0,16},{8,24},{16,0},{24,8},{1,17},{9,25},{17,1},{25,9},{2,18},{10... | collective-permute-start | bytes 49160 | tf_op jit(solution)/shard_map/ppermute | solution.py:29
  20.4 7.0 %collective-permute-start.7 = (bf16[64,2048]{1,0:T(8,128)(2,1)S(1)}, bf16[64,2048]{1,0:T(8,128)(2,1)S(1)}, u32[]{:S(2)}, u32[]{:S(2)}) collective-permute-start(bf16[64,2048]{1,0:T(8,128)(2,1)S(1)} %slice.49), channel_id=1, source_target_pairs={{0,4},{1,5},{2,6},{3,7},{4,0},{5,1},{6,2},{7,3},{8,12},{9,13},{10,... | collective-permute-start | bytes 786440 | tf_op jit(solution)/shard_map/ppermute | solution.py:24
  22.1 6.9 %collective-permute-start.8 = (bf16[64,2048]{1,0:T(8,128)(2,1)S(1)}, bf16[64,2048]{1,0:T(8,128)(2,1)S(1)}, u32[]{:S(2)}, u32[]{:S(2)}) collective-permute-start(bf16[64,2048]{1,0:T(8,128)(2,1)S(1)} %slice.50), channel_id=1, source_target_pairs={{0,2},{1,3},{2,0},{3,1},{4,6},{5,7},{6,4},{7,5},{8,10},{9,11},{10,... | collective-permute-start | bytes 786440 | tf_op jit(solution)/shard_map/ppermute | solution.py:24
  29.1 2.0 collective-permute-start.9
  31.0 23.9 %collective-permute-start.10 = (bf16[512,2048]{1,0:T(8,128)(2,1)}, bf16[512,2048]{1,0:T(8,128)(2,1)S(1)}, u32[]{:S(2)}, u32[]{:S(2)}) collective-permute-start(bf16[512,2048]{1,0:T(8,128)(2,1)} %bitcast.35), channel_id=1, source_target_pairs={{0,1},{1,0},{2,3},{3,2},{4,5},{5,4},{6,7},{7,6},{8,9},{9,8},{10,11... | collective-permute-start | bytes 6291464 | tf_op jit(solution)/shard_map/ppermute | solution.py:24
  31.3 7.6 %collective-permute-start.5 = (bf16[256,2048]{1,0:T(8,128)(2,1)S(1)}, bf16[256,2048]{1,0:T(8,128)(2,1)S(1)}, u32[]{:S(2)}, u32[]{:S(2)}) collective-permute-start(bf16[256,2048]{1,0:T(8,128)(2,1)S(1)} %constant_dynamic-update-slice_fusion.refs_7_), channel_id=1, source_target_pairs={{0,1},{1,0},{2,3},{3,2},{4,5},{5,4},{6,7},{7,6},{8,9},{9,8},{10,11... | collective-permute-start | bytes 3145736 | tf_op jit(solution)/shard_map/ppermute | solution.py:24
  32.5 5.4 %collective-permute-start.3 = (bf16[128,2048]{1,0:T(8,128)(2,1)S(1)}, bf16[128,2048]{1,0:T(8,128)(2,1)S(1)}, u32[]{:S(2)}, u32[]{:S(2)}) collective-permute-start(bf16[128,2048]{1,0:T(8,128)(2,1)S(1)} %norm.1.refs_5_), channel_id=1, source_target_pairs={{0,1},{1,0},{2,3},{3,2},{4,5},{5,4},{6,7},{7,6},{8,9},{9,8},{10,11... | collective-permute-start | bytes 1572872 | tf_op jit(solution)/shard_map/ppermute | solution.py:24
  34.9 22.6 %collective-permute-start.16 = (bf16[128,2048]{1,0:T(8,128)(2,1)S(1)}, bf16[128,2048]{1,0:T(8,128)(2,1)S(1)}, u32[]{:S(2)}, u32[]{:S(2)}) collective-permute-start(bf16[128,2048]{1,0:T(8,128)(2,1)S(1)} %copy-done.3), channel_id=1, source_target_pairs={{0,6},{1,7},{2,4},{3,5},{4,2},{5,3},{6,0},{7,1},{8,14},{9,15},{10,... | collective-permute-start | bytes 1572872 | tf_op jit(solution)/shard_map/ppermute | solution.py:24
  37.2 24.7 %collective-permute-start.15 = (bf16[128,2048]{1,0:T(8,128)(2,1)S(1)}, bf16[128,2048]{1,0:T(8,128)(2,1)S(1)}, u32[]{:S(2)}, u32[]{:S(2)}) collective-permute-start(bf16[128,2048]{1,0:T(8,128)(2,1)S(1)} %copy-done.3), channel_id=1, source_target_pairs={{0,4},{1,5},{2,6},{3,7},{4,0},{5,1},{6,2},{7,3},{8,12},{9,13},{10,... | collective-permute-start | bytes 1572872 | tf_op jit(solution)/shard_map/ppermute | solution.py:24
  37.9 24.1 %collective-permute-start.14 = (bf16[128,2048]{1,0:T(8,128)(2,1)S(1)}, bf16[128,2048]{1,0:T(8,128)(2,1)S(1)}, u32[]{:S(2)}, u32[]{:S(2)}) collective-permute-start(bf16[128,2048]{1,0:T(8,128)(2,1)S(1)} %copy-done.3), channel_id=1, source_target_pairs={{0,2},{1,3},{2,0},{3,1},{4,6},{5,7},{6,4},{7,5},{8,10},{9,11},{10,... | collective-permute-start | bytes 1572872 | tf_op jit(solution)/shard_map/ppermute | solution.py:24
  55.0 8.3 %collective-permute-start.13 = (bf16[256,128]{1,0:T(8,128)(2,1)S(1)}, bf16[256,128]{1,0:T(8,128)(2,1)S(1)}, u32[]{:S(2)}, u32[]{:S(2)}) collective-permute-start(bf16[256,128]{1,0:T(8,128)(2,1)S(1)} %get-tuple-element.174), channel_id=1, source_target_pairs={{0,6},{1,7},{2,4},{3,5},{4,2},{5,3},{6,0},{7,1},{8,14},{9,15},{10,... | collective-permute-start | bytes 196616 | tf_op jit(solution)/shard_map/ppermute | solution.py:24
  56.9 7.2 %collective-permute-start.12 = (bf16[256,128]{1,0:T(8,128)(2,1)S(1)}, bf16[256,128]{1,0:T(8,128)(2,1)S(1)}, u32[]{:S(2)}, u32[]{:S(2)}) collective-permute-start(bf16[256,128]{1,0:T(8,128)(2,1)S(1)} %get-tuple-element.175), channel_id=1, source_target_pairs={{0,4},{1,5},{2,6},{3,7},{4,0},{5,1},{6,2},{7,3},{8,12},{9,13},{10,... | collective-permute-start | bytes 196616 | tf_op jit(solution)/shard_map/ppermute | solution.py:24
  57.5 6.6 %collective-permute-start.11 = (bf16[256,128]{1,0:T(8,128)(2,1)S(1)}, bf16[256,128]{1,0:T(8,128)(2,1)S(1)}, u32[]{:S(2)}, u32[]{:S(2)}) collective-permute-start(bf16[256,128]{1,0:T(8,128)(2,1)S(1)} %get-tuple-element.176), channel_id=1, source_target_pairs={{0,2},{1,3},{2,0},{3,1},{4,6},{5,7},{6,4},{7,5},{8,10},{9,11},{10,... | collective-permute-start | bytes 196616 | tf_op jit(solution)/shard_map/ppermute | solution.py:24
  65.0 2.0 collective-permute-start.17
  67.4 20.8 %collective-permute-start.21 = (bf16[128,2048]{1,0:T(8,128)(2,1)S(1)}, bf16[128,2048]{1,0:T(8,128)(2,1)S(1)}, u32[]{:S(2)}, u32[]{:S(2)}) collective-permute-start(bf16[128,2048]{1,0:T(8,128)(2,1)S(1)} %get-tuple-element.98.rows_ref), channel_id=1, source_target_pairs={{0,8},{8,16},{16,24},{24,0},{1,9},{9,17},{17,25},{25,1},{2,10},{10... | collective-permute-start | bytes 1572872 | tf_op jit(solution)/shard_map/ppermute | solution.py:29
  70.4 10.7 %collective-permute-start.18 = (bf16[80,2048]{1,0:T(8,128)(2,1)S(1)}, bf16[80,2048]{1,0:T(8,128)(2,1)S(1)}, u32[]{:S(2)}, u32[]{:S(2)}) collective-permute-start(bf16[80,2048]{1,0:T(8,128)(2,1)S(1)} %get-tuple-element.103), channel_id=1, source_target_pairs={{0,2},{1,3},{2,0},{3,1},{4,6},{5,7},{6,4},{7,5},{8,10},{9,11},{10,... | collective-permute-start | bytes 983048 | tf_op jit(solution)/shard_map/ppermute | solution.py:24
  71.9 16.2 %collective-permute-start.19 = (bf16[80,2048]{1,0:T(8,128)(2,1)S(1)}, bf16[80,2048]{1,0:T(8,128)(2,1)S(1)}, u32[]{:S(2)}, u32[]{:S(2)}) collective-permute-start(bf16[80,2048]{1,0:T(8,128)(2,1)S(1)} %get-tuple-element.104), channel_id=1, source_target_pairs={{0,4},{1,5},{2,6},{3,7},{4,0},{5,1},{6,2},{7,3},{8,12},{9,13},{10,... | collective-permute-start | bytes 983048 | tf_op jit(solution)/shard_map/ppermute | solution.py:24
  72.8 15.4 %collective-permute-start.20 = (bf16[80,2048]{1,0:T(8,128)(2,1)S(1)}, bf16[80,2048]{1,0:T(8,128)(2,1)S(1)}, u32[]{:S(2)}, u32[]{:S(2)}) collective-permute-start(bf16[80,2048]{1,0:T(8,128)(2,1)S(1)} %get-tuple-element.105), channel_id=1, source_target_pairs={{0,6},{1,7},{2,4},{3,5},{4,2},{5,3},{6,0},{7,1},{8,14},{9,15},{10,... | collective-permute-start | bytes 983048 | tf_op jit(solution)/shard_map/ppermute | solution.py:24
  88.2 18.6 %collective-permute-start.22 = (bf16[128,2048]{1,0:T(8,128)(2,1)S(1)}, bf16[128,2048]{1,0:T(8,128)(2,1)S(1)}, u32[]{:S(2)}, u32[]{:S(2)}) collective-permute-start(bf16[128,2048]{1,0:T(8,128)(2,1)S(1)} %collective-permute-done.21.rows_ref), channel_id=1, source_target_pairs={{0,8},{8,16},{16,24},{24,0},{1,9},{9,17},{17,25},{25,1},{2,10},{10... | collective-permute-start | bytes 1572872 | tf_op jit(solution)/shard_map/ppermute | solution.py:29
  91.1 11.1 %collective-permute-start.26 = (bf16[80,2048]{1,0:T(8,128)(2,1)S(1)}, bf16[80,2048]{1,0:T(8,128)(2,1)S(1)}, u32[]{:S(2)}, u32[]{:S(2)}) collective-permute-start(bf16[80,2048]{1,0:T(8,128)(2,1)S(1)} %get-tuple-element.126), channel_id=1, source_target_pairs={{0,2},{1,3},{2,0},{3,1},{4,6},{5,7},{6,4},{7,5},{8,10},{9,11},{10,... | collective-permute-start | bytes 983048 | tf_op jit(solution)/shard_map/ppermute | solution.py:24
  91.7 15.1 %collective-permute-start.27 = (bf16[80,2048]{1,0:T(8,128)(2,1)S(1)}, bf16[80,2048]{1,0:T(8,128)(2,1)S(1)}, u32[]{:S(2)}, u32[]{:S(2)}) collective-permute-start(bf16[80,2048]{1,0:T(8,128)(2,1)S(1)} %get-tuple-element.127), channel_id=1, source_target_pairs={{0,4},{1,5},{2,6},{3,7},{4,0},{5,1},{6,2},{7,3},{8,12},{9,13},{10,... | collective-permute-start | bytes 983048 | tf_op jit(solution)/shard_map/ppermute | solution.py:24
  93.1 13.7 %collective-permute-start.28 = (bf16[80,2048]{1,0:T(8,128)(2,1)S(1)}, bf16[80,2048]{1,0:T(8,128)(2,1)S(1)}, u32[]{:S(2)}, u32[]{:S(2)}) collective-permute-start(bf16[80,2048]{1,0:T(8,128)(2,1)S(1)} %get-tuple-element.128), channel_id=1, source_target_pairs={{0,6},{1,7},{2,4},{3,5},{4,2},{5,3},{6,0},{7,1},{8,14},{9,15},{10,... | collective-permute-start | bytes 983048 | tf_op jit(solution)/shard_map/ppermute | solution.py:24
  108.2 13.0 %collective-permute-start.23 = (bf16[80,2048]{1,0:T(8,128)(2,1)S(1)}, bf16[80,2048]{1,0:T(8,128)(2,1)S(1)}, u32[]{:S(2)}, u32[]{:S(2)}) collective-permute-start(bf16[80,2048]{1,0:T(8,128)(2,1)S(1)} %get-tuple-element.119), channel_id=1, source_target_pairs={{0,2},{1,3},{2,0},{3,1},{4,6},{5,7},{6,4},{7,5},{8,10},{9,11},{10,... | collective-permute-start | bytes 983048 | tf_op jit(solution)/shard_map/ppermute | solution.py:24
  109.4 13.5 %collective-permute-start.24 = (bf16[80,2048]{1,0:T(8,128)(2,1)S(1)}, bf16[80,2048]{1,0:T(8,128)(2,1)S(1)}, u32[]{:S(2)}, u32[]{:S(2)}) collective-permute-start(bf16[80,2048]{1,0:T(8,128)(2,1)S(1)} %get-tuple-element.120), channel_id=1, source_target_pairs={{0,4},{1,5},{2,6},{3,7},{4,0},{5,1},{6,2},{7,3},{8,12},{9,13},{10,... | collective-permute-start | bytes 983048 | tf_op jit(solution)/shard_map/ppermute | solution.py:24
  110.1 16.4 %collective-permute-start.25 = (bf16[80,2048]{1,0:T(8,128)(2,1)S(1)}, bf16[80,2048]{1,0:T(8,128)(2,1)S(1)}, u32[]{:S(2)}, u32[]{:S(2)}) collective-permute-start(bf16[80,2048]{1,0:T(8,128)(2,1)S(1)} %get-tuple-element.121), channel_id=1, source_target_pairs={{0,6},{1,7},{2,4},{3,5},{4,2},{5,3},{6,0},{7,1},{8,14},{9,15},{10,... | collective-permute-start | bytes 983048 | tf_op jit(solution)/shard_map/ppermute | solution.py:24
  119.3 15.1 %collective-permute-start.29 = (bf16[80,2048]{1,0:T(8,128)(2,1)S(1)}, bf16[80,2048]{1,0:T(8,128)(2,1)S(1)}, u32[]{:S(2)}, u32[]{:S(2)}) collective-permute-start(bf16[80,2048]{1,0:T(8,128)(2,1)S(1)} %get-tuple-element.145), channel_id=1, source_target_pairs={{0,2},{1,3},{2,0},{3,1},{4,6},{5,7},{6,4},{7,5},{8,10},{9,11},{10,... | collective-permute-start | bytes 983048 | tf_op jit(solution)/shard_map/ppermute | solution.py:24
  120.6 16.7 %collective-permute-start.30 = (bf16[80,2048]{1,0:T(8,128)(2,1)S(1)}, bf16[80,2048]{1,0:T(8,128)(2,1)S(1)}, u32[]{:S(2)}, u32[]{:S(2)}) collective-permute-start(bf16[80,2048]{1,0:T(8,128)(2,1)S(1)} %get-tuple-element.146), channel_id=1, source_target_pairs={{0,4},{1,5},{2,6},{3,7},{4,0},{5,1},{6,2},{7,3},{8,12},{9,13},{10,... | collective-permute-start | bytes 983048 | tf_op jit(solution)/shard_map/ppermute | solution.py:24
  121.2 16.3 %collective-permute-start.31 = (bf16[80,2048]{1,0:T(8,128)(2,1)S(1)}, bf16[80,2048]{1,0:T(8,128)(2,1)S(1)}, u32[]{:S(2)}, u32[]{:S(2)}) collective-permute-start(bf16[80,2048]{1,0:T(8,128)(2,1)S(1)} %get-tuple-element.147), channel_id=1, source_target_pairs={{0,6},{1,7},{2,4},{3,5},{4,2},{5,3},{6,0},{7,1},{8,14},{9,15},{10,... | collective-permute-start | bytes 983048 | tf_op jit(solution)/shard_map/ppermute | solution.py:24
  122.9 21.9 %collective-permute-start.38 = (bf16[128,2048]{1,0:T(8,128)(2,1)S(1)}, bf16[128,2048]{1,0:T(8,128)(2,1)S(1)}, u32[]{:S(2)}, u32[]{:S(2)}) collective-permute-start(bf16[128,2048]{1,0:T(8,128)(2,1)S(1)} %collective-permute-done.22.rows_ref), channel_id=1, source_target_pairs={{0,8},{8,16},{16,24},{24,0},{1,9},{9,17},{17,25},{25,1},{2,10},{10... | collective-permute-start | bytes 1572872 | tf_op jit(solution)/shard_map/ppermute | solution.py:29
  137.5 10.3 %collective-permute-start.32 = (bf16[80,2048]{1,0:T(8,128)(2,1)S(1)}, bf16[80,2048]{1,0:T(8,128)(2,1)S(1)}, u32[]{:S(2)}, u32[]{:S(2)}) collective-permute-start(bf16[80,2048]{1,0:T(8,128)(2,1)S(1)} %get-tuple-element.148), channel_id=1, source_target_pairs={{0,2},{1,3},{2,0},{3,1},{4,6},{5,7},{6,4},{7,5},{8,10},{9,11},{10,... | collective-permute-start | bytes 983048 | tf_op jit(solution)/shard_map/ppermute | solution.py:24
  138.5 15.4 %collective-permute-start.33 = (bf16[80,2048]{1,0:T(8,128)(2,1)S(1)}, bf16[80,2048]{1,0:T(8,128)(2,1)S(1)}, u32[]{:S(2)}, u32[]{:S(2)}) collective-permute-start(bf16[80,2048]{1,0:T(8,128)(2,1)S(1)} %get-tuple-element.149), channel_id=1, source_target_pairs={{0,4},{1,5},{2,6},{3,7},{4,0},{5,1},{6,2},{7,3},{8,12},{9,13},{10,... | collective-permute-start | bytes 983048 | tf_op jit(solution)/shard_map/ppermute | solution.py:24
  141.4 13.9 %collective-permute-start.45 = (bf16[128,2048]{1,0:T(8,128)(2,1)S(1)}, bf16[128,2048]{1,0:T(8,128)(2,1)S(1)}, u32[]{:S(2)}, u32[]{:S(2)}) collective-permute-start(bf16[128,2048]{1,0:T(8,128)(2,1)S(1)} %merge.4), channel_id=1, source_target_pairs={{0,8},{8,16},{16,24},{24,0},{1,9},{9,17},{17,25},{25,1},{2,10},{10... | collective-permute-start | bytes 1572872 | tf_op jit(solution)/shard_map/ppermute | solution.py:29
  143.0 12.3 %collective-permute-start.34 = (bf16[80,2048]{1,0:T(8,128)(2,1)S(1)}, bf16[80,2048]{1,0:T(8,128)(2,1)S(1)}, u32[]{:S(2)}, u32[]{:S(2)}) collective-permute-start(bf16[80,2048]{1,0:T(8,128)(2,1)S(1)} %get-tuple-element.150), channel_id=1, source_target_pairs={{0,6},{1,7},{2,4},{3,5},{4,2},{5,3},{6,0},{7,1},{8,14},{9,15},{10,... | collective-permute-start | bytes 983048 | tf_op jit(solution)/shard_map/ppermute | solution.py:24
  146.2 15.6 %collective-permute-start.39 = (bf16[80,2048]{1,0:T(8,128)(2,1)S(1)}, bf16[80,2048]{1,0:T(8,128)(2,1)S(1)}, u32[]{:S(2)}, u32[]{:S(2)}) collective-permute-start(bf16[80,2048]{1,0:T(8,128)(2,1)S(1)} %get-tuple-element.158), channel_id=1, source_target_pairs={{0,2},{1,3},{2,0},{3,1},{4,6},{5,7},{6,4},{7,5},{8,10},{9,11},{10,... | collective-permute-start | bytes 983048 | tf_op jit(solution)/shard_map/ppermute | solution.py:24
  147.8 18.6 %collective-permute-start.40 = (bf16[80,2048]{1,0:T(8,128)(2,1)S(1)}, bf16[80,2048]{1,0:T(8,128)(2,1)S(1)}, u32[]{:S(2)}, u32[]{:S(2)}) collective-permute-start(bf16[80,2048]{1,0:T(8,128)(2,1)S(1)} %get-tuple-element.159), channel_id=1, source_target_pairs={{0,4},{1,5},{2,6},{3,7},{4,0},{5,1},{6,2},{7,3},{8,12},{9,13},{10,... | collective-permute-start | bytes 983048 | tf_op jit(solution)/shard_map/ppermute | solution.py:24
  154.0 12.4 %collective-permute-start.41 = (bf16[80,2048]{1,0:T(8,128)(2,1)S(1)}, bf16[80,2048]{1,0:T(8,128)(2,1)S(1)}, u32[]{:S(2)}, u32[]{:S(2)}) collective-permute-start(bf16[80,2048]{1,0:T(8,128)(2,1)S(1)} %get-tuple-element.160), channel_id=1, source_target_pairs={{0,6},{1,7},{2,4},{3,5},{4,2},{5,3},{6,0},{7,1},{8,14},{9,15},{10,... | collective-permute-start | bytes 983048 | tf_op jit(solution)/shard_map/ppermute | solution.py:24
  157.2 30.9 %collective-permute-start.46 = (bf16[128,2048]{1,0:T(8,128)(2,1)S(1)}, bf16[128,2048]{1,0:T(8,128)(2,1)S(1)}, u32[]{:S(2)}, u32[]{:S(2)}) collective-permute-start(bf16[128,2048]{1,0:T(8,128)(2,1)S(1)} %merge.5), channel_id=1, source_target_pairs={{0,8},{8,16},{16,24},{24,0},{1,9},{9,17},{17,25},{25,1},{2,10},{10... | collective-permute-start | bytes 1572872 | tf_op jit(solution)/shard_map/ppermute | solution.py:29
  174.1 9.5 %collective-permute-start.42 = (bf16[80,2048]{1,0:T(8,128)(2,1)S(1)}, bf16[80,2048]{1,0:T(8,128)(2,1)S(1)}, u32[]{:S(2)}, u32[]{:S(2)}) collective-permute-start(bf16[80,2048]{1,0:T(8,128)(2,1)S(1)} %get-tuple-element.169), channel_id=1, source_target_pairs={{0,2},{1,3},{2,0},{3,1},{4,6},{5,7},{6,4},{7,5},{8,10},{9,11},{10,... | collective-permute-start | bytes 983048 | tf_op jit(solution)/shard_map/ppermute | solution.py:24
  174.4 10.0 %collective-permute-start.43 = (bf16[80,2048]{1,0:T(8,128)(2,1)S(1)}, bf16[80,2048]{1,0:T(8,128)(2,1)S(1)}, u32[]{:S(2)}, u32[]{:S(2)}) collective-permute-start(bf16[80,2048]{1,0:T(8,128)(2,1)S(1)} %get-tuple-element.170), channel_id=1, source_target_pairs={{0,4},{1,5},{2,6},{3,7},{4,0},{5,1},{6,2},{7,3},{8,12},{9,13},{10,... | collective-permute-start | bytes 983048 | tf_op jit(solution)/shard_map/ppermute | solution.py:24
  175.8 12.3 %collective-permute-start.44 = (bf16[80,2048]{1,0:T(8,128)(2,1)S(1)}, bf16[80,2048]{1,0:T(8,128)(2,1)S(1)}, u32[]{:S(2)}, u32[]{:S(2)}) collective-permute-start(bf16[80,2048]{1,0:T(8,128)(2,1)S(1)} %get-tuple-element.171), channel_id=1, source_target_pairs={{0,6},{1,7},{2,4},{3,5},{4,2},{5,3},{6,0},{7,1},{8,14},{9,15},{10,... | collective-permute-start | bytes 983048 | tf_op jit(solution)/shard_map/ppermute | solution.py:24
  189.9 12.4 %collective-permute-start.47 = (bf16[128,2048]{1,0:T(8,128)(2,1)S(1)}, bf16[128,2048]{1,0:T(8,128)(2,1)S(1)}, u32[]{:S(2)}, u32[]{:S(2)}) collective-permute-start(bf16[128,2048]{1,0:T(8,128)(2,1)S(1)} %merge.6), channel_id=1, source_target_pairs={{0,8},{8,16},{16,24},{24,0},{1,9},{9,17},{17,25},{25,1},{2,10},{10... | collective-permute-start | bytes 1572872 | tf_op jit(solution)/shard_map/ppermute | solution.py:29
  190.0 8.2 %collective-permute-start.35 = (bf16[80,2048]{1,0:T(8,128)(2,1)S(1)}, bf16[80,2048]{1,0:T(8,128)(2,1)S(1)}, u32[]{:S(2)}, u32[]{:S(2)}) collective-permute-start(bf16[80,2048]{1,0:T(8,128)(2,1)S(1)} %get-tuple-element.151), channel_id=1, source_target_pairs={{0,2},{1,3},{2,0},{3,1},{4,6},{5,7},{6,4},{7,5},{8,10},{9,11},{10,... | collective-permute-start | bytes 983048 | tf_op jit(solution)/shard_map/ppermute | solution.py:24
  190.8 11.5 %collective-permute-start.36 = (bf16[80,2048]{1,0:T(8,128)(2,1)S(1)}, bf16[80,2048]{1,0:T(8,128)(2,1)S(1)}, u32[]{:S(2)}, u32[]{:S(2)}) collective-permute-start(bf16[80,2048]{1,0:T(8,128)(2,1)S(1)} %get-tuple-element.152), channel_id=1, source_target_pairs={{0,4},{1,5},{2,6},{3,7},{4,0},{5,1},{6,2},{7,3},{8,12},{9,13},{10,... | collective-permute-start | bytes 983048 | tf_op jit(solution)/shard_map/ppermute | solution.py:24
  192.3 9.9 %collective-permute-start.37 = (bf16[80,2048]{1,0:T(8,128)(2,1)S(1)}, bf16[80,2048]{1,0:T(8,128)(2,1)S(1)}, u32[]{:S(2)}, u32[]{:S(2)}) collective-permute-start(bf16[80,2048]{1,0:T(8,128)(2,1)S(1)} %get-tuple-element.153), channel_id=1, source_target_pairs={{0,6},{1,7},{2,4},{3,5},{4,2},{5,3},{6,0},{7,1},{8,14},{9,15},{10,... | collective-permute-start | bytes 983048 | tf_op jit(solution)/shard_map/ppermute | solution.py:24
  (11 other events, 239.6 us)
